TPU v7x, 128 devices: a whole 4x4x4 slice. The times are simulated.
128 devices in a mesh: gx: 4 (over z_lo, core), gy: 4 (over x), gz: 8 (over y, z_hi).
Axes of the slice: x: 4, y: 4, z: 4 (z_hi: 2, z_lo: 2; z = z_hi * 2 + z_lo), core: 2. Of those that a mesh axis runs over, the one named last changes fastest.
Arguments:
- fine_in: bfloat16 [64, 256, 2048], P('gx', 'gy', 'gz'), may hold values from -6 to 6
- fine_weights: bfloat16 [2, 2, 8, 8, 3, 3, 3], replicated, may hold values from -0.4375 to 0.4375
- coarse_out: bfloat16 [4, 16, 64, 2048], P(None, 'gx', 'gy', 'gz'), may hold values from -6 to 6
- coarse_cot: bfloat16 [4, 16, 64, 2048], P(None, 'gx', 'gy', 'gz'), may hold values from -6 to 6
- coarse_weights: bfloat16 [2, 32, 32, 3, 3, 3], replicated, may hold values from -0.21875 to 0.21875
Outputs:
- fine_out: bfloat16 [64, 256, 2048], P('gx', 'gy', 'gz')
- rebuilt: bfloat16 [4, 16, 64, 2048], P('gx', None, 'gy', 'gz')
- grads_in: bfloat16 [4, 16, 64, 2048], P('gx', None, 'gy', 'gz')
- weight_grads: float32 [2, 32, 32, 3, 3, 3], replicated
All inputs are finite; a program needn't handle non-finite values.
Results may differ from a plain program's by a relative error of at most 0.015.
Values may be sent and summed in bfloat16 or wider, within the bound.
A program may use at most 128 MiB of HBM per device.

v0:
```python
import jax
import jax.numpy as jnp
from jax import lax
from jax.sharding import PartitionSpec as P


def extended(block, sides, width):
    for axis, dim in sides:
        count = lax.axis_size(axis)
        forward = [(i, i + 1) for i in range(count - 1)]
        backward = [(target, source) for source, target in forward]
        low = lax.ppermute(
            lax.slice_in_dim(block, block.shape[dim] - width, None, axis=dim), axis, forward
        )
        high = lax.ppermute(lax.slice_in_dim(block, 0, width, axis=dim), axis, backward)
        block = jnp.concatenate([low, block, high], axis=dim)
    return block


def tap_table(width):
    inner = jnp.arange(width + 2)[None, :, None]
    outer = jnp.arange(width)[None, None, :]
    taps = jnp.arange(3)[:, None, None]
    return (inner == outer + taps).astype(jnp.float32)


def z_blocks(depth):
    step = min(depth, 16)
    starts = list(range(0, depth, step))
    return [(start, min(step, depth - start)) for start in starts]


def band_for(weight_ab, width):
    out_ch = weight_ab.shape[0]
    in_ch = weight_ab.shape[1]
    table = jnp.einsum(
        "ock,kiz->iczo",
        weight_ab.astype(jnp.float32),
        tap_table(width),
        precision=lax.Precision.HIGHEST,
    )
    return table.reshape((width + 2) * in_ch, width * out_ch).astype(jnp.bfloat16)


def conv_padded(weight, padded, shape):
    sx, sy, sz = shape
    count = padded.shape[0]
    in_ch = padded.shape[4]
    out_ch = weight.shape[0]
    pieces = []
    for start, width in z_blocks(sz):
        total = None
        for a in range(3):
            for b in range(3):
                band = band_for(weight[:, :, a, b, :], width)
                rows = padded[:, a : a + sx, b : b + sy, start : start + width + 2, :].reshape(
                    count * sx * sy, (width + 2) * in_ch
                )
                term = jnp.dot(rows, band, preferred_element_type=jnp.float32)
                total = term if total is None else total + term
        pieces.append(total.reshape(count, sx, sy, width, out_ch))
    return pieces[0]


def flipped(weight):
    return jnp.transpose(jnp.flip(weight, (2, 3, 4)), (1, 0, 2, 3, 4))


def weight_grad(cotangent, padded, shape):
    sx, sy, sz = shape
    count = padded.shape[0]
    in_ch = padded.shape[4]
    out_ch = cotangent.shape[4]
    rows_ab = []
    for a in range(3):
        row_b = []
        for b in range(3):
            total = jnp.zeros((out_ch, in_ch, 3), jnp.float32)
            for start, width in z_blocks(sz):
                rows = padded[:, a : a + sx, b : b + sy, start : start + width + 2, :].reshape(
                    count * sx * sy, (width + 2) * in_ch
                )
                cots = cotangent.reshape(count * sx * sy, width * out_ch)
                product = lax.dot_general(
                    rows, cots, (((0,), (0,)), ((), ())), preferred_element_type=jnp.float32
                )
                folded = jnp.einsum(
                    "iczo,kiz->ock",
                    product.reshape(width + 2, in_ch, width, out_ch),
                    tap_table(width),
                    precision=lax.Precision.HIGHEST,
                )
                total = folded
            row_b.append(total)
        rows_ab.append(jnp.stack(row_b))
    stacked = jnp.stack(rows_ab)
    return jnp.transpose(stacked, (2, 3, 0, 1, 4))


def silu_grad(value):
    sigma = jax.nn.sigmoid(value)
    return sigma * (1.0 + value * (1.0 - sigma))


def silu_bf(value):
    return jax.nn.silu(value.astype(jnp.float32)).astype(jnp.bfloat16)


def split_cells(merged, channels):
    return merged.reshape(merged.shape[:-1] + (merged.shape[-1] // channels, channels))


def join_cells(field):
    return field.reshape(field.shape[:-2] + (field.shape[-2] * field.shape[-1],))


def coarse_block(y_all, cot_all, weight_f, weight_g, pad_first, pad_pair):
    half = y_all.shape[4] // 2
    y_one = y_all[..., :half]
    y_two = y_all[..., half:]
    cot_one = cot_all[..., :half]
    cot_two = cot_all[..., half:]
    shape = y_one.shape[1:4]
    u_one = silu_bf(y_one)
    padded_both = pad_first(jnp.concatenate([u_one, cot_two], axis=4))
    padded_u_one = padded_both[..., :half]
    padded_cot_two = padded_both[..., half:]
    x_two = (y_two.astype(jnp.float32) - conv_padded(weight_g, padded_u_one, shape)).astype(
        jnp.bfloat16
    )
    u_two = silu_bf(x_two)
    back_g = conv_padded(flipped(weight_g), padded_cot_two, shape)
    carried = (cot_one.astype(jnp.float32) + silu_grad(y_one.astype(jnp.float32)) * back_g).astype(
        jnp.bfloat16
    )
    padded_pair = pad_pair(jnp.concatenate([u_two, carried], axis=4))
    padded_u_two = padded_pair[..., :half]
    padded_carried = padded_pair[..., half:]
    x_one = (y_one.astype(jnp.float32) - conv_padded(weight_f, padded_u_two, shape)).astype(
        jnp.bfloat16
    )
    back_f = conv_padded(flipped(weight_f), padded_carried, shape)
    dx_two = (cot_two.astype(jnp.float32) + silu_grad(x_two.astype(jnp.float32)) * back_f).astype(
        jnp.bfloat16
    )
    grad_f = weight_grad(carried, padded_u_two, shape)
    grad_g = weight_grad(cot_two, padded_u_one, shape)
    rebuilt = jnp.concatenate([x_one, x_two], axis=4)
    grads_in = jnp.concatenate([carried, dx_two], axis=4)
    return (rebuilt, grads_in, jnp.stack([grad_f, grad_g]))


def on_device(fine_in, fine_weights, coarse_out, coarse_cot, coarse_weights):
    channels_fine = fine_weights.shape[2] * 2
    channels_coarse = coarse_weights.shape[1] * 2
    state = split_cells(fine_in, channels_fine)[None]
    half = channels_fine // 2
    shape = state.shape[1:4]
    for block in range(fine_weights.shape[0]):
        first = state[..., :half]
        second = state[..., half:]
        weight_f = fine_weights[block, 0]
        weight_g = fine_weights[block, 1]
        s_two = silu_bf(second)
        padded_two = extended(s_two, (("gx", 1), ("gy", 2), ("gz", 3)), 1)
        y_one = (first.astype(jnp.float32) + conv_padded(weight_f, padded_two, shape)).astype(
            jnp.bfloat16
        )
        s_one = silu_bf(y_one)
        padded_one = extended(s_one, (("gx", 1), ("gy", 2), ("gz", 3)), 1)
        y_two = (second.astype(jnp.float32) + conv_padded(weight_g, padded_one, shape)).astype(
            jnp.bfloat16
        )
        state = jnp.concatenate([y_one, y_two], axis=4)
    fine_out = join_cells(state[0])
    coarse_f = coarse_weights[0]
    coarse_g = coarse_weights[1]

    def tile_one(values):
        return extended(values, (("gx", 1), ("gy", 2), ("gz", 3)), 1)

    def tile_both(values):
        return extended(values, (("gx", 1), ("gy", 2), ("gz", 3)), 1)

    rebuilt_tiles, grads_tiles, grad_terms = coarse_block(
        split_cells(coarse_out, channels_coarse),
        split_cells(coarse_cot, channels_coarse),
        coarse_f,
        coarse_g,
        tile_one,
        tile_both,
    )
    rebuilt, grads_in = (
        lax.all_to_all(join_cells(rebuilt_tiles), "gx", split_axis=0, concat_axis=1, tiled=True),
        lax.all_to_all(join_cells(grads_tiles), "gx", split_axis=0, concat_axis=1, tiled=True),
    )
    weight_grads = lax.psum(grad_terms, ("gx", "gy", "gz"))
    return (fine_out, rebuilt, grads_in, weight_grads)


def solution(mesh):
    placed = (P("gx", "gy", "gz"), P(), P(None, "gx", "gy", "gz"), P(None, "gx", "gy", "gz"), P())
    return jax.shard_map(
        on_device,
        mesh=mesh,
        in_specs=placed,
        out_specs=(P("gx", "gy", "gz"), P("gx", None, "gy", "gz"), P("gx", None, "gy", "gz"), P()),
        check_vma=False,
    )
```

profile of v0, /device:TPU:1, one launch (start us, length us, event | category | flops | bytes accessed | tf_op | source)
XLA Modules:
  0.0 964.7 jit_solution(7276683546614827454)
XLA Ops:
  11.6 4.9 collective-permute-start.24
  20.0 3.6 collective-permute-start
  108.4 3.7 collective-permute-start.2
  123.2 5.8 collective-permute-start.4
  204.4 4.6 collective-permute-start.6
  295.0 3.5 copy.418
  420.0 3.3 collective-permute-start.8
  428.6 4.0 collective-permute-start.26
  439.8 6.4 collective-permute-start.10
  483.6 5.3 collective-permute-start.12
  491.9 5.7 collective-permute-start.28
  503.4 4.9 collective-permute-start.14
  514.8 4.4 fusion.242
  569.4 3.6 collective-permute-start.30
  619.4 6.4 collective-permute-start.16
  688.1 4.6 collective-permute-start.18
  701.4 4.3 collective-permute-start.20
  710.3 4.0 collective-permute-start.32
  720.7 4.7 collective-permute-start.22
  729.2 6.2 collective-permute-start.34
  773.3 4.1 fusion.241
  815.4 3.4 all-to-all-start.1
  822.6 4.0 all-to-all-start
  830.2 123.7 %all-reduce.2.cloned.1.call-done = f32[2,32,32,3,3,3]{1,5,2,4,3,0:T(4,128)} async-done(((f32[2,32,32,3,3,3]{1,5,2,4,3,0:T(4,128)}), f32[2,32,32,3,3,3]{1,5,2,4,3,0:T(4,128)}) %all-reduce.2.cloned.1.call-update) | async-done | bytes 221200 | tf_op jit(solution)/shard_map/psum | solution.py:197
  (978 shorter events, 718.0 us)
Async XLA Ops:
  7.2 946.8 %all-reduce.2.cloned.1.call-start = ((), (), s32[]{:S(2)}) async-start(), calls=%async_computation.2 | async-start | bytes 2359296 | tf_op jit(solution)/shard_map/psum | solution.py:197
  11.6 415.5 %collective-permute-start.24 = (bf16[4,1,16,4,64]{4,3,2,1,0:T(4,128)(2,1)}, bf16[4,1,16,4,64]{4,3,2,1,0:T(4,128)(2,1)}, u32[]{:S(2)}, u32[]{:S(2)}) collective-permute-start(bf16[4,1,16,4,64]{4,3,2,1,0:T(4,128)(2,1)} %get-tuple-element.118), channel_id=1, source_target_pairs={{0,32},{32,64},{64,96},{1,33},{33,65},{65,97},{2,34},{34,66},{66,9... | collective-permute-start | bytes 98312 | tf_op jit(solution)/shard_map/ppermute | solution.py:12
  16.6 410.6 %collective-permute-start.25 = (bf16[4,1,16,4,64]{4,3,2,1,0:T(4,128)(2,1)}, bf16[4,1,16,4,64]{4,3,2,1,0:T(4,128)(2,1)}, u32[]{:S(2)}, u32[]{:S(2)}) collective-permute-start(bf16[4,1,16,4,64]{4,3,2,1,0:T(4,128)(2,1)} %get-tuple-element.119), channel_id=1, source_target_pairs={{32,0},{64,32},{96,64},{33,1},{65,33},{97,65},{34,2},{66,34},{98,6... | collective-permute-start | bytes 98312 | tf_op jit(solution)/shard_map/ppermute | solution.py:15
  20.0 84.1 %collective-permute-start = (bf16[1,1,64,16,8]{2,4,3,1,0:T(8,128)(2,1)}, bf16[1,1,64,16,8]{2,4,3,1,0:T(8,128)(2,1)S(1)}, u32[]{:S(2)}, u32[]{:S(2)}) collective-permute-start(bf16[1,1,64,16,8]{2,4,3,1,0:T(8,128)(2,1)} %get-tuple-element.126), channel_id=1, source_target_pairs={{0,32},{32,64},{64,96},{1,33},{33,65},{65,97},{2,34},{34,66},{66,9... | collective-permute-start | bytes 49160 | tf_op jit(solution)/shard_map/ppermute | solution.py:12
  23.7 80.5 %collective-permute-start.1 = (bf16[1,1,64,16,8]{2,4,3,1,0:T(8,128)(2,1)}, bf16[1,1,64,16,8]{2,4,3,1,0:T(8,128)(2,1)S(1)}, u32[]{:S(2)}, u32[]{:S(2)}) collective-permute-start(bf16[1,1,64,16,8]{2,4,3,1,0:T(8,128)(2,1)} %get-tuple-element.127), channel_id=1, source_target_pairs={{32,0},{64,32},{96,64},{33,1},{65,33},{97,65},{34,2},{66,34},{98,6... | collective-permute-start | bytes 49160 | tf_op jit(solution)/shard_map/ppermute | solution.py:15
  123.2 53.4 %collective-permute-start.4 = (bf16[1,18,66,1,8]{2,4,3,1,0:T(8,128)(2,1)}, bf16[1,18,66,1,8]{2,4,3,1,0:T(8,128)(2,1)}, u32[]{:S(2)}, u32[]{:S(2)}) collective-permute-start(bf16[1,18,66,1,8]{2,4,3,1,0:T(8,128)(2,1)} %get-tuple-element.30), channel_id=1, source_target_pairs={{0,1},{1,2},{2,3},{3,4},{4,5},{5,6},{6,7},{8,9},{9,10},{10,11},{11... | collective-permute-start | bytes 57032 | tf_op jit(solution)/shard_map/ppermute | solution.py:12
  129.0 47.6 %collective-permute-start.5 = (bf16[1,18,66,1,8]{2,4,3,1,0:T(8,128)(2,1)}, bf16[1,18,66,1,8]{2,4,3,1,0:T(8,128)(2,1)}, u32[]{:S(2)}, u32[]{:S(2)}) collective-permute-start(bf16[1,18,66,1,8]{2,4,3,1,0:T(8,128)(2,1)} %get-tuple-element.31), channel_id=1, source_target_pairs={{1,0},{2,1},{3,2},{4,3},{5,4},{6,5},{7,6},{9,8},{10,9},{11,10},{12... | collective-permute-start | bytes 57032 | tf_op jit(solution)/shard_map/ppermute | solution.py:15
  204.4 212.2 %collective-permute-start.6 = (bf16[1,1,64,16,8]{2,4,3,1,0:T(8,128)(2,1)}, bf16[1,1,64,16,8]{2,4,3,1,0:T(8,128)(2,1)S(1)}, u32[]{:S(2)}, u32[]{:S(2)}) collective-permute-start(bf16[1,1,64,16,8]{2,4,3,1,0:T(8,128)(2,1)} %get-tuple-element.124), channel_id=1, source_target_pairs={{0,32},{32,64},{64,96},{1,33},{33,65},{65,97},{2,34},{34,66},{66,9... | collective-permute-start | bytes 49160 | tf_op jit(solution)/shard_map/ppermute | solution.py:12
  209.0 207.6 %collective-permute-start.7 = (bf16[1,1,64,16,8]{2,4,3,1,0:T(8,128)(2,1)}, bf16[1,1,64,16,8]{2,4,3,1,0:T(8,128)(2,1)S(1)}, u32[]{:S(2)}, u32[]{:S(2)}) collective-permute-start(bf16[1,1,64,16,8]{2,4,3,1,0:T(8,128)(2,1)} %get-tuple-element.125), channel_id=1, source_target_pairs={{32,0},{64,32},{96,64},{33,1},{65,33},{97,65},{34,2},{66,34},{98,6... | collective-permute-start | bytes 49160 | tf_op jit(solution)/shard_map/ppermute | solution.py:15
  420.0 13.9 %collective-permute-start.8 = (bf16[1,18,1,16,8]{1,4,3,2,0:T(8,128)(2,1)S(1)}, bf16[1,18,1,16,8]{1,4,3,2,0:T(8,128)(2,1)S(1)}, u32[]{:S(2)}, u32[]{:S(2)}) collective-permute-start(bf16[1,18,1,16,8]{1,4,3,2,0:T(8,128)(2,1)S(1)} %copy.404), channel_id=1, source_target_pairs={{0,8},{8,16},{16,24},{1,9},{9,17},{17,25},{2,10},{10,18},{18,26},{... | collective-permute-start | bytes 13832 | tf_op jit(solution)/shard_map/ppermute | solution.py:12
  428.6 19.3 %collective-permute-start.26 = (bf16[4,6,1,4,64]{4,3,2,1,0:T(4,128)(2,1)}, bf16[4,6,1,4,64]{4,3,2,1,0:T(4,128)(2,1)S(1)}, u32[]{:S(2)}, u32[]{:S(2)}) collective-permute-start(bf16[4,6,1,4,64]{4,3,2,1,0:T(4,128)(2,1)} %get-tuple-element.106), channel_id=1, source_target_pairs={{0,8},{8,16},{16,24},{1,9},{9,17},{17,25},{2,10},{10,18},{18,26},{... | collective-permute-start | bytes 36872 | tf_op jit(solution)/shard_map/ppermute | solution.py:12
  432.6 15.4 %collective-permute-start.27 = (bf16[4,6,1,4,64]{4,3,2,1,0:T(4,128)(2,1)}, bf16[4,6,1,4,64]{4,3,2,1,0:T(4,128)(2,1)S(1)}, u32[]{:S(2)}, u32[]{:S(2)}) collective-permute-start(bf16[4,6,1,4,64]{4,3,2,1,0:T(4,128)(2,1)} %get-tuple-element.107), channel_id=1, source_target_pairs={{8,0},{16,8},{24,16},{9,1},{17,9},{25,17},{10,2},{18,10},{26,18},{... | collective-permute-start | bytes 36872 | tf_op jit(solution)/shard_map/ppermute | solution.py:15
  483.6 15.3 %collective-permute-start.12 = (bf16[1,1,64,16,8]{2,4,3,1,0:T(8,128)(2,1)S(1)}, bf16[1,1,64,16,8]{2,4,3,1,0:T(8,128)(2,1)S(1)}, u32[]{:S(2)}, u32[]{:S(2)}) collective-permute-start(bf16[1,1,64,16,8]{2,4,3,1,0:T(8,128)(2,1)S(1)} %get-tuple-element.122), channel_id=1, source_target_pairs={{0,32},{32,64},{64,96},{1,33},{33,65},{65,97},{2,34},{34,66},{66,9... | collective-permute-start | bytes 49160 | tf_op jit(solution)/shard_map/ppermute | solution.py:12
  491.9 20.4 %collective-permute-start.28 = (bf16[4,6,18,1,64]{4,3,2,1,0:T(2,128)(2,1)}, bf16[4,6,18,1,64]{4,3,2,1,0:T(2,128)(2,1)}, u32[]{:S(2)}, u32[]{:S(2)}) collective-permute-start(bf16[4,6,18,1,64]{4,3,2,1,0:T(2,128)(2,1)} %get-tuple-element.132), channel_id=1, source_target_pairs={{0,1},{1,2},{2,3},{3,4},{4,5},{5,6},{6,7},{8,9},{9,10},{10,11},{11... | collective-permute-start | bytes 165896 | tf_op jit(solution)/shard_map/ppermute | solution.py:12
  497.6 14.7 %collective-permute-start.29 = (bf16[4,6,18,1,64]{4,3,2,1,0:T(2,128)(2,1)}, bf16[4,6,18,1,64]{4,3,2,1,0:T(2,128)(2,1)}, u32[]{:S(2)}, u32[]{:S(2)}) collective-permute-start(bf16[4,6,18,1,64]{4,3,2,1,0:T(2,128)(2,1)} %get-tuple-element.133), channel_id=1, source_target_pairs={{1,0},{2,1},{3,2},{4,3},{5,4},{6,5},{7,6},{9,8},{10,9},{11,10},{12... | collective-permute-start | bytes 165896 | tf_op jit(solution)/shard_map/ppermute | solution.py:15
  503.4 109.1 %collective-permute-start.14 = (bf16[1,18,1,16,8]{1,4,3,2,0:T(8,128)(2,1)}, bf16[1,18,1,16,8]{1,4,3,2,0:T(8,128)(2,1)}, u32[]{:S(2)}, u32[]{:S(2)}) collective-permute-start(bf16[1,18,1,16,8]{1,4,3,2,0:T(8,128)(2,1)} %copy.429), channel_id=1, source_target_pairs={{0,8},{8,16},{16,24},{1,9},{9,17},{17,25},{2,10},{10,18},{18,26},{... | collective-permute-start | bytes 13832 | tf_op jit(solution)/shard_map/ppermute | solution.py:12
  510.8 104.5 %collective-permute-start.15 = (bf16[1,18,1,16,8]{1,4,3,2,0:T(8,128)(2,1)}, bf16[1,18,1,16,8]{1,4,3,2,0:T(8,128)(2,1)}, u32[]{:S(2)}, u32[]{:S(2)}) collective-permute-start(bf16[1,18,1,16,8]{1,4,3,2,0:T(8,128)(2,1)} %copy.430), channel_id=1, source_target_pairs={{8,0},{16,8},{24,16},{9,1},{17,9},{25,17},{10,2},{18,10},{26,18},{... | collective-permute-start | bytes 13832 | tf_op jit(solution)/shard_map/ppermute | solution.py:15
  569.4 139.5 %collective-permute-start.30 = (bf16[4,1,16,4,64]{4,3,2,1,0:T(4,128)(2,1)}, bf16[4,1,16,4,64]{4,3,2,1,0:T(4,128)(2,1)S(1)}, u32[]{:S(2)}, u32[]{:S(2)}) collective-permute-start(bf16[4,1,16,4,64]{4,3,2,1,0:T(4,128)(2,1)} %get-tuple-element.116), channel_id=1, source_target_pairs={{0,32},{32,64},{64,96},{1,33},{33,65},{65,97},{2,34},{34,66},{66,9... | collective-permute-start | bytes 98312 | tf_op jit(solution)/shard_map/ppermute | solution.py:12
  573.0 135.9 %collective-permute-start.31 = (bf16[4,1,16,4,64]{4,3,2,1,0:T(4,128)(2,1)}, bf16[4,1,16,4,64]{4,3,2,1,0:T(4,128)(2,1)}, u32[]{:S(2)}, u32[]{:S(2)}) collective-permute-start(bf16[4,1,16,4,64]{4,3,2,1,0:T(4,128)(2,1)} %get-tuple-element.117), channel_id=1, source_target_pairs={{32,0},{64,32},{96,64},{33,1},{65,33},{97,65},{34,2},{66,34},{98,6... | collective-permute-start | bytes 98312 | tf_op jit(solution)/shard_map/ppermute | solution.py:15
  701.4 14.2 %collective-permute-start.20 = (bf16[1,18,1,16,8]{1,4,3,2,0:T(8,128)(2,1)S(1)}, bf16[1,18,1,16,8]{1,4,3,2,0:T(8,128)(2,1)S(1)}, u32[]{:S(2)}, u32[]{:S(2)}) collective-permute-start(bf16[1,18,1,16,8]{1,4,3,2,0:T(8,128)(2,1)S(1)} %copy.454), channel_id=1, source_target_pairs={{0,8},{8,16},{16,24},{1,9},{9,17},{17,25},{2,10},{10,18},{18,26},{... | collective-permute-start | bytes 13832 | tf_op jit(solution)/shard_map/ppermute | solution.py:12
  710.3 16.4 %collective-permute-start.32 = (bf16[4,6,1,4,64]{4,3,2,1,0:T(4,128)(2,1)}, bf16[4,6,1,4,64]{4,3,2,1,0:T(4,128)(2,1)S(1)}, u32[]{:S(2)}, u32[]{:S(2)}) collective-permute-start(bf16[4,6,1,4,64]{4,3,2,1,0:T(4,128)(2,1)} %get-tuple-element.104), channel_id=1, source_target_pairs={{0,8},{8,16},{16,24},{1,9},{9,17},{17,25},{2,10},{10,18},{18,26},{... | collective-permute-start | bytes 36872 | tf_op jit(solution)/shard_map/ppermute | solution.py:12
  720.7 15.9 %collective-permute-start.22 = (bf16[1,18,66,1,8]{2,4,3,1,0:T(8,128)(2,1)S(1)}, bf16[1,18,66,1,8]{2,4,3,1,0:T(8,128)(2,1)S(1)}, u32[]{:S(2)}, u32[]{:S(2)}) collective-permute-start(bf16[1,18,66,1,8]{2,4,3,1,0:T(8,128)(2,1)S(1)} %get-tuple-element.24), channel_id=1, source_target_pairs={{0,1},{1,2},{2,3},{3,4},{4,5},{5,6},{6,7},{8,9},{9,10},{10,11},{11... | collective-permute-start | bytes 57032 | tf_op jit(solution)/shard_map/ppermute | solution.py:12
  729.2 41.8 %collective-permute-start.34 = (bf16[4,6,18,1,64]{4,3,2,1,0:T(2,128)(2,1)}, bf16[4,6,18,1,64]{4,3,2,1,0:T(2,128)(2,1)}, u32[]{:S(2)}, u32[]{:S(2)}) collective-permute-start(bf16[4,6,18,1,64]{4,3,2,1,0:T(2,128)(2,1)} %get-tuple-element.130), channel_id=1, source_target_pairs={{0,1},{1,2},{2,3},{3,4},{4,5},{5,6},{6,7},{8,9},{9,10},{10,11},{11... | collective-permute-start | bytes 165896 | tf_op jit(solution)/shard_map/ppermute | solution.py:12
  735.3 35.6 %collective-permute-start.35 = (bf16[4,6,18,1,64]{4,3,2,1,0:T(2,128)(2,1)}, bf16[4,6,18,1,64]{4,3,2,1,0:T(2,128)(2,1)}, u32[]{:S(2)}, u32[]{:S(2)}) collective-permute-start(bf16[4,6,18,1,64]{4,3,2,1,0:T(2,128)(2,1)} %get-tuple-element.131), channel_id=1, source_target_pairs={{1,0},{2,1},{3,2},{4,3},{5,4},{6,5},{7,6},{9,8},{10,9},{11,10},{12... | collective-permute-start | bytes 165896 | tf_op jit(solution)/shard_map/ppermute | solution.py:15
  (206 other events, 1728.2 us)
Sparse Core Ops, SparseCore 0:
  802.7 151.1 all-reduce.1
where the time goes:
time: 979 us; the launch traced here: 965 us
  local copies, waits for them, and re-layouts  511 us (52%)
  matrix products  141 us (14%)
  waiting for transfers between devices  133 us (14%)
  starting transfers between devices  122 us (12%)
  other arithmetic  39.7 us (4%)
  between operations  17.9 us (2%)
    convert_element_type x108, local copies, waits for them, and re-layouts, band_for(): table.reshape((width + 2) * in_ch, width * out_ch).astype(jnp.bfloat16)  247 us
    psum x1, waiting for transfers between devices, on_device(): weight_grads = lax.psum(grad_terms, ('gx', 'gy', 'gz'))  124 us
    reshape x72, local copies, waits for them, and re-layouts, conv_padded(): padded[:, a:a + sx, b:b + sy, start:start + width + 2, :]  93.1 us
    ppermute x18, starting transfers between devices, extended(): lax.ppermute(lax.slice_in_dim(block, block.shape[dim] - width, None, axis...  85.8 us
    dot_general x72, matrix products, band_for(): jnp.einsum('ock,kiz->iczo', weight_ab.astype(jnp.float32), tap_table(widt...  75 us
    slice x42, local copies, waits for them, and re-layouts, conv_padded(): padded[:, a:a + sx, b:b + sy, start:start + width + 2, :]  65.7 us
    dot_general x72, matrix products, conv_padded(): term = jnp.dot(rows, band, preferred_element_type=jnp.float32)  32.3 us
    ppermute x18, starting transfers between devices, extended(): lax.ppermute(lax.slice_in_dim(block, 0, width, axis=dim), axis, backward)  28.7 us
  transfers between devices with their start and end apart: 39, of which 5 were waited for; matrix products, arithmetic and copies ran while one was open for 64% of the time, Pallas kernels for 0%

commit v1 on v0

v1 whole, which is shorter than its diff:
```python
import functools

import jax
import jax.numpy as jnp
import numpy as np
from jax import lax
from jax.experimental import pallas as pl
from jax.experimental.pallas import tpu as pltpu
from jax.sharding import PartitionSpec as P

MESH = pl.DeviceIdType.MESH
BF = jnp.bfloat16
F32 = jnp.float32

FX, FY, FZ, FH = 16, 64, 16, 4
XX, YY = FX + 2 * FH, 80
CX, CY, CZ = 16, 16, 4
NONE = 99

Z_X2 = list(range(16)) + [-4, -3, -2, -1] + [NONE] * 4 + [16, 17, 18, 19] + [NONE] * 4
Z_X1 = list(range(16)) + [NONE] * 4 + [-4, -3, -2, -1] + [NONE] * 4 + [16, 17, 18, 19]
Z_H1 = [0, 1, 2, 3, -2, -1, 4, 5]
Z_H2 = [0, 1, 2, 3, 4, 5, -2, -1]


def band_masks(z_in, z_out, width):
    table = np.zeros((3, 256, 256), np.float32)
    for i, zi in enumerate(z_in):
        for o, zo in enumerate(z_out):
            if zi == NONE or zo == NONE:
                continue
            k = zi - zo + 1
            if 0 <= k <= 2:
                table[k, i * width:(i + 1) * width, o * width:(o + 1) * width] = 1.0
    return table


def constants():
    masks = np.stack([
        band_masks(Z_X2, Z_X1, 8),
        band_masks(Z_X1, Z_X2, 8),
        band_masks(Z_H1, Z_H2, 32),
        band_masks(Z_H2, Z_H1, 32),
    ])
    split_fine = np.zeros((256, 256), np.float32)
    for z in range(16):
        for c in range(8):
            split_fine[z * 16 + 8 + c, z * 8 + c] = 1.0
            split_fine[z * 16 + c, 128 + z * 8 + c] = 1.0
    edge_fine = np.zeros((512, 256), np.float32)
    for part in range(2):
        for side, z_first in ((0, 0), (1, 12)):
            for z in range(4):
                for c in range(8):
                    base = side * 128 + part * 64 + z * 8 + c
                    edge_fine[part * 256 + (z_first + z) * 16 + 8 + c, base] = 1.0
                    edge_fine[part * 256 + (z_first + z) * 16 + c, base + 32] = 1.0
    swap = np.zeros((256, 256), np.float32)
    for x in range(16):
        for y in range(16):
            swap[y * 16 + x, x * 16 + y] = 1.0
    split_coarse = np.zeros((256, 512), np.float32)
    for z in range(4):
        for c in range(32):
            split_coarse[z * 64 + c, z * 32 + c] = 1.0
            split_coarse[z * 64 + 32 + c, 128 + z * 32 + c] = 1.0
            if z < 2:
                split_coarse[z * 64 + 32 + c, 256 + z * 32 + c] = 1.0
                split_coarse[z * 64 + c, 256 + 64 + z * 32 + c] = 1.0
            else:
                split_coarse[z * 64 + c, 384 + (z - 2) * 32 + c] = 1.0
                split_coarse[z * 64 + 32 + c, 384 + 64 + (z - 2) * 32 + c] = 1.0
    perms = np.concatenate([
        split_fine, split_fine.T, edge_fine, swap,
        split_coarse[:, :256], split_coarse[:, 256:], split_coarse[:, :256].T,
    ])
    return masks.reshape(12 * 256, 256), perms


MASKS, PERMS = constants()
SPLIT_F, JOIN_F, EDGE_F, SWAP, SPLIT_C, EDGE_C, JOIN_C = 0, 256, 512, 1024, 1280, 1536, 1792


def silu(v):
    h = v * 0.5
    return h + h * jnp.tanh(h)


def silu_grad(v):
    s = 0.5 + 0.5 * jnp.tanh(v * 0.5)
    return s * (1.0 + v * (1.0 - s))


def mm(a, b):
    return jnp.dot(a, b, preferred_element_type=F32)


def iota(shape, dim):
    return lax.broadcasted_iota(jnp.int32, shape, dim)


def fine_limits(sizes):
    nx, ny, nz = sizes
    gx, gy, gz = lax.axis_index("gx"), lax.axis_index("gy"), lax.axis_index("gz")
    return (jnp.where(gx == 0, FH, 0), jnp.where(gx == nx - 1, FX + FH, XX),
            jnp.where(gy == 0, 8, 4), jnp.where(gy == ny - 1, 72, 76),
            jnp.where(gz == 0, 64, 0), jnp.where(gz == nz - 1, 64, 128))


def fine_input(state, x, column, limits):
    x_first, x_end, y_first, y_end, rim_first, rim_end = limits
    first = jnp.where((x >= x_first) & (x < x_end), y_first, YY)
    row = iota((YY, 128), 0)
    at = iota((YY, 128), 1)
    ok = (row >= first) & (row < y_end)
    rim_ok = ok & (at >= rim_first) & (at < rim_end)
    own = jnp.where(ok, silu(state[x, :, column:column + 128]), 0.0)
    rim = jnp.where(rim_ok, silu(state[x, :, 256:384]), 0.0)
    return jnp.concatenate([own, rim], axis=1)


def kernel(sizes, fine_in, fine_w, c_out, c_cot, coarse_w, masks_h, perms_h,
           state, last_band, rb_s, gi_s, wg_s,
           xraw, craw, wf, wc, masks, perms, t_fine, t_fwd, t_nat,
           bands_f, bands_c, u_fine, esend, erecv, yf, ysend, yrecv, kf, ksend, krecv,
           cs, ce, y1s, y2s, d1s, d2s, su1, sd2, su2, se,
           part, r1, r2, red, red_bf, final,
           load_sem, in_send, in_recv, x_send, x_recv, c_send, c_recv, f_send, f_recv,
           p1_send, p1_recv, p2_send, p2_recv, p3_send, p3_recv):
    nx, ny, nz = sizes
    gx, gy, gz = lax.axis_index("gx"), lax.axis_index("gy"), lax.axis_index("gz")
    ky = nz // 2
    wide, deep = ny * ky, nx * 2
    me_wide = gy * ky + gz // 2
    me_deep = gx * 2 + lax.rem(gz, 2)

    def peer_wide(d):
        p = lax.rem(me_wide + d, wide)
        return {"gy": p // ky, "gz": lax.rem(p, ky) * 2 + lax.rem(gz, 2)}

    def peer_deep(d):
        p = lax.rem(me_deep + d, deep)
        return {"gx": p // 2, "gz": gz // 2 * 2 + lax.rem(p, 2)}

    def peer_x(d):
        return {"gx": lax.rem(gx + d, nx)}

    barrier = pltpu.get_barrier_semaphore()
    for d in range(1, wide):
        pl.semaphore_signal(barrier, inc=1, device_id=peer_wide(d), device_id_type=MESH)
    for d in range(1, deep):
        pl.semaphore_signal(barrier, inc=1, device_id=peer_deep(d), device_id_type=MESH)
    for sy in (-1, 0, 1):
        for sz in (-1, 1):
            to = {"gy": lax.rem(gy + sy + ny, ny), "gz": lax.rem(gz + sz + nz, nz)}
            pl.semaphore_signal(barrier, inc=1, device_id=to, device_id_type=MESH)

    loads = [
        (coarse_w, wc.at[pl.ds(0, 1728)]),
        (masks_h.at[pl.ds(1536, 1536)], masks.at[pl.ds(1536, 1536)]),
        (perms_h, perms),
        (c_out.at[gx], craw.at[0, pl.ds(gx * 4, 4)]),
        (c_cot.at[gx], craw.at[1, pl.ds(gx * 4, 4)]),
        (fine_in, xraw.at[pl.ds(FH, FX)]),
        (fine_w, wf.at[pl.ds(0, 864)]),
        (masks_h.at[pl.ds(0, 1536)], masks.at[pl.ds(0, 1536)]),
    ]
    loads = [pltpu.make_async_copy(s, t, load_sem.at[i]) for i, (s, t) in enumerate(loads)]
    for copy in loads:
        copy.start()
    state[:, 0:8, :] = jnp.zeros((XX, 8, 384), F32)
    state[:, 72:80, :] = jnp.zeros((XX, 8, 384), F32)
    wf[864:896] = jnp.zeros((32, 8), BF)
    wc[1728:1792] = jnp.zeros((64, 32), BF)
    part[14 * 32:, :] = jnp.zeros((64, 128), F32)
    pl.semaphore_wait(barrier, wide - 1 + deep - 1 + 6)

    def remote(src, dst, send, recv, to):
        return pltpu.make_async_remote_copy(
            src_ref=src, dst_ref=dst, send_sem=send, recv_sem=recv,
            device_id=to, device_id_type=MESH)

    gathers = []
    for d in range(1, nx):
        to = lax.rem(gx + d, nx)
        for i, src in enumerate((c_out, c_cot)):
            gathers.append(remote(src.at[to], craw.at[i, pl.ds(gx * 4, 4)],
                                  in_send.at[d, i], in_recv.at[d, i], peer_x(d)))
    for copy in gathers:
        copy.start()
    low_x = remote(fine_in.at[pl.ds(0, FH)], xraw.at[pl.ds(FX + FH, FH)],
                   x_send.at[0], x_recv.at[0], {"gx": lax.max(gx - 1, 0)})
    high_x = remote(fine_in.at[pl.ds(FX - FH, FH)], xraw.at[pl.ds(0, FH)],
                    x_send.at[1], x_recv.at[1], {"gx": lax.min(gx + 1, nx - 1)})

    def exchange(copies):
        def inside(step, sign):
            at = [(g + sign * s >= 0) & (g + sign * s < n)
                  for g, s, n in zip((gx, gy, gz), step, sizes) if s != 0]
            return functools.reduce(jnp.logical_and, at)

        def start():
            for step, copy in copies:
                @pl.when(inside(step, 1))
                def _():
                    copy.start()

        def wait():
            for step, copy in copies:
                @pl.when(inside(step, 1))
                def _():
                    copy.wait_send()

                @pl.when(inside(step, -1))
                def _():
                    copy.wait_recv()
        return start, wait

    def beside(sy, sz):
        return {"gy": lax.clamp(0, gy + sy, ny - 1), "gz": lax.clamp(0, gz + sz, nz - 1)}

    start_x, wait_x = exchange([((-1, 0, 0), low_x), ((1, 0, 0), high_x)])
    start_x()

    @pl.when(gx == 0)
    def _():
        xraw[0:FH] = jnp.zeros((FH, FY, 256), BF)

    @pl.when(gx == nx - 1)
    def _():
        xraw[FX + FH:] = jnp.zeros((FH, FY, 256), BF)

    loads[0].wait()
    nt = (((1,), (1,)), ((), ()))
    eye32 = (iota((32, 32), 0) == iota((32, 32), 1)).astype(F32).astype(BF)
    tile32 = (iota((32, 256), 0) == iota((32, 256), 1) % 32).astype(F32).astype(BF)
    t_nat[...] = mm(wc[...], tile32).astype(BF)
    turned = lax.dot_general(eye32, wc[...], nt, preferred_element_type=F32)
    own = iota((128, 128), 0) // 32 == iota((128, 128), 1) // 32
    tile128 = (iota((128, 256), 0) % 32 == iota((128, 256), 1) % 32).astype(F32).astype(BF)
    for j in range(14):
        cut = turned[:, 128 * j:128 * (j + 1)]
        spread = jnp.where(own, jnp.concatenate([cut] * 4, axis=0), 0.0).astype(BF)
        t_fwd[128 * j:128 * (j + 1)] = mm(spread, tile128).astype(BF)

    def build(bands, conv, taps, rows, first, mask_base, flip=False):
        def body(i, carry):
            p, q = i // 3, i % 3
            base = p * 9 + q * 3 if rows == 16 else q * 9 + p * 3
            if flip:
                base = 24 - base
            tiles = [taps[pl.ds(pl.multiple_of((first + base + (2 - k if flip else k)) * rows, rows), rows), :]
                     for k in range(3)]
            for r in range(0, 256, rows):
                total = None
                for k in range(3):
                    at = (mask_base + k) * 256 + r
                    term = masks[at:at + rows, :] * tiles[k]
                    total = term if total is None else total + term
                bands[conv, pl.ds(pl.multiple_of(i * 256 + r, rows), rows), :] = total
            return carry
        lax.fori_loop(0, 9, body, 0)

    loads[1].wait()
    build(bands_c, 0, t_fwd, 32, 27, 6)
    build(bands_c, 1, t_nat, 32, 27, 9, True)
    build(bands_c, 2, t_fwd, 32, 0, 9)
    build(bands_c, 3, t_nat, 32, 0, 6, True)

    for copy in loads[2:5]:
        copy.wait()
    for copy in gathers:
        copy.wait()
    swap = perms[SWAP:SWAP + 256, :]
    for i in range(2):
        raw = craw[i].reshape(256, 256)
        turned_rows = mm(swap, raw).astype(BF)
        halves = mm(turned_rows, perms[SPLIT_C:SPLIT_C + 256, :]).astype(BF)
        edges = mm(turned_rows, perms[EDGE_C:EDGE_C + 256, :]).astype(BF)
        cs[i, 2:18, :, 0:256] = halves.reshape(16, 16, 256)
        ce[0, i] = edges[:, :128].reshape(16, 16, 128)
        ce[1, i] = edges[:, 128:].reshape(16, 16, 128)
    copies = []
    for sy in (-1, 0, 1):
        source_y, target_y, deep_y = ((0, 18, 2), (0, 2, 16), (14, 0, 2))[sy + 1]
        for sz in (-1, 0, 1):
            if sy == 0 and sz == 0:
                continue
            if sz == 0:
                src = cs.at[:, pl.ds(source_y + 2, deep_y), :, pl.ds(0, 256)]
                dst = cs.at[:, pl.ds(target_y, deep_y), :, pl.ds(0, 256)]
            else:
                src = ce.at[(sz + 1) // 2, :, pl.ds(source_y, deep_y)]
                dst = cs.at[:, pl.ds(target_y, deep_y), :, pl.ds(384 if sz < 0 else 256, 128)]
            n = len(copies)
            copies.append(((0, sy, sz), remote(src, dst, c_send.at[n], c_recv.at[n], beside(sy, sz))))
    start_c, wait_c = exchange(copies)
    start_c()

    @pl.when(gz == 0)
    def _():
        cs[:, :, :, 256:384] = jnp.zeros((2, 20, 16, 128), BF)

    @pl.when(gz == nz - 1)
    def _():
        cs[:, :, :, 384:512] = jnp.zeros((2, 20, 16, 128), BF)

    @pl.when(gy == 0)
    def _():
        cs[:, 0:2] = jnp.zeros((2, 2, 16, 512), BF)

    @pl.when(gy == ny - 1)
    def _():
        cs[:, 18:20] = jnp.zeros((2, 2, 16, 512), BF)

    loads[5].wait()
    wait_x()
    packed = jnp.concatenate([xraw[0:12].reshape(768, 256), xraw[12:24].reshape(768, 256)], axis=1)
    edges = mm(packed, perms[EDGE_F:EDGE_F + 512, :])
    esend[0] = edges[:, :128].astype(BF).reshape(12, 64, 128)
    esend[1] = edges[:, 128:].astype(BF).reshape(12, 64, 128)
    for x in range(XX // 2):
        kf[0, 4 * x:4 * x + 4, :] = edges[64 * x:64 * x + 4]
        kf[1, 4 * x:4 * x + 4, :] = edges[64 * x + 60:64 * x + 64]
    for y in range(2):
        for z in range(2):
            ksend[y, z] = kf[y, :, 128 * z:128 * z + 128].astype(BF)
    halves = mm(xraw[...].reshape(XX * FY, 256), perms[SPLIT_F:SPLIT_F + 256, :])
    state[:, 8:72, 0:256] = halves.reshape(XX, FY, 256)
    for x in range(XX):
        yf[0, 4 * x:4 * x + 4, :] = state[x, 8:12, 0:256]
        yf[1, 4 * x:4 * x + 4, :] = state[x, 68:72, 0:256]
    ysend[...] = yf[...].astype(BF)
    copies = []
    for sy in (-1, 0, 1):
        y = (sy + 1) // 2
        for sz in (-1, 0, 1):
            z = (sz + 1) // 2
            if sy == 0 and sz == 0:
                continue
            src, dst = ((esend.at[z], erecv.at[1 - z]) if sy == 0 else
                        (ysend.at[y], yrecv.at[1 - y]) if sz == 0 else
                        (ksend.at[y, z], krecv.at[1 - y, 1 - z]))
            n = len(copies)
            copies.append(((0, sy, sz), remote(src, dst, f_send.at[n], f_recv.at[n], beside(sy, sz))))
    start_f, wait_f = exchange(copies)
    start_f()
    for side in range(2):
        @pl.when(gz == side * (nz - 1))
        def _():
            erecv[side] = jnp.zeros((12, 64, 128), BF)
            krecv[:, side] = jnp.zeros((2, 48, 128), BF)

        @pl.when(gy == side * (ny - 1))
        def _():
            yrecv[side] = jnp.zeros((96, 256), BF)
            krecv[side] = jnp.zeros((2, 48, 128), BF)

    loads[6].wait()
    loads[7].wait()
    dup = (iota((16, 8), 0) % 8 == iota((16, 8), 1)).astype(F32).astype(BF)
    turned = lax.dot_general(dup, wf[...], nt, preferred_element_type=F32)
    own = iota((256, 128), 0) // 16 == iota((256, 128), 1) // 8
    tile8 = (iota((128, 256), 0) % 8 == iota((128, 256), 1) % 8).astype(F32).astype(BF)
    for j in range(7):
        cut = turned[:, 128 * j:128 * (j + 1)]
        spread = jnp.where(own, jnp.concatenate([cut] * 16, axis=0), 0.0).astype(BF)
        t_fine[256 * j:256 * (j + 1)] = mm(spread, tile8).astype(BF)
    for conv in range(4):
        build(bands_f, conv, t_fine, 16, 27 * conv, 3 * (conv % 2))
    last_band[...] = bands_f[3, :, 0:128]

    wait_c()
    left = iota((320, 128), 1) < 64
    for i, (one, two) in enumerate(((y1s, y2s), (d1s, d2s))):
        rows = cs[i].reshape(320, 512).astype(F32)
        low, high = rows[:, 256:384], rows[:, 384:512]
        one[:, 0:128] = rows[:, 0:128]
        one[:, 128:256] = jnp.where(left, low, high)
        two[:, 0:128] = rows[:, 128:256]
        two[:, 128:256] = jnp.where(left, high, low)

    def spread_x(values, target, count):
        row = iota((count * 16, 256), 0) % 16
        n = count * 16
        before = jnp.where(row == 0, 0.0, pltpu.roll(values, 1, 0))
        after = jnp.where(row == 15, 0.0, pltpu.roll(values, n - 1, 0))
        target[0:n, 0:256] = before.astype(BF)
        target[0:n, 256:512] = values.astype(BF)
        target[0:n, 512:768] = after.astype(BF)

    def conv_c(source, conv, count, width):
        lhs = jnp.concatenate([source[16 * p:16 * (p + count), :] for p in range(3)], axis=1)
        return mm(lhs, bands_c[conv][:, :width])

    spread_x(silu(y1s[...]), su1, 20)
    spread_x(d2s[...], sd2, 20)
    x2 = y2s[16:304] - conv_c(su1, 0, 18, 256)
    e = d1s[16:304] + silu_grad(y1s[16:304]) * conv_c(sd2, 1, 18, 256)
    z_low = jnp.where(gz == 0, 64, 0)
    z_high = jnp.where(gz == nz - 1, 64, 0)
    y_row = iota((288, 128), 0) // 16
    lane = iota((288, 128), 1)
    y_ok = (y_row >= jnp.where(gy == 0, 1, 0)) & (y_row < jnp.where(gy == ny - 1, 17, 18))
    h1_ok = y_ok & (lane >= z_low) & (lane < 128 - z_high)
    h2_ok = y_ok & (lane >= z_high) & (lane < 128 - z_low)
    x2_own = x2[16:272, 0:128]
    e_own = e[16:272, 0:128]
    u2 = silu(x2)
    u2 = jnp.concatenate([jnp.where(y_ok, u2[:, :128], 0.0), jnp.where(h2_ok, u2[:, 128:], 0.0)], axis=1)
    e = jnp.concatenate([jnp.where(y_ok, e[:, :128], 0.0), jnp.where(h1_ok, e[:, 128:], 0.0)], axis=1)
    spread_x(u2, su2, 18)
    spread_x(e, se, 18)

    place_lane = iota((32, 128), 1) // 32
    held = None
    for fg, (cot, source, first, z_order) in enumerate((
            (e_own, su2, 0, Z_H2), (d2s[32:288, 0:128], su1, 1, Z_H1))):
        turned_cot = jnp.transpose(cot).astype(BF)
        blocks = [mm(turned_cot, source[16 * (first + p):16 * (first + p + 16), :]) for p in range(3)]
        for q in range(3):
            for p in range(3):
                block = blocks[p][:, q * 256:(q + 1) * 256]
                for k in range(3):
                    acc = None
                    for z in range(4):
                        slot = z_order.index(z + k - 1)
                        at = 128 * (slot // 4)
                        term = jnp.where(place_lane == slot % 4, block[32 * z:32 * z + 32, at:at + 128], 0.0)
                        acc = term if acc is None else acc + term
                    acc = acc + pltpu.roll(acc, 64, 1)
                    acc = acc + pltpu.roll(acc, 32, 1)
                    t = fg * 27 + q * 9 + p * 3 + k
                    held = acc if t % 4 == 0 else jnp.where(place_lane == t % 4, acc, held)
                    if t % 4 == 3 or t == 53:
                        part[t // 4 * 32:t // 4 * 32 + 32, :] = held

    ch = 512 // wide
    mine = pl.ds(pl.multiple_of(me_wide * ch, 8), ch)
    sends1 = []
    for d in range(1, wide):
        theirs = pl.ds(pl.multiple_of(lax.rem(me_wide + d, wide) * ch, 8), ch)
        sends1.append(remote(part.at[theirs], r1.at[d], p1_send.at[d], p1_recv.at[d], peer_wide(d)))
    for copy in sends1:
        copy.start()

    x1 = y1s[32:288, 0:128] - conv_c(su2, 2, 16, 128)
    dx2 = d2s[32:288, 0:128] + silu_grad(x2_own) * conv_c(se, 3, 16, 128)
    join = perms[JOIN_C:JOIN_C + 256, :]
    for one, two, target in ((x1, x2_own, rb_s), (e_own, dx2, gi_s)):
        both = jnp.concatenate([one.astype(BF), two.astype(BF)], axis=1)
        target[...] = mm(swap, mm(both, join).astype(BF)).astype(BF).reshape(16, 16, 256)

    wait_f()
    def rims(from_left, from_right, count):
        left_lane = iota((count, 128), 1) < 64
        return (jnp.where(left_lane, from_left, pltpu.roll(from_right, 64, 1)),
                jnp.where(left_lane, pltpu.roll(from_left, 64, 1), from_right))

    early, late = rims(erecv[0].reshape(768, 128).astype(F32), erecv[1].reshape(768, 128).astype(F32), 768)
    state[0:12, 8:72, 256:384] = early.reshape(12, 64, 128)
    state[12:24, 8:72, 256:384] = late.reshape(12, 64, 128)
    for y, row in ((0, 4), (1, 72)):
        early, late = rims(krecv[y, 0].astype(F32), krecv[y, 1].astype(F32), 48)
        edge = yrecv[y].astype(F32)
        for x in range(XX):
            state[x, row:row + 4, 0:256] = edge[4 * x:4 * x + 4]
        for x in range(XX // 2):
            state[x, row:row + 4, 256:384] = early[4 * x:4 * x + 4]
            state[x + 12, row:row + 4, 256:384] = late[4 * x:4 * x + 4]

    limits = fine_limits(sizes)

    def fine_conv(step, column, conv):
        def spread(x, carry):
            v = fine_input(state, x, column, limits)
            u_fine[x, :, 0:256] = pltpu.roll(v, 1, 0).astype(BF)
            u_fine[x, :, 256:512] = v.astype(BF)
            u_fine[x, :, 512:768] = pltpu.roll(v, YY - 1, 0).astype(BF)
            return carry
        lax.fori_loop(step, XX - step, spread, 0)
        half = (XX - 2 * step - 2) // 2
        into = 128 - column
        for part_index in range(2):
            x0 = step + part_index * half
            lhs = jnp.concatenate(
                [u_fine[x0 + p:x0 + p + half].reshape(half * YY, 768) for p in range(3)], axis=1)
            out = mm(lhs, bands_f[conv]).reshape(half, YY, 256)
            state[x0 + 1:x0 + 1 + half, :, into:into + 128] += out[:, :, :128]
            state[x0 + 1:x0 + 1 + half, :, 256:384] += out[:, :, 128:]

    fine_conv(0, 0, 0)

    for copy in sends1:
        copy.wait()
    total = part[mine, :]
    for d in range(1, wide):
        total = total + r1[d]
    red[...] = total
    r2[me_deep] = total
    sends2 = [remote(red, r2.at[me_deep], p2_send.at[d], p2_recv.at[d], peer_deep(d)) for d in range(1, deep)]
    for copy in sends2:
        copy.start()

    fine_conv(1, 128, 1)

    for copy in sends2:
        copy.wait()
    total = r2[0]
    for i in range(1, deep):
        total = total + r2[i]
    red_bf[...] = total.astype(BF)
    final[mine, :] = total.astype(BF)
    sends3 = [remote(red_bf, final.at[mine], p3_send.at[d], p3_recv.at[d], peer_wide(d)) for d in range(1, wide)]
    for copy in sends3:
        copy.start()

    fine_conv(2, 0, 2)

    for copy in sends3:
        copy.wait()
    for g in range(14):
        rows = final[32 * g:32 * g + 32, :].astype(F32)
        for j in range(4):
            t = 4 * g + j
            if t < 54:
                turned_rows = rows if j == 0 else pltpu.roll(rows, 128 - 32 * j, 1)
                wg_s[t] = turned_rows[:, :32]


def finish(sizes, state, last_band, rb_s, gi_s, wg_s, join_h,
           fine_out, rebuilt, grads_in, wg_out, u_last, join, fo_s, sems):
    nx, ny, nz = sizes
    copies = [pltpu.make_async_copy(s, t, sems.at[i]) for i, (s, t) in enumerate((
        (join_h, join), (rb_s, rebuilt.at[0]), (gi_s, grads_in.at[0]), (wg_s, wg_out)))]
    for copy in copies:
        copy.start()
    limits = fine_limits(sizes)

    def spread(x, carry):
        v = fine_input(state, x, 128, limits)
        u_last[x, :, 0:256] = pltpu.roll(v, 1, 0)[8:72].astype(BF)
        u_last[x, :, 256:512] = v[8:72].astype(BF)
        u_last[x, :, 512:768] = pltpu.roll(v, YY - 1, 0)[8:72].astype(BF)
        return carry
    lax.fori_loop(3, XX - 3, spread, 0)
    copies[0].wait()
    for c in range(2):
        x0 = 3 + 8 * c
        lhs = jnp.concatenate(
            [u_last[x0 + p:x0 + p + 8].reshape(512, 768) for p in range(3)], axis=1)
        two = mm(lhs, last_band[...]).reshape(8, FY, 128) + state[x0 + 1:x0 + 9, 8:72, 0:128]
        one = state[x0 + 1:x0 + 9, 8:72, 128:256]
        both = jnp.concatenate([two, one], axis=2).astype(BF).reshape(512, 256)
        fo_s[8 * c:8 * c + 8] = mm(both, join[...]).astype(BF).reshape(8, FY, 256)
        copies.append(pltpu.make_async_copy(
            fo_s.at[pl.ds(8 * c, 8)], fine_out.at[pl.ds(8 * c, 8)], sems.at[4 + c]))
        copies[-1].start()
    for copy in copies[1:]:
        copy.wait()


def on_device(sizes, fine_in, fine_weights, coarse_out, coarse_cot, coarse_weights):
    nx, ny, nz = sizes
    wide, deep = ny * (nz // 2), nx * 2
    ch = 512 // wide
    fine_w = jnp.transpose(fine_weights, (0, 1, 4, 5, 6, 2, 3)).reshape(864, 8)
    coarse_w = jnp.transpose(coarse_weights, (0, 3, 4, 5, 1, 2)).reshape(1728, 32)
    vm, dma = pltpu.VMEM, pltpu.SemaphoreType.DMA
    hbm = pl.BlockSpec(memory_space=pltpu.HBM)
    scratch = [
        vm((XX, FY, 256), BF), vm((2, CX, CY, 256), BF), vm((896, 8), BF), vm((1792, 32), BF),
        vm((3072, 256), BF), vm((2048, 256), BF),
        vm((1792, 256), BF), vm((1792, 256), BF), vm((1792, 256), BF),
        vm((4, 2304, 256), BF), vm((4, 2304, 256), BF),
        vm((XX, YY, 768), BF),
        vm((2, 12, 64, 128), BF), vm((2, 12, 64, 128), BF),
        vm((2, 96, 256), F32), vm((2, 96, 256), BF), vm((2, 96, 256), BF),
        vm((2, 48, 256), F32), vm((2, 2, 48, 128), BF), vm((2, 2, 48, 128), BF),
        vm((2, 20, 16, 512), BF), vm((2, 2, 16, 16, 128), BF),
        vm((320, 256), F32), vm((320, 256), F32), vm((320, 256), F32), vm((320, 256), F32),
        vm((320, 768), BF), vm((320, 768), BF), vm((288, 768), BF), vm((288, 768), BF),
        vm((512, 128), F32), vm((wide, ch, 128), F32), vm((deep, ch, 128), F32),
        vm((ch, 128), F32), vm((ch, 128), BF), vm((512, 128), BF),
        dma((8,)), dma((nx, 2)), dma((nx, 2)), dma((2,)), dma((2,)),
        dma((8,)), dma((8,)), dma((8,)), dma((8,)),
        dma((wide,)), dma((wide,)), dma((deep,)), dma((deep,)), dma((wide,)), dma((wide,)),
    ]
    inside = pl.BlockSpec(memory_space=pltpu.VMEM)
    held = pl.pallas_call(
        functools.partial(kernel, sizes),
        out_shape=(vm((XX, YY, 384), F32), vm((2304, 128), BF), vm((16, 16, 256), BF),
                   vm((16, 16, 256), BF), vm((54, 32, 32), F32)),
        in_specs=[hbm] * 7,
        out_specs=(inside,) * 5,
        scratch_shapes=scratch,
        compiler_params=pltpu.CompilerParams(
            collective_id=0, has_side_effects=True, vmem_limit_bytes=44 * 1024 * 1024),
    )(*(pltpu.with_memory_space_constraint(v, pltpu.HBM) for v in (
        fine_in, fine_w, coarse_out, coarse_cot, coarse_w,
        jnp.asarray(MASKS, BF), jnp.asarray(PERMS, BF))))
    fine_out, rebuilt, grads_in, wg = pl.pallas_call(
        functools.partial(finish, sizes),
        out_shape=(
            jax.ShapeDtypeStruct((FX, FY, 256), BF),
            jax.ShapeDtypeStruct((1, 16, 16, 256), BF),
            jax.ShapeDtypeStruct((1, 16, 16, 256), BF),
            jax.ShapeDtypeStruct((54, 32, 32), F32),
        ),
        in_specs=[inside] * 5 + [hbm],
        out_specs=(hbm,) * 4,
        scratch_shapes=[vm((XX, FY, 768), BF), vm((256, 256), BF), vm((FX, FY, 256), BF), dma((6,))],
        compiler_params=pltpu.CompilerParams(vmem_limit_bytes=24 * 1024 * 1024),
    )(*held, jnp.asarray(PERMS[JOIN_F:JOIN_F + 256], BF))
    wg = jnp.transpose(wg.reshape(2, 3, 3, 3, 32, 32), (0, 4, 5, 1, 2, 3))
    return fine_out, rebuilt, grads_in, wg


def solution(mesh):
    placed = (P("gx", "gy", "gz"), P(), P(None, "gx", "gy", "gz"), P(None, "gx", "gy", "gz"), P())
    sizes = tuple(mesh.shape[axis] for axis in ("gx", "gy", "gz"))
    return jax.shard_map(
        functools.partial(on_device, sizes),
        mesh=mesh,
        in_specs=placed,
        out_specs=(P("gx", "gy", "gz"), P("gx", None, "gy", "gz"), P("gx", None, "gy", "gz"), P()),
        check_vma=False,
    )
```

time: 979 us -> 50.3 us (0.05); the launches traced: 965 us -> 50.2 us
  local copies, waits for them, and re-layouts: 511 us -> 0.01 us
  matrix products: 141 us -> 0 us
  waiting for transfers between devices: 133 us -> 0 us
  starting transfers between devices: 122 us -> 0 us
  Pallas kernels: 0 us -> 49.6 us
  other arithmetic: 39.7 us -> 0 us
  between operations: 17.9 us -> 0.66 us
    convert_element_type x108 -> x0, local copies, waits for them, and re-layouts: 247 us -> none  [band_for(): table.reshape((width + 2) * in_ch, width * out_ch).astype(jnp.bfloat16)]
    dot_general x180 -> x0, matrix products: 141 us -> none  [the longest x72 75 us: band_for(): jnp.einsum('ock,kiz->iczo', weight_ab.astype(jnp.float32), tap_table(widt...]
    psum x1 -> x0, waiting for transfers between devices: 124 us -> none  [on_device(): weight_grads = lax.psum(grad_terms, ('gx', 'gy', 'gz'))]
    ppermute x36 -> x0, starting transfers between devices: 115 us -> none  [the longest x18 85.8 us: extended(): lax.ppermute(lax.slice_in_dim(block, block.shape[dim] - width, None, axis...]
    reshape x86 -> x0, local copies, waits for them, and re-layouts: 106 us -> none  [the longest x72 93.1 us: conv_padded(): padded[:, a:a + sx, b:b + sy, start:start + width + 2, :]]
    slice x63 -> x0, local copies, waits for them, and re-layouts: 92.5 us -> none  [the longest x42 65.7 us: conv_padded(): padded[:, a:a + sx, b:b + sy, start:start + width + 2, :]]
    pallas_call x0 -> x2, Pallas kernels: none -> 49.6 us  [the longest x1 46.1 us: on_device(): pl.pallas_call(functools.partial(kernel, sizes), out_shape=(vm((XX, YY, 3...]
    ppermute x8 -> x0, local copies, waits for them, and re-layouts: 19.6 us -> none  [the longest x4 10.6 us: extended(): lax.ppermute(lax.slice_in_dim(block, 0, width, axis=dim), axis, backward)]
  transfers between devices with their start and end apart: 39 -> 0, of which waited for: 5 -> 0; matrix products, arithmetic and copies ran while one was open for 64% -> 0% of each run, Pallas kernels for 0% -> 0%
where the time goes in v1:
time: 50.3 us; the launch traced here: 50.2 us
  Pallas kernels  49.6 us (99%)
  between operations  0.66 us (1%)
    pallas_call x1, Pallas kernels, on_device(): pl.pallas_call(functools.partial(kernel, sizes), out_shape=(vm((XX, YY, 3...  46.1 us
    pallas_call x1, Pallas kernels, on_device(): pl.pallas_call(functools.partial(finish, sizes), out_shape=(jax.ShapeDtyp...  3.42 us

profile of v1, /device:TPU:1, one launch (start us, length us, event | category | flops | bytes accessed | tf_op | source)
XLA Modules:
  0.0 50.2 jit_solution(4650341120031488096)
XLA Ops:
  0.6 0.0 copy-start
  0.6 46.1 %shard_map.111 = (f32[24,80,384]{2,1,0:T(8,128)S(1)}, bf16[2304,128]{1,0:T(8,128)(2,1)S(1)}, bf16[16,16,256]{2,1,0:T(8,128)(2,1)S(1)}, bf16[16,16,256]{2,1,0:T(8,128)(2,1)S(1)}, f32[54,32,32]{2,1,0:T(8,128)S(1)}) custom-call(bf16[16,64,256]{2,1,0:T(8,128)(2,1)} %fine_in.1, bf16[864,8]{1,0:T(8,128)(2,1)} %bitcast.10, bf16[4,4,16,256]{3,2,1,0:T(8,128)(2,1)} %c_out.1, ...), custom_call_target="tpu_custom_call" | custom-call | tf_op jit(solution)/shard_map/pallas_call | solution.py:590
  46.8 0.0 copy-done
  46.8 3.4 %shard_map.112 = (bf16[16,64,256]{2,1,0:T(8,128)(2,1)}, bf16[1,16,16,256]{3,2,1,0:T(8,128)(2,1)}, bf16[1,16,16,256]{3,2,1,0:T(8,128)(2,1)}, f32[54,32,32]{2,1,0:T(8,128)}) custom-call(f32[24,80,384]{2,1,0:T(8,128)S(1)} %get-tuple-element.13.state, bf16[2304,128]{1,0:T(8,128)(2,1)S(1)} %get-tuple-element.14.last_band, ...), custom_call_target="tpu_custom_call" | custom-call | tf_op jit(solution)/shard_map/pallas_call | solution.py:602
Async XLA Ops:
  0.6 46.2 %copy-start = (bf16[256,256]{1,0:T(8,128)(2,1)S(1)}, bf16[256,256]{1,0:T(8,128)(2,1)}, u32[]{:S(2)}) copy-start(bf16[256,256]{1,0:T(8,128)(2,1)} %constant.8.clone.join_h) | copy-start | bytes 393220

commit v2 on v1

--- a/solution.py
+++ b/solution.py
@@ -23,25 +23,7 @@
 Z_H2 = [0, 1, 2, 3, 4, 5, -2, -1]
 
 
-def band_masks(z_in, z_out, width):
-    table = np.zeros((3, 256, 256), np.float32)
-    for i, zi in enumerate(z_in):
-        for o, zo in enumerate(z_out):
-            if zi == NONE or zo == NONE:
-                continue
-            k = zi - zo + 1
-            if 0 <= k <= 2:
-                table[k, i * width:(i + 1) * width, o * width:(o + 1) * width] = 1.0
-    return table
-
-
 def constants():
-    masks = np.stack([
-        band_masks(Z_X2, Z_X1, 8),
-        band_masks(Z_X1, Z_X2, 8),
-        band_masks(Z_H1, Z_H2, 32),
-        band_masks(Z_H2, Z_H1, 32),
-    ])
     split_fine = np.zeros((256, 256), np.float32)
     for z in range(16):
         for c in range(8):
@@ -70,14 +52,13 @@
             else:
                 split_coarse[z * 64 + c, 384 + (z - 2) * 32 + c] = 1.0
                 split_coarse[z * 64 + 32 + c, 384 + 64 + (z - 2) * 32 + c] = 1.0
-    perms = np.concatenate([
+    return np.concatenate([
         split_fine, split_fine.T, edge_fine, swap,
         split_coarse[:, :256], split_coarse[:, 256:], split_coarse[:, :256].T,
     ])
-    return masks.reshape(12 * 256, 256), perms
-
-
-MASKS, PERMS = constants()
+
+
+PERMS = constants()
 SPLIT_F, JOIN_F, EDGE_F, SWAP, SPLIT_C, EDGE_C, JOIN_C = 0, 256, 512, 1024, 1280, 1536, 1792
 
 
@@ -97,6 +78,84 @@
 
 def iota(shape, dim):
     return lax.broadcasted_iota(jnp.int32, shape, dim)
+
+
+def bands(fine_w, coarse_w, bands_f, bands_c, last_band, wf, wc, t_fine, t_fwd, t_nat, sems):
+    loads = [pltpu.make_async_copy(coarse_w, wc.at[pl.ds(0, 1728)], sems.at[0]),
+             pltpu.make_async_copy(fine_w, wf.at[pl.ds(0, 864)], sems.at[1])]
+    for copy in loads:
+        copy.start()
+    wf[864:896] = jnp.zeros((32, 8), BF)
+    wc[1728:1792] = jnp.zeros((64, 32), BF)
+    nt = (((1,), (1,)), ((), ()))
+
+    def same(shape, f, g):
+        return f(iota(shape, 0)) == g(iota(shape, 1))
+
+    def one_hot(match):
+        return match.astype(F32).astype(BF)
+
+    def tile_taps(taps, width, target):
+        eye = one_hot(same((width, width), lambda r: r, lambda l: l))
+        turned = lax.dot_general(eye, taps[...], nt, preferred_element_type=F32)
+        own = same((128, 128), lambda r: r // width, lambda l: l // width)
+        repeat = one_hot(same((128, 128), lambda r: r % width, lambda l: l % width))
+        for j in range(taps.shape[0] // 128):
+            cut = turned[:, 128 * j:128 * (j + 1)]
+            spread = jnp.where(own, jnp.concatenate([cut] * (128 // width), axis=0), 0.0).astype(BF)
+            target[128 * j:128 * (j + 1)] = mm(spread, repeat)
+
+    def build(store, taps, width, first, z_in, z_out, columns, flip=False):
+        slots = 128 // width
+        group = max(16 // width, 1)
+
+        def body(i, carry):
+            p, q = i // 3, i % 3
+            base = p * 9 + q * 3 if width == 8 else q * 9 + p * 3
+            if flip:
+                base = 24 - base
+            tiles = [taps[pl.ds(pl.multiple_of((first + base + (2 - k if flip else k)) * width, width), width), :]
+                     for k in range(3)]
+            lane_slot = iota((width, 128), 1) // width
+            for start in range(0, 2 * slots, group):
+                for column in range(columns):
+                    pieces = []
+                    for z in z_in[start:start + group]:
+                        piece = jnp.zeros((width, 128), F32)
+                        for k in range(3):
+                            if z != NONE and z + 1 - k in z_out:
+                                slot = z_out.index(z + 1 - k)
+                                if slot // slots == column:
+                                    piece = jnp.where(lane_slot == slot % slots, tiles[k], piece)
+                        pieces.append(piece)
+                    value = pieces[0] if group == 1 else jnp.concatenate(pieces, axis=0)
+                    store(pl.ds(pl.multiple_of(i * 256 + start * width, 16), group * width),
+                          slice(128 * column, 128 * column + 128), value.astype(BF))
+            return carry
+        lax.fori_loop(0, 9, body, 0)
+
+    def into(target, conv):
+        def store(rows, lanes, value):
+            target[conv, rows, lanes] = value
+        return store
+
+    def into_last(rows, lanes, value):
+        last_band[rows, lanes] = value
+
+    loads[0].wait()
+    repeat = one_hot(same((32, 128), lambda r: r, lambda l: l % 32))
+    t_nat[...] = mm(wc[...], repeat)
+    tile_taps(wc, 32, t_fwd)
+    build(into(bands_c, 0), t_fwd, 32, 27, Z_H1, Z_H2, 2)
+    build(into(bands_c, 1), t_nat, 32, 27, Z_H2, Z_H1, 2, True)
+    build(into(bands_c, 2), t_fwd, 32, 0, Z_H2, Z_H1, 1)
+    build(into(bands_c, 3), t_nat, 32, 0, Z_H1, Z_H2, 1, True)
+    loads[1].wait()
+    tile_taps(wf, 8, t_fine)
+    build(into(bands_f, 0), t_fine, 8, 0, Z_X2, Z_X1, 2)
+    build(into(bands_f, 1), t_fine, 8, 27, Z_X1, Z_X2, 2)
+    build(into(bands_f, 2), t_fine, 8, 54, Z_X2, Z_X1, 2)
+    build(into_last, t_fine, 8, 81, Z_X1, Z_X2, 1)
 
 
 def fine_limits(sizes):
@@ -119,10 +178,9 @@
     return jnp.concatenate([own, rim], axis=1)
 
 
-def kernel(sizes, fine_in, fine_w, c_out, c_cot, coarse_w, masks_h, perms_h,
-           state, last_band, rb_s, gi_s, wg_s,
-           xraw, craw, wf, wc, masks, perms, t_fine, t_fwd, t_nat,
-           bands_f, bands_c, u_fine, esend, erecv, yf, ysend, yrecv, kf, ksend, krecv,
+def kernel(sizes, fine_in, c_out, c_cot, perms_h, bands_f, bands_c,
+           state, rb_s, gi_s, wg_s,
+           xraw, craw, perms, u_fine, esend, erecv, yf, ysend, yrecv, kf, ksend, krecv,
            cs, ce, y1s, y2s, d1s, d2s, su1, sd2, su2, se,
            part, r1, r2, red, red_bf, final,
            load_sem, in_send, in_recv, x_send, x_recv, c_send, c_recv, f_send, f_recv,
@@ -156,22 +214,16 @@
             pl.semaphore_signal(barrier, inc=1, device_id=to, device_id_type=MESH)
 
     loads = [
-        (coarse_w, wc.at[pl.ds(0, 1728)]),
-        (masks_h.at[pl.ds(1536, 1536)], masks.at[pl.ds(1536, 1536)]),
         (perms_h, perms),
         (c_out.at[gx], craw.at[0, pl.ds(gx * 4, 4)]),
         (c_cot.at[gx], craw.at[1, pl.ds(gx * 4, 4)]),
         (fine_in, xraw.at[pl.ds(FH, FX)]),
-        (fine_w, wf.at[pl.ds(0, 864)]),
-        (masks_h.at[pl.ds(0, 1536)], masks.at[pl.ds(0, 1536)]),
     ]
     loads = [pltpu.make_async_copy(s, t, load_sem.at[i]) for i, (s, t) in enumerate(loads)]
     for copy in loads:
         copy.start()
     state[:, 0:8, :] = jnp.zeros((XX, 8, 384), F32)
     state[:, 72:80, :] = jnp.zeros((XX, 8, 384), F32)
-    wf[864:896] = jnp.zeros((32, 8), BF)
-    wc[1728:1792] = jnp.zeros((64, 32), BF)
     part[14 * 32:, :] = jnp.zeros((64, 128), F32)
     pl.semaphore_wait(barrier, wide - 1 + deep - 1 + 6)
 
@@ -230,44 +282,7 @@
     def _():
         xraw[FX + FH:] = jnp.zeros((FH, FY, 256), BF)
 
-    loads[0].wait()
-    nt = (((1,), (1,)), ((), ()))
-    eye32 = (iota((32, 32), 0) == iota((32, 32), 1)).astype(F32).astype(BF)
-    tile32 = (iota((32, 256), 0) == iota((32, 256), 1) % 32).astype(F32).astype(BF)
-    t_nat[...] = mm(wc[...], tile32).astype(BF)
-    turned = lax.dot_general(eye32, wc[...], nt, preferred_element_type=F32)
-    own = iota((128, 128), 0) // 32 == iota((128, 128), 1) // 32
-    tile128 = (iota((128, 256), 0) % 32 == iota((128, 256), 1) % 32).astype(F32).astype(BF)
-    for j in range(14):
-        cut = turned[:, 128 * j:128 * (j + 1)]
-        spread = jnp.where(own, jnp.concatenate([cut] * 4, axis=0), 0.0).astype(BF)
-        t_fwd[128 * j:128 * (j + 1)] = mm(spread, tile128).astype(BF)
-
-    def build(bands, conv, taps, rows, first, mask_base, flip=False):
-        def body(i, carry):
-            p, q = i // 3, i % 3
-            base = p * 9 + q * 3 if rows == 16 else q * 9 + p * 3
-            if flip:
-                base = 24 - base
-            tiles = [taps[pl.ds(pl.multiple_of((first + base + (2 - k if flip else k)) * rows, rows), rows), :]
-                     for k in range(3)]
-            for r in range(0, 256, rows):
-                total = None
-                for k in range(3):
-                    at = (mask_base + k) * 256 + r
-                    term = masks[at:at + rows, :] * tiles[k]
-                    total = term if total is None else total + term
-                bands[conv, pl.ds(pl.multiple_of(i * 256 + r, rows), rows), :] = total
-            return carry
-        lax.fori_loop(0, 9, body, 0)
-
-    loads[1].wait()
-    build(bands_c, 0, t_fwd, 32, 27, 6)
-    build(bands_c, 1, t_nat, 32, 27, 9, True)
-    build(bands_c, 2, t_fwd, 32, 0, 9)
-    build(bands_c, 3, t_nat, 32, 0, 6, True)
-
-    for copy in loads[2:5]:
+    for copy in loads[0:3]:
         copy.wait()
     for copy in gathers:
         copy.wait()
@@ -313,7 +328,7 @@
     def _():
         cs[:, 18:20] = jnp.zeros((2, 2, 16, 512), BF)
 
-    loads[5].wait()
+    loads[3].wait()
     wait_x()
     packed = jnp.concatenate([xraw[0:12].reshape(768, 256), xraw[12:24].reshape(768, 256)], axis=1)
     edges = mm(packed, perms[EDGE_F:EDGE_F + 512, :])
@@ -356,20 +371,6 @@
             yrecv[side] = jnp.zeros((96, 256), BF)
             krecv[side] = jnp.zeros((2, 48, 128), BF)
 
-    loads[6].wait()
-    loads[7].wait()
-    dup = (iota((16, 8), 0) % 8 == iota((16, 8), 1)).astype(F32).astype(BF)
-    turned = lax.dot_general(dup, wf[...], nt, preferred_element_type=F32)
-    own = iota((256, 128), 0) // 16 == iota((256, 128), 1) // 8
-    tile8 = (iota((128, 256), 0) % 8 == iota((128, 256), 1) % 8).astype(F32).astype(BF)
-    for j in range(7):
-        cut = turned[:, 128 * j:128 * (j + 1)]
-        spread = jnp.where(own, jnp.concatenate([cut] * 16, axis=0), 0.0).astype(BF)
-        t_fine[256 * j:256 * (j + 1)] = mm(spread, tile8).astype(BF)
-    for conv in range(4):
-        build(bands_f, conv, t_fine, 16, 27 * conv, 3 * (conv % 2))
-    last_band[...] = bands_f[3, :, 0:128]
-
     wait_c()
     left = iota((320, 128), 1) < 64
     for i, (one, two) in enumerate(((y1s, y2s), (d1s, d2s))):
@@ -391,7 +392,7 @@
 
     def conv_c(source, conv, count, width):
         lhs = jnp.concatenate([source[16 * p:16 * (p + count), :] for p in range(3)], axis=1)
-        return mm(lhs, bands_c[conv][:, :width])
+        return mm(lhs, bands_c[conv, :, 0:width])
 
     spread_x(silu(y1s[...]), su1, 20)
     spread_x(d2s[...], sd2, 20)
@@ -569,10 +570,7 @@
     vm, dma = pltpu.VMEM, pltpu.SemaphoreType.DMA
     hbm = pl.BlockSpec(memory_space=pltpu.HBM)
     scratch = [
-        vm((XX, FY, 256), BF), vm((2, CX, CY, 256), BF), vm((896, 8), BF), vm((1792, 32), BF),
-        vm((3072, 256), BF), vm((2048, 256), BF),
-        vm((1792, 256), BF), vm((1792, 256), BF), vm((1792, 256), BF),
-        vm((4, 2304, 256), BF), vm((4, 2304, 256), BF),
+        vm((XX, FY, 256), BF), vm((2, CX, CY, 256), BF), vm((2048, 256), BF),
         vm((XX, YY, 768), BF),
         vm((2, 12, 64, 128), BF), vm((2, 12, 64, 128), BF),
         vm((2, 96, 256), F32), vm((2, 96, 256), BF), vm((2, 96, 256), BF),
@@ -582,23 +580,32 @@
         vm((320, 768), BF), vm((320, 768), BF), vm((288, 768), BF), vm((288, 768), BF),
         vm((512, 128), F32), vm((wide, ch, 128), F32), vm((deep, ch, 128), F32),
         vm((ch, 128), F32), vm((ch, 128), BF), vm((512, 128), BF),
-        dma((8,)), dma((nx, 2)), dma((nx, 2)), dma((2,)), dma((2,)),
+        dma((4,)), dma((nx, 2)), dma((nx, 2)), dma((2,)), dma((2,)),
         dma((8,)), dma((8,)), dma((8,)), dma((8,)),
         dma((wide,)), dma((wide,)), dma((deep,)), dma((deep,)), dma((wide,)), dma((wide,)),
     ]
     inside = pl.BlockSpec(memory_space=pltpu.VMEM)
+    in_hbm = functools.partial(pltpu.with_memory_space_constraint, memory_space=pltpu.HBM)
+    perms = jnp.asarray(PERMS, BF)
+    bands_f, bands_c, last_band = pl.pallas_call(
+        bands,
+        out_shape=(vm((3, 2304, 256), BF), vm((4, 2304, 256), BF), vm((2304, 128), BF)),
+        in_specs=[hbm] * 2,
+        out_specs=(inside,) * 3,
+        scratch_shapes=[vm((896, 8), BF), vm((1792, 32), BF), vm((896, 128), F32),
+                        vm((1792, 128), F32), vm((1792, 128), F32), dma((2,))],
+        compiler_params=pltpu.CompilerParams(vmem_limit_bytes=24 * 1024 * 1024),
+    )(in_hbm(fine_w), in_hbm(coarse_w))
     held = pl.pallas_call(
         functools.partial(kernel, sizes),
-        out_shape=(vm((XX, YY, 384), F32), vm((2304, 128), BF), vm((16, 16, 256), BF),
+        out_shape=(vm((XX, YY, 384), F32), vm((16, 16, 256), BF),
                    vm((16, 16, 256), BF), vm((54, 32, 32), F32)),
-        in_specs=[hbm] * 7,
-        out_specs=(inside,) * 5,
+        in_specs=[hbm] * 4 + [inside] * 2,
+        out_specs=(inside,) * 4,
         scratch_shapes=scratch,
         compiler_params=pltpu.CompilerParams(
-            collective_id=0, has_side_effects=True, vmem_limit_bytes=44 * 1024 * 1024),
-    )(*(pltpu.with_memory_space_constraint(v, pltpu.HBM) for v in (
-        fine_in, fine_w, coarse_out, coarse_cot, coarse_w,
-        jnp.asarray(MASKS, BF), jnp.asarray(PERMS, BF))))
+            collective_id=0, has_side_effects=True, vmem_limit_bytes=32 * 1024 * 1024),
+    )(in_hbm(fine_in), in_hbm(coarse_out), in_hbm(coarse_cot), in_hbm(perms), bands_f, bands_c)
     fine_out, rebuilt, grads_in, wg = pl.pallas_call(
         functools.partial(finish, sizes),
         out_shape=(
@@ -611,7 +618,7 @@
         out_specs=(hbm,) * 4,
         scratch_shapes=[vm((XX, FY, 768), BF), vm((256, 256), BF), vm((FX, FY, 256), BF), dma((6,))],
         compiler_params=pltpu.CompilerParams(vmem_limit_bytes=24 * 1024 * 1024),
-    )(*held, jnp.asarray(PERMS[JOIN_F:JOIN_F + 256], BF))
+    )(held[0], last_band, *held[1:], jnp.asarray(PERMS[JOIN_F:JOIN_F + 256], BF))
     wg = jnp.transpose(wg.reshape(2, 3, 3, 3, 32, 32), (0, 4, 5, 1, 2, 3))
     return fine_out, rebuilt, grads_in, wg
 

time: 50.3 us -> 54.7 us (1.087)
  Pallas kernels: 49.6 us -> 53.9 us
    pallas_call x0 -> x1, Pallas kernels: none -> 4.27 us  [on_device(): pl.pallas_call(bands, out_shape=(vm((3, 2304, 256), BF), vm((4, 2304, 256...]
where the time goes in v2:
time: 54.7 us; the launch traced here: 54.5 us
  Pallas kernels  53.9 us (99%)
  between operations  0.66 us (1%)
    pallas_call x1, Pallas kernels, on_device(): pl.pallas_call(functools.partial(kernel, sizes), out_shape=(vm((XX, YY, 3...  46.2 us
    pallas_call x1, Pallas kernels, on_device(): pl.pallas_call(bands, out_shape=(vm((3, 2304, 256), BF), vm((4, 2304, 256...  4.27 us
    pallas_call x1, Pallas kernels, on_device(): pl.pallas_call(functools.partial(finish, sizes), out_shape=(jax.ShapeDtyp...  3.42 us

profile of v2, /device:TPU:1, one launch (start us, length us, event | category | flops | bytes accessed | tf_op | source)
XLA Modules:
  0.0 54.5 jit_solution(4268147624920055036)
XLA Ops:
  0.6 4.3 %shard_map.102 = (bf16[3,2304,256]{2,1,0:T(8,128)(2,1)S(1)}, bf16[4,2304,256]{2,1,0:T(8,128)(2,1)S(1)}, bf16[2304,128]{1,0:T(8,128)(2,1)S(1)}) custom-call(bf16[864,8]{1,0:T(8,128)(2,1)} %bitcast.10, bf16[1728,32]{1,0:T(8,128)(2,1)} %bitcast.9), custom_call_target="tpu_custom_call" | custom-call | tf_op jit(solution)/shard_map/pallas_call | solution.py:590
  4.9 0.0 copy-start
  4.9 46.2 %shard_map.103 = (f32[24,80,384]{2,1,0:T(8,128)S(1)}, bf16[16,16,256]{2,1,0:T(8,128)(2,1)S(1)}, bf16[16,16,256]{2,1,0:T(8,128)(2,1)S(1)}, f32[54,32,32]{2,1,0:T(8,128)S(1)}) custom-call(bf16[16,64,256]{2,1,0:T(8,128)(2,1)} %fine_in.1, bf16[4,4,16,256]{3,2,1,0:T(8,128)(2,1)} %c_out.1, bf16[4,4,16,256]{3,2,1,0:T(8,128)(2,1)} %c_cot.1, ...), custom_call_target="tpu_custom_call" | custom-call | tf_op jit(solution)/shard_map/pallas_call | solution.py:599
  51.1 0.0 copy-done
  51.1 3.4 %shard_map.104 = (bf16[16,64,256]{2,1,0:T(8,128)(2,1)}, bf16[1,16,16,256]{3,2,1,0:T(8,128)(2,1)}, bf16[1,16,16,256]{3,2,1,0:T(8,128)(2,1)}, f32[54,32,32]{2,1,0:T(8,128)}) custom-call(f32[24,80,384]{2,1,0:T(8,128)S(1)} %get-tuple-element.17.state, bf16[2304,128]{1,0:T(8,128)(2,1)S(1)} %get-tuple-element.18.last_band, ...), custom_call_target="tpu_custom_call" | custom-call | tf_op jit(solution)/shard_map/pallas_call | solution.py:609
Async XLA Ops:
  4.9 46.2 %copy-start = (bf16[256,256]{1,0:T(8,128)(2,1)S(1)}, bf16[256,256]{1,0:T(8,128)(2,1)}, u32[]{:S(2)}) copy-start(bf16[256,256]{1,0:T(8,128)(2,1)} %constant.5.clone.join_h) | copy-start | bytes 393220

commit v3 on v2

--- a/solution.py
+++ b/solution.py
@@ -19,8 +19,8 @@
 
 Z_X2 = list(range(16)) + [-4, -3, -2, -1] + [NONE] * 4 + [16, 17, 18, 19] + [NONE] * 4
 Z_X1 = list(range(16)) + [NONE] * 4 + [-4, -3, -2, -1] + [NONE] * 4 + [16, 17, 18, 19]
-Z_H1 = [0, 1, 2, 3, -2, -1, 4, 5]
-Z_H2 = [0, 1, 2, 3, 4, 5, -2, -1]
+C_SLOTS = ([(0, z) for z in range(4)] + [(0, -1), (1, -1), (0, 4), (1, 4)]
+           + [(1, z) for z in range(4)])
 
 
 def constants():
@@ -41,25 +41,27 @@
     for x in range(16):
         for y in range(16):
             swap[y * 16 + x, x * 16 + y] = 1.0
-    split_coarse = np.zeros((256, 512), np.float32)
+    split_coarse = np.zeros((256, 256), np.float32)
     for z in range(4):
         for c in range(32):
             split_coarse[z * 64 + c, z * 32 + c] = 1.0
             split_coarse[z * 64 + 32 + c, 128 + z * 32 + c] = 1.0
-            if z < 2:
-                split_coarse[z * 64 + 32 + c, 256 + z * 32 + c] = 1.0
-                split_coarse[z * 64 + c, 256 + 64 + z * 32 + c] = 1.0
-            else:
-                split_coarse[z * 64 + c, 384 + (z - 2) * 32 + c] = 1.0
-                split_coarse[z * 64 + 32 + c, 384 + 64 + (z - 2) * 32 + c] = 1.0
+    pack = np.zeros((512, 256), np.float32)
+    unpack = np.zeros((256, 256), np.float32)
+    lanes = np.arange(32)
+    for half in range(2):
+        for field in range(2):
+            for side in range(2):
+                pack[half * 256 + field * 128 + side * 96 + lanes,
+                     side * 128 + half * 64 + field * 32 + lanes] = 1.0
+                unpack[side * 128 + half * 64 + field * 32 + lanes,
+                       half * 128 + side * 64 + field * 32 + lanes] = 1.0
     return np.concatenate([
-        split_fine, split_fine.T, edge_fine, swap,
-        split_coarse[:, :256], split_coarse[:, 256:], split_coarse[:, :256].T,
-    ])
+        split_fine, split_fine.T, edge_fine, swap, split_coarse, split_coarse.T, pack, unpack])
 
 
 PERMS = constants()
-SPLIT_F, JOIN_F, EDGE_F, SWAP, SPLIT_C, EDGE_C, JOIN_C = 0, 256, 512, 1024, 1280, 1536, 1792
+SPLIT_F, JOIN_F, EDGE_F, SWAP, SPLIT_C, JOIN_C, PACK_C, UNPACK_C = 0, 256, 512, 1024, 1280, 1536, 1792, 2304
 
 
 def silu(v):
@@ -80,13 +82,7 @@
     return lax.broadcasted_iota(jnp.int32, shape, dim)
 
 
-def bands(fine_w, coarse_w, bands_f, bands_c, last_band, wf, wc, t_fine, t_fwd, t_nat, sems):
-    loads = [pltpu.make_async_copy(coarse_w, wc.at[pl.ds(0, 1728)], sems.at[0]),
-             pltpu.make_async_copy(fine_w, wf.at[pl.ds(0, 864)], sems.at[1])]
-    for copy in loads:
-        copy.start()
-    wf[864:896] = jnp.zeros((32, 8), BF)
-    wc[1728:1792] = jnp.zeros((64, 32), BF)
+def band_builders(bands_f, bands_c, last_band, wf, wc, t_fine, t_fwd, t_nat):
     nt = (((1,), (1,)), ((), ()))
 
     def same(shape, f, g):
@@ -105,57 +101,66 @@
             spread = jnp.where(own, jnp.concatenate([cut] * (128 // width), axis=0), 0.0).astype(BF)
             target[128 * j:128 * (j + 1)] = mm(spread, repeat)
 
-    def build(store, taps, width, first, z_in, z_out, columns, flip=False):
-        slots = 128 // width
-        group = max(16 // width, 1)
+    def build_fine(conv, z_in, z_out):
+        columns = 1 if conv == 3 else 2
 
         def body(i, carry):
-            p, q = i // 3, i % 3
-            base = p * 9 + q * 3 if width == 8 else q * 9 + p * 3
-            if flip:
-                base = 24 - base
-            tiles = [taps[pl.ds(pl.multiple_of((first + base + (2 - k if flip else k)) * width, width), width), :]
-                     for k in range(3)]
-            lane_slot = iota((width, 128), 1) // width
-            for start in range(0, 2 * slots, group):
+            tiles = [t_fine[pl.ds(pl.multiple_of((conv * 27 + i * 3 + k) * 8, 8), 8), :] for k in range(3)]
+            lane_slot = iota((8, 128), 1) // 8
+            for start in range(0, 32, 2):
+                rows = pl.ds(pl.multiple_of(i * 256 + start * 8, 16), 16)
                 for column in range(columns):
                     pieces = []
-                    for z in z_in[start:start + group]:
-                        piece = jnp.zeros((width, 128), F32)
+                    for z in z_in[start:start + 2]:
+                        piece = jnp.zeros((8, 128), F32)
                         for k in range(3):
                             if z != NONE and z + 1 - k in z_out:
                                 slot = z_out.index(z + 1 - k)
-                                if slot // slots == column:
-                                    piece = jnp.where(lane_slot == slot % slots, tiles[k], piece)
+                                if slot // 16 == column:
+                                    piece = jnp.where(lane_slot == slot % 16, tiles[k], piece)
                         pieces.append(piece)
-                    value = pieces[0] if group == 1 else jnp.concatenate(pieces, axis=0)
-                    store(pl.ds(pl.multiple_of(i * 256 + start * width, 16), group * width),
-                          slice(128 * column, 128 * column + 128), value.astype(BF))
+                    value = jnp.concatenate(pieces, axis=0).astype(BF)
+                    if conv == 3:
+                        last_band[rows, :] = value
+                    else:
+                        bands_f[conv, rows, 128 * column:128 * column + 128] = value
             return carry
         lax.fori_loop(0, 9, body, 0)
 
-    def into(target, conv):
-        def store(rows, lanes, value):
-            target[conv, rows, lanes] = value
-        return store
-
-    def into_last(rows, lanes, value):
-        last_band[rows, lanes] = value
-
-    loads[0].wait()
-    repeat = one_hot(same((32, 128), lambda r: r, lambda l: l % 32))
-    t_nat[...] = mm(wc[...], repeat)
-    tile_taps(wc, 32, t_fwd)
-    build(into(bands_c, 0), t_fwd, 32, 27, Z_H1, Z_H2, 2)
-    build(into(bands_c, 1), t_nat, 32, 27, Z_H2, Z_H1, 2, True)
-    build(into(bands_c, 2), t_fwd, 32, 0, Z_H2, Z_H1, 1)
-    build(into(bands_c, 3), t_nat, 32, 0, Z_H1, Z_H2, 1, True)
-    loads[1].wait()
-    tile_taps(wf, 8, t_fine)
-    build(into(bands_f, 0), t_fine, 8, 0, Z_X2, Z_X1, 2)
-    build(into(bands_f, 1), t_fine, 8, 27, Z_X1, Z_X2, 2)
-    build(into(bands_f, 2), t_fine, 8, 54, Z_X2, Z_X1, 2)
-    build(into_last, t_fine, 8, 81, Z_X1, Z_X2, 1)
+    def build_coarse(stage):
+        first = 27 * (1 - stage)
+
+        def body(i, carry):
+            base = i % 3 * 9 + i // 3 * 3
+            tiles = [[t_fwd[pl.ds(pl.multiple_of((first + base + k) * 32, 32), 32), :] for k in range(3)],
+                     [t_nat[pl.ds(pl.multiple_of((first + 26 - base - k) * 32, 32), 32), :] for k in range(3)]]
+            lane_slot = iota((32, 128), 1) // 32
+            for at, (field, z) in enumerate(C_SLOTS):
+                rows = pl.ds(pl.multiple_of(i * 384 + at * 32, 32), 32)
+                piece = jnp.zeros((32, 128), F32)
+                for k in range(3):
+                    if 0 <= z + 1 - k < 4:
+                        piece = jnp.where(lane_slot == z + 1 - k, tiles[field][k], piece)
+                bands_c[stage, rows, 128 * field:128 * field + 128] = piece.astype(BF)
+                other = 128 - 128 * field
+                bands_c[stage, rows, other:other + 128] = jnp.zeros((32, 128), BF)
+            return carry
+        lax.fori_loop(0, 9, body, 0)
+
+    def coarse():
+        wc[1728:1792] = jnp.zeros((64, 32), BF)
+        repeat = one_hot(same((32, 128), lambda r: r, lambda l: l % 32))
+        t_nat[...] = mm(wc[...], repeat)
+        tile_taps(wc, 32, t_fwd)
+        build_coarse(0)
+        build_coarse(1)
+
+    def fine():
+        wf[864:896] = jnp.zeros((32, 8), BF)
+        tile_taps(wf, 8, t_fine)
+        for conv in range(4):
+            build_fine(conv, (Z_X2, Z_X1)[conv % 2], (Z_X1, Z_X2)[conv % 2])
+    return coarse, fine
 
 
 def fine_limits(sizes):
@@ -178,10 +183,11 @@
     return jnp.concatenate([own, rim], axis=1)
 
 
-def kernel(sizes, fine_in, c_out, c_cot, perms_h, bands_f, bands_c,
-           state, rb_s, gi_s, wg_s,
+def kernel(sizes, fine_in, fine_w, c_out, c_cot, coarse_w, perms_h,
+           state, last_band, rb_s, gi_s, wg_s,
+           wf, wc, t_fine, t_fwd, t_nat, bands_f, bands_c,
            xraw, craw, perms, u_fine, esend, erecv, yf, ysend, yrecv, kf, ksend, krecv,
-           cs, ce, y1s, y2s, d1s, d2s, su1, sd2, su2, se,
+           cown, cpack, crecv, ckrecv, cspread,
            part, r1, r2, red, red_bf, final,
            load_sem, in_send, in_recv, x_send, x_recv, c_send, c_recv, f_send, f_recv,
            p1_send, p1_recv, p2_send, p2_recv, p3_send, p3_recv):
@@ -214,10 +220,12 @@
             pl.semaphore_signal(barrier, inc=1, device_id=to, device_id_type=MESH)
 
     loads = [
+        (coarse_w, wc.at[pl.ds(0, 1728)]),
         (perms_h, perms),
         (c_out.at[gx], craw.at[0, pl.ds(gx * 4, 4)]),
         (c_cot.at[gx], craw.at[1, pl.ds(gx * 4, 4)]),
         (fine_in, xraw.at[pl.ds(FH, FX)]),
+        (fine_w, wf.at[pl.ds(0, 864)]),
     ]
     loads = [pltpu.make_async_copy(s, t, load_sem.at[i]) for i, (s, t) in enumerate(loads)]
     for copy in loads:
@@ -282,53 +290,75 @@
     def _():
         xraw[FX + FH:] = jnp.zeros((FH, FY, 256), BF)
 
-    for copy in loads[0:3]:
+    build_coarse, build_fine = band_builders(bands_f, bands_c, last_band, wf, wc, t_fine, t_fwd, t_nat)
+    loads[0].wait()
+    build_coarse()
+
+    for copy in loads[1:4]:
         copy.wait()
     for copy in gathers:
         copy.wait()
     swap = perms[SWAP:SWAP + 256, :]
-    for i in range(2):
-        raw = craw[i].reshape(256, 256)
-        turned_rows = mm(swap, raw).astype(BF)
-        halves = mm(turned_rows, perms[SPLIT_C:SPLIT_C + 256, :]).astype(BF)
-        edges = mm(turned_rows, perms[EDGE_C:EDGE_C + 256, :]).astype(BF)
-        cs[i, 2:18, :, 0:256] = halves.reshape(16, 16, 256)
-        ce[0, i] = edges[:, :128].reshape(16, 16, 128)
-        ce[1, i] = edges[:, 128:].reshape(16, 16, 128)
-    copies = []
-    for sy in (-1, 0, 1):
-        source_y, target_y, deep_y = ((0, 18, 2), (0, 2, 16), (14, 0, 2))[sy + 1]
-        for sz in (-1, 0, 1):
-            if sy == 0 and sz == 0:
-                continue
-            if sz == 0:
-                src = cs.at[:, pl.ds(source_y + 2, deep_y), :, pl.ds(0, 256)]
-                dst = cs.at[:, pl.ds(target_y, deep_y), :, pl.ds(0, 256)]
-            else:
-                src = ce.at[(sz + 1) // 2, :, pl.ds(source_y, deep_y)]
-                dst = cs.at[:, pl.ds(target_y, deep_y), :, pl.ds(384 if sz < 0 else 256, 128)]
-            n = len(copies)
-            copies.append(((0, sy, sz), remote(src, dst, c_send.at[n], c_recv.at[n], beside(sy, sz))))
-    start_c, wait_c = exchange(copies)
-    start_c()
-
-    @pl.when(gz == 0)
-    def _():
-        cs[:, :, :, 256:384] = jnp.zeros((2, 20, 16, 128), BF)
-
-    @pl.when(gz == nz - 1)
-    def _():
-        cs[:, :, :, 384:512] = jnp.zeros((2, 20, 16, 128), BF)
-
-    @pl.when(gy == 0)
-    def _():
-        cs[:, 0:2] = jnp.zeros((2, 2, 16, 512), BF)
-
-    @pl.when(gy == ny - 1)
-    def _():
-        cs[:, 18:20] = jnp.zeros((2, 2, 16, 512), BF)
-
-    loads[3].wait()
+
+    def halves_of(raw):
+        both = mm(mm(swap, raw.reshape(256, 256)).astype(BF), perms[SPLIT_C:SPLIT_C + 256, :])
+        return both[:, :128], both[:, 128:]
+
+    def send_rims(stage, a, b):
+        both = jnp.concatenate([a, b], axis=1).astype(BF)
+        cown[stage, 1:17] = both.reshape(16, 16, 256)
+        packed = mm(jnp.concatenate([both[:128], both[128:]], axis=1), perms[PACK_C:PACK_C + 512, :]).astype(BF)
+        cpack[stage, 0] = packed[:, :128]
+        cpack[stage, 1] = packed[:, 128:]
+        copies = []
+        for sy in (-1, 0, 1):
+            y = (sy + 1) // 2
+            for sz in (-1, 0, 1):
+                z = (sz + 1) // 2
+                if sy == 0 and sz == 0:
+                    continue
+                src, dst = ((cpack.at[stage, z], crecv.at[stage, 1 - z]) if sy == 0 else
+                            (cown.at[stage, 1 + 15 * y], cown.at[stage, 17 - 17 * y]) if sz == 0 else
+                            (cpack.at[stage, z, pl.ds(112 * y, 16)], ckrecv.at[stage, 1 - y, 1 - z]))
+                n = len(copies)
+                copies.append(((0, sy, sz), remote(
+                    src, dst, c_send.at[stage, n], c_recv.at[stage, n], beside(sy, sz))))
+        start, wait = exchange(copies)
+        start()
+        for side in range(2):
+            @pl.when(gz == side * (nz - 1))
+            def _():
+                crecv[stage, side] = jnp.zeros((128, 128), BF)
+                ckrecv[stage, :, side] = jnp.zeros((2, 16, 128), BF)
+
+            @pl.when(gy == side * (ny - 1))
+            def _():
+                cown[stage, 17 * side] = jnp.zeros((16, 256), BF)
+                ckrecv[stage, side] = jnp.zeros((2, 16, 128), BF)
+        return wait
+
+    def spread_rows(stage):
+        unpack = perms[UNPACK_C:UNPACK_C + 256, :]
+        inner = mm(jnp.concatenate([crecv[stage, 0], crecv[stage, 1]], axis=1), unpack)
+        ends = [mm(jnp.concatenate([ckrecv[stage, y, 0], ckrecv[stage, y, 1]], axis=1), unpack) for y in range(2)]
+        rim = jnp.concatenate([ends[0][:, 128:], inner[:, :128], inner[:, 128:], ends[1][:, :128]], axis=0)
+        both = cown[stage].reshape(288, 256).astype(F32)
+        values = jnp.concatenate([both[:, :128], rim, both[:, 128:]], axis=1)
+        row = iota((288, 384), 0) % 16
+        cspread[stage, :, 0:384] = jnp.where(row == 0, 0.0, pltpu.roll(values, 1, 0)).astype(BF)
+        cspread[stage, :, 384:768] = values.astype(BF)
+        cspread[stage, :, 768:1152] = jnp.where(row == 15, 0.0, pltpu.roll(values, 287, 0)).astype(BF)
+
+    def conv_pair(stage):
+        lhs = jnp.concatenate([cspread[stage, 16 * p:16 * p + 256, :] for p in range(3)], axis=1)
+        both = mm(lhs, bands_c[stage])
+        return both[:, :128], both[:, 128:]
+
+    y1, y2 = halves_of(craw[0])
+    d1, d2 = halves_of(craw[1])
+    wait_c0 = send_rims(0, silu(y1), d2)
+
+    loads[4].wait()
     wait_x()
     packed = jnp.concatenate([xraw[0:12].reshape(768, 256), xraw[12:24].reshape(768, 256)], axis=1)
     edges = mm(packed, perms[EDGE_F:EDGE_F + 512, :])
@@ -371,70 +401,42 @@
             yrecv[side] = jnp.zeros((96, 256), BF)
             krecv[side] = jnp.zeros((2, 48, 128), BF)
 
-    wait_c()
-    left = iota((320, 128), 1) < 64
-    for i, (one, two) in enumerate(((y1s, y2s), (d1s, d2s))):
-        rows = cs[i].reshape(320, 512).astype(F32)
-        low, high = rows[:, 256:384], rows[:, 384:512]
-        one[:, 0:128] = rows[:, 0:128]
-        one[:, 128:256] = jnp.where(left, low, high)
-        two[:, 0:128] = rows[:, 128:256]
-        two[:, 128:256] = jnp.where(left, high, low)
-
-    def spread_x(values, target, count):
-        row = iota((count * 16, 256), 0) % 16
-        n = count * 16
-        before = jnp.where(row == 0, 0.0, pltpu.roll(values, 1, 0))
-        after = jnp.where(row == 15, 0.0, pltpu.roll(values, n - 1, 0))
-        target[0:n, 0:256] = before.astype(BF)
-        target[0:n, 256:512] = values.astype(BF)
-        target[0:n, 512:768] = after.astype(BF)
-
-    def conv_c(source, conv, count, width):
-        lhs = jnp.concatenate([source[16 * p:16 * (p + count), :] for p in range(3)], axis=1)
-        return mm(lhs, bands_c[conv, :, 0:width])
-
-    spread_x(silu(y1s[...]), su1, 20)
-    spread_x(d2s[...], sd2, 20)
-    x2 = y2s[16:304] - conv_c(su1, 0, 18, 256)
-    e = d1s[16:304] + silu_grad(y1s[16:304]) * conv_c(sd2, 1, 18, 256)
-    z_low = jnp.where(gz == 0, 64, 0)
-    z_high = jnp.where(gz == nz - 1, 64, 0)
-    y_row = iota((288, 128), 0) // 16
-    lane = iota((288, 128), 1)
-    y_ok = (y_row >= jnp.where(gy == 0, 1, 0)) & (y_row < jnp.where(gy == ny - 1, 17, 18))
-    h1_ok = y_ok & (lane >= z_low) & (lane < 128 - z_high)
-    h2_ok = y_ok & (lane >= z_high) & (lane < 128 - z_low)
-    x2_own = x2[16:272, 0:128]
-    e_own = e[16:272, 0:128]
-    u2 = silu(x2)
-    u2 = jnp.concatenate([jnp.where(y_ok, u2[:, :128], 0.0), jnp.where(h2_ok, u2[:, 128:], 0.0)], axis=1)
-    e = jnp.concatenate([jnp.where(y_ok, e[:, :128], 0.0), jnp.where(h1_ok, e[:, 128:], 0.0)], axis=1)
-    spread_x(u2, su2, 18)
-    spread_x(e, se, 18)
+    loads[5].wait()
+    build_fine()
+
+    wait_c0()
+    spread_rows(0)
+    image_g, back_g = conv_pair(0)
+    x2 = y2 - image_g
+    e = d1 + silu_grad(y1) * back_g
+    wait_c1 = send_rims(1, silu(x2), e)
 
     place_lane = iota((32, 128), 1) // 32
-    held = None
-    for fg, (cot, source, first, z_order) in enumerate((
-            (e_own, su2, 0, Z_H2), (d2s[32:288, 0:128], su1, 1, Z_H1))):
+
+    def fold(stage, cot):
         turned_cot = jnp.transpose(cot).astype(BF)
-        blocks = [mm(turned_cot, source[16 * (first + p):16 * (first + p + 16), :]) for p in range(3)]
         for q in range(3):
             for p in range(3):
-                block = blocks[p][:, q * 256:(q + 1) * 256]
+                block = mm(turned_cot, cspread[stage, 16 * p:16 * p + 256, 384 * q:384 * q + 256])
                 for k in range(3):
                     acc = None
                     for z in range(4):
-                        slot = z_order.index(z + k - 1)
-                        at = 128 * (slot // 4)
-                        term = jnp.where(place_lane == slot % 4, block[32 * z:32 * z + 32, at:at + 128], 0.0)
+                        at = C_SLOTS.index((0, z + k - 1))
+                        column = 128 * (at // 4)
+                        term = jnp.where(place_lane == at % 4,
+                                         block[32 * z:32 * z + 32, column:column + 128], 0.0)
                         acc = term if acc is None else acc + term
                     acc = acc + pltpu.roll(acc, 64, 1)
                     acc = acc + pltpu.roll(acc, 32, 1)
-                    t = fg * 27 + q * 9 + p * 3 + k
+                    t = (1 - stage) * 28 + q * 9 + p * 3 + k
                     held = acc if t % 4 == 0 else jnp.where(place_lane == t % 4, acc, held)
-                    if t % 4 == 3 or t == 53:
+                    if t % 4 == 3 or t in (26, 54):
                         part[t // 4 * 32:t // 4 * 32 + 32, :] = held
+
+    fold(0, d2)
+    wait_c1()
+    spread_rows(1)
+    fold(1, e)
 
     ch = 512 // wide
     mine = pl.ds(pl.multiple_of(me_wide * ch, 8), ch)
@@ -445,10 +447,11 @@
     for copy in sends1:
         copy.start()
 
-    x1 = y1s[32:288, 0:128] - conv_c(su2, 2, 16, 128)
-    dx2 = d2s[32:288, 0:128] + silu_grad(x2_own) * conv_c(se, 3, 16, 128)
+    image_f, back_f = conv_pair(1)
+    x1 = y1 - image_f
+    dx2 = d2 + silu_grad(x2) * back_f
     join = perms[JOIN_C:JOIN_C + 256, :]
-    for one, two, target in ((x1, x2_own, rb_s), (e_own, dx2, gi_s)):
+    for one, two, target in ((x1, x2, rb_s), (e, dx2, gi_s)):
         both = jnp.concatenate([one.astype(BF), two.astype(BF)], axis=1)
         target[...] = mm(swap, mm(both, join).astype(BF)).astype(BF).reshape(16, 16, 256)
 
@@ -524,9 +527,9 @@
         rows = final[32 * g:32 * g + 32, :].astype(F32)
         for j in range(4):
             t = 4 * g + j
-            if t < 54:
+            if t % 28 < 27:
                 turned_rows = rows if j == 0 else pltpu.roll(rows, 128 - 32 * j, 1)
-                wg_s[t] = turned_rows[:, :32]
+                wg_s[t - t // 28] = turned_rows[:, :32]
 
 
 def finish(sizes, state, last_band, rb_s, gi_s, wg_s, join_h,
@@ -570,42 +573,34 @@
     vm, dma = pltpu.VMEM, pltpu.SemaphoreType.DMA
     hbm = pl.BlockSpec(memory_space=pltpu.HBM)
     scratch = [
-        vm((XX, FY, 256), BF), vm((2, CX, CY, 256), BF), vm((2048, 256), BF),
+        vm((896, 8), BF), vm((1792, 32), BF), vm((896, 128), F32), vm((1792, 128), F32), vm((1792, 128), F32),
+        vm((3, 2304, 256), BF), vm((2, 3456, 256), BF),
+        vm((XX, FY, 256), BF), vm((2, CX, CY, 256), BF), vm((2560, 256), BF),
         vm((XX, YY, 768), BF),
         vm((2, 12, 64, 128), BF), vm((2, 12, 64, 128), BF),
         vm((2, 96, 256), F32), vm((2, 96, 256), BF), vm((2, 96, 256), BF),
         vm((2, 48, 256), F32), vm((2, 2, 48, 128), BF), vm((2, 2, 48, 128), BF),
-        vm((2, 20, 16, 512), BF), vm((2, 2, 16, 16, 128), BF),
-        vm((320, 256), F32), vm((320, 256), F32), vm((320, 256), F32), vm((320, 256), F32),
-        vm((320, 768), BF), vm((320, 768), BF), vm((288, 768), BF), vm((288, 768), BF),
+        vm((2, 18, 16, 256), BF), vm((2, 2, 128, 128), BF), vm((2, 2, 128, 128), BF),
+        vm((2, 2, 2, 16, 128), BF), vm((2, 288, 1152), BF),
         vm((512, 128), F32), vm((wide, ch, 128), F32), vm((deep, ch, 128), F32),
         vm((ch, 128), F32), vm((ch, 128), BF), vm((512, 128), BF),
-        dma((4,)), dma((nx, 2)), dma((nx, 2)), dma((2,)), dma((2,)),
-        dma((8,)), dma((8,)), dma((8,)), dma((8,)),
+        dma((6,)), dma((nx, 2)), dma((nx, 2)), dma((2,)), dma((2,)),
+        dma((2, 8)), dma((2, 8)), dma((8,)), dma((8,)),
         dma((wide,)), dma((wide,)), dma((deep,)), dma((deep,)), dma((wide,)), dma((wide,)),
     ]
     inside = pl.BlockSpec(memory_space=pltpu.VMEM)
     in_hbm = functools.partial(pltpu.with_memory_space_constraint, memory_space=pltpu.HBM)
     perms = jnp.asarray(PERMS, BF)
-    bands_f, bands_c, last_band = pl.pallas_call(
-        bands,
-        out_shape=(vm((3, 2304, 256), BF), vm((4, 2304, 256), BF), vm((2304, 128), BF)),
-        in_specs=[hbm] * 2,
-        out_specs=(inside,) * 3,
-        scratch_shapes=[vm((896, 8), BF), vm((1792, 32), BF), vm((896, 128), F32),
-                        vm((1792, 128), F32), vm((1792, 128), F32), dma((2,))],
-        compiler_params=pltpu.CompilerParams(vmem_limit_bytes=24 * 1024 * 1024),
-    )(in_hbm(fine_w), in_hbm(coarse_w))
     held = pl.pallas_call(
         functools.partial(kernel, sizes),
-        out_shape=(vm((XX, YY, 384), F32), vm((16, 16, 256), BF),
+        out_shape=(vm((XX, YY, 384), F32), vm((2304, 128), BF), vm((16, 16, 256), BF),
                    vm((16, 16, 256), BF), vm((54, 32, 32), F32)),
-        in_specs=[hbm] * 4 + [inside] * 2,
-        out_specs=(inside,) * 4,
+        in_specs=[hbm] * 6,
+        out_specs=(inside,) * 5,
         scratch_shapes=scratch,
         compiler_params=pltpu.CompilerParams(
-            collective_id=0, has_side_effects=True, vmem_limit_bytes=32 * 1024 * 1024),
-    )(in_hbm(fine_in), in_hbm(coarse_out), in_hbm(coarse_cot), in_hbm(perms), bands_f, bands_c)
+            collective_id=0, has_side_effects=True, vmem_limit_bytes=40 * 1024 * 1024),
+    )(*(in_hbm(v) for v in (fine_in, fine_w, coarse_out, coarse_cot, coarse_w, perms)))
     fine_out, rebuilt, grads_in, wg = pl.pallas_call(
         functools.partial(finish, sizes),
         out_shape=(
@@ -618,7 +613,7 @@
         out_specs=(hbm,) * 4,
         scratch_shapes=[vm((XX, FY, 768), BF), vm((256, 256), BF), vm((FX, FY, 256), BF), dma((6,))],
         compiler_params=pltpu.CompilerParams(vmem_limit_bytes=24 * 1024 * 1024),
-    )(held[0], last_band, *held[1:], jnp.asarray(PERMS[JOIN_F:JOIN_F + 256], BF))
+    )(*held, jnp.asarray(PERMS[JOIN_F:JOIN_F + 256], BF))
     wg = jnp.transpose(wg.reshape(2, 3, 3, 3, 32, 32), (0, 4, 5, 1, 2, 3))
     return fine_out, rebuilt, grads_in, wg
 

time: 54.7 us -> 52 us (0.951)
  Pallas kernels: 53.9 us -> 50.3 us
  local copies, waits for them, and re-layouts: 0.01 us -> 0.9 us
    pallas_call x1 -> x0, Pallas kernels: 4.27 us -> none  [on_device(): pl.pallas_call(bands, out_shape=(vm((3, 2304, 256), BF), vm((4, 2304, 256...]
    unnamed x2, local copies, waits for them, and re-layouts: 0.01 us -> 0.9 us
    pallas_call x1, Pallas kernels: 46.2 us -> 46.9 us  [on_device(): pl.pallas_call(functools.partial(kernel, sizes), out_shape=(vm((XX, YY, 3...]
where the time goes in v3:
time: 52 us; the launch traced here: 51.9 us
  Pallas kernels  50.3 us (97%)
  local copies, waits for them, and re-layouts  0.9 us (2%)
  between operations  0.65 us (1%)
    pallas_call x1, Pallas kernels, on_device(): pl.pallas_call(functools.partial(kernel, sizes), out_shape=(vm((XX, YY, 3...  46.9 us
    pallas_call x1, Pallas kernels, on_device(): pl.pallas_call(functools.partial(finish, sizes), out_shape=(jax.ShapeDtyp...  3.38 us

profile of v3, /device:TPU:1, one launch (start us, length us, event | category | flops | bytes accessed | tf_op | source)
XLA Modules:
  0.0 51.9 jit_solution(13505923820675475028)
XLA Ops:
  0.6 46.9 %shard_map.102 = (f32[24,80,384]{2,1,0:T(8,128)S(1)}, bf16[2304,128]{1,0:T(8,128)(2,1)S(1)}, bf16[16,16,256]{2,1,0:T(8,128)(2,1)S(1)}, bf16[16,16,256]{2,1,0:T(8,128)(2,1)S(1)}, f32[54,32,32]{2,1,0:T(8,128)S(1)}) custom-call(bf16[16,64,256]{2,1,0:T(8,128)(2,1)} %fine_in.1, bf16[864,8]{1,0:T(8,128)(2,1)} %bitcast.10, bf16[4,4,16,256]{3,2,1,0:T(8,128)(2,1)} %c_out.1, ...), custom_call_target="tpu_custom_call" | custom-call | tf_op jit(solution)/shard_map/pallas_call | solution.py:594
  47.6 0.0 copy-start
  47.6 0.9 %copy-done = bf16[256,256]{1,0:T(8,128)(2,1)S(1)} copy-done((bf16[256,256]{1,0:T(8,128)(2,1)S(1)}, bf16[256,256]{1,0:T(8,128)(2,1)}, u32[]{:S(2)}) %copy-start) | copy-done | bytes 131096
  48.5 3.4 %shard_map.103 = (bf16[16,64,256]{2,1,0:T(8,128)(2,1)}, bf16[1,16,16,256]{3,2,1,0:T(8,128)(2,1)}, bf16[1,16,16,256]{3,2,1,0:T(8,128)(2,1)}, f32[54,32,32]{2,1,0:T(8,128)}) custom-call(f32[24,80,384]{2,1,0:T(8,128)S(1)} %get-tuple-element.13.state, bf16[2304,128]{1,0:T(8,128)(2,1)S(1)} %get-tuple-element.14.last_band, ...), custom_call_target="tpu_custom_call" | custom-call | tf_op jit(solution)/shard_map/pallas_call | solution.py:604
Async XLA Ops:
  47.6 0.9 %copy-start = (bf16[256,256]{1,0:T(8,128)(2,1)S(1)}, bf16[256,256]{1,0:T(8,128)(2,1)}, u32[]{:S(2)}) copy-start(bf16[256,256]{1,0:T(8,128)(2,1)} %constant.5.clone.join_h) | copy-start | bytes 393220

commit v4 on v3

--- a/solution.py
+++ b/solution.py
@@ -15,10 +15,6 @@
 FX, FY, FZ, FH = 16, 64, 16, 4
 XX, YY = FX + 2 * FH, 80
 CX, CY, CZ = 16, 16, 4
-NONE = 99
-
-Z_X2 = list(range(16)) + [-4, -3, -2, -1] + [NONE] * 4 + [16, 17, 18, 19] + [NONE] * 4
-Z_X1 = list(range(16)) + [NONE] * 4 + [-4, -3, -2, -1] + [NONE] * 4 + [16, 17, 18, 19]
 C_SLOTS = ([(0, z) for z in range(4)] + [(0, -1), (1, -1), (0, 4), (1, 4)]
            + [(1, z) for z in range(4)])
 
@@ -29,14 +25,6 @@
         for c in range(8):
             split_fine[z * 16 + 8 + c, z * 8 + c] = 1.0
             split_fine[z * 16 + c, 128 + z * 8 + c] = 1.0
-    edge_fine = np.zeros((512, 256), np.float32)
-    for part in range(2):
-        for side, z_first in ((0, 0), (1, 12)):
-            for z in range(4):
-                for c in range(8):
-                    base = side * 128 + part * 64 + z * 8 + c
-                    edge_fine[part * 256 + (z_first + z) * 16 + 8 + c, base] = 1.0
-                    edge_fine[part * 256 + (z_first + z) * 16 + c, base + 32] = 1.0
     swap = np.zeros((256, 256), np.float32)
     for x in range(16):
         for y in range(16):
@@ -57,11 +45,11 @@
                 unpack[side * 128 + half * 64 + field * 32 + lanes,
                        half * 128 + side * 64 + field * 32 + lanes] = 1.0
     return np.concatenate([
-        split_fine, split_fine.T, edge_fine, swap, split_coarse, split_coarse.T, pack, unpack])
+        split_fine, split_fine.T, swap, split_coarse, split_coarse.T, pack, unpack])
 
 
 PERMS = constants()
-SPLIT_F, JOIN_F, EDGE_F, SWAP, SPLIT_C, JOIN_C, PACK_C, UNPACK_C = 0, 256, 512, 1024, 1280, 1536, 1792, 2304
+SPLIT_F, JOIN_F, SWAP, SPLIT_C, JOIN_C, PACK_C, UNPACK_C = 0, 256, 512, 768, 1024, 1280, 1792
 
 
 def silu(v):
@@ -82,7 +70,7 @@
     return lax.broadcasted_iota(jnp.int32, shape, dim)
 
 
-def band_builders(bands_f, bands_c, last_band, wf, wc, t_fine, t_fwd, t_nat):
+def band_builders(bands_own, bands_rim, last_rim, bands_c, wf, wc, t_fine, t_fwd, t_nat):
     nt = (((1,), (1,)), ((), ()))
 
     def same(shape, f, g):
@@ -101,29 +89,28 @@
             spread = jnp.where(own, jnp.concatenate([cut] * (128 // width), axis=0), 0.0).astype(BF)
             target[128 * j:128 * (j + 1)] = mm(spread, repeat)
 
-    def build_fine(conv, z_in, z_out):
-        columns = 1 if conv == 3 else 2
-
+    def build_fine(conv):
         def body(i, carry):
             tiles = [t_fine[pl.ds(pl.multiple_of((conv * 27 + i * 3 + k) * 8, 8), 8), :] for k in range(3)]
             lane_slot = iota((8, 128), 1) // 8
-            for start in range(0, 32, 2):
-                rows = pl.ds(pl.multiple_of(i * 256 + start * 8, 16), 16)
-                for column in range(columns):
-                    pieces = []
-                    for z in z_in[start:start + 2]:
-                        piece = jnp.zeros((8, 128), F32)
-                        for k in range(3):
-                            if z != NONE and z + 1 - k in z_out:
-                                slot = z_out.index(z + 1 - k)
-                                if slot // 16 == column:
-                                    piece = jnp.where(lane_slot == slot % 16, tiles[k], piece)
-                        pieces.append(piece)
-                    value = jnp.concatenate(pieces, axis=0).astype(BF)
-                    if conv == 3:
-                        last_band[rows, :] = value
-                    else:
-                        bands_f[conv, rows, 128 * column:128 * column + 128] = value
+
+            def rows_of(pair):
+                pieces = []
+                for z in pair:
+                    piece = jnp.zeros((8, 128), F32)
+                    for k in range(3):
+                        if 0 <= z + 1 - k < 16:
+                            piece = jnp.where(lane_slot == z + 1 - k, tiles[k], piece)
+                    pieces.append(piece)
+                return jnp.concatenate(pieces, axis=0).astype(BF)
+
+            for z in range(0, 16, 2):
+                bands_own[conv, pl.ds(pl.multiple_of(i * 128 + z * 8, 16), 16), :] = rows_of((z, z + 1))
+            rim = pl.ds(pl.multiple_of(i // 3 * 128 + i % 3 * 16, 16), 16)
+            if conv == 3:
+                last_rim[rim, :] = rows_of((-1, 16))
+            else:
+                bands_rim[conv, rim, :] = rows_of((-1, 16))
             return carry
         lax.fori_loop(0, 9, body, 0)
 
@@ -158,38 +145,43 @@
     def fine():
         wf[864:896] = jnp.zeros((32, 8), BF)
         tile_taps(wf, 8, t_fine)
+        bands_rim[...] = jnp.zeros((3, 384, 128), BF)
+        last_rim[...] = jnp.zeros((384, 128), BF)
         for conv in range(4):
-            build_fine(conv, (Z_X2, Z_X1)[conv % 2], (Z_X1, Z_X2)[conv % 2])
+            build_fine(conv)
     return coarse, fine
 
 
-def fine_limits(sizes):
-    nx, ny, nz = sizes
-    gx, gy, gz = lax.axis_index("gx"), lax.axis_index("gy"), lax.axis_index("gz")
-    return (jnp.where(gx == 0, FH, 0), jnp.where(gx == nx - 1, FX + FH, XX),
-            jnp.where(gy == 0, 8, 4), jnp.where(gy == ny - 1, 72, 76),
-            jnp.where(gz == 0, 64, 0), jnp.where(gz == nz - 1, 64, 128))
-
-
-def fine_input(state, x, column, limits):
-    x_first, x_end, y_first, y_end, rim_first, rim_end = limits
-    first = jnp.where((x >= x_first) & (x < x_end), y_first, YY)
-    row = iota((YY, 128), 0)
-    at = iota((YY, 128), 1)
-    ok = (row >= first) & (row < y_end)
-    rim_ok = ok & (at >= rim_first) & (at < rim_end)
-    own = jnp.where(ok, silu(state[x, :, column:column + 128]), 0.0)
-    rim = jnp.where(rim_ok, silu(state[x, :, 256:384]), 0.0)
-    return jnp.concatenate([own, rim], axis=1)
+def lay_rims(zrf, target):
+    def body(b, carry):
+        even = iota((40, 128), 1) % 16 < 8
+        lane = iota((YY, 128), 1)
+        rows = pl.ds(pl.multiple_of(b * 40, 8), 40)
+        low, high = zrf[0, rows, :], zrf[1, rows, :]
+        both = jnp.concatenate([jnp.where(even, low, pltpu.roll(high, 8, 1)),
+                                jnp.where(even, pltpu.roll(low, 120, 1), high)], axis=0)
+        taps = (pltpu.roll(both, 1, 0), both, pltpu.roll(both, YY - 1, 0))
+        for j in range(8):
+            a, m, c = [pltpu.roll(tap, (16 * q - 16 * j) % 128, 1) if (q - j) % 8 else tap
+                       for q, tap in enumerate(taps)]
+            target[b * 8 + j] = jnp.where(lane < 16, a, jnp.where(lane < 32, m, c)).astype(BF)
+        return carry
+    lax.fori_loop(0, 3, body, 0)
+
+
+def taps_x(source, x0, count):
+    width = source.shape[2]
+    return jnp.concatenate(
+        [source[x0 + p:x0 + p + count].reshape(count * YY, width) for p in range(3)], axis=1)
 
 
 def kernel(sizes, fine_in, fine_w, c_out, c_cot, coarse_w, perms_h,
-           state, last_band, rb_s, gi_s, wg_s,
-           wf, wc, t_fine, t_fwd, t_nat, bands_f, bands_c,
-           xraw, craw, perms, u_fine, esend, erecv, yf, ysend, yrecv, kf, ksend, krecv,
+           state, last_rim, last_edges, rb_s, gi_s, wg_s,
+           wf, wc, t_fine, t_fwd, t_nat, bands_own, bands_rim, bands_c,
+           xraw, craw, perms, u_own, u_rim, yf, ysend, yrecv, zf, zsend, zrecv, zrf,
            cown, cpack, crecv, ckrecv, cspread,
            part, r1, r2, red, red_bf, final,
-           load_sem, in_send, in_recv, x_send, x_recv, c_send, c_recv, f_send, f_recv,
+           load_sem, in_send, in_recv, x_send, x_recv, c_send, c_recv, y_send, y_recv, z_send, z_recv,
            p1_send, p1_recv, p2_send, p2_recv, p3_send, p3_recv):
     nx, ny, nz = sizes
     gx, gy, gz = lax.axis_index("gx"), lax.axis_index("gy"), lax.axis_index("gz")
@@ -230,8 +222,9 @@
     loads = [pltpu.make_async_copy(s, t, load_sem.at[i]) for i, (s, t) in enumerate(loads)]
     for copy in loads:
         copy.start()
-    state[:, 0:8, :] = jnp.zeros((XX, 8, 384), F32)
-    state[:, 72:80, :] = jnp.zeros((XX, 8, 384), F32)
+    state[:, 0:8, :] = jnp.zeros((XX, 8, 256), F32)
+    state[:, 72:80, :] = jnp.zeros((XX, 8, 256), F32)
+    zf[:, 120:128, :] = jnp.zeros((2, 8, 128), F32)
     part[14 * 32:, :] = jnp.zeros((64, 128), F32)
     pl.semaphore_wait(barrier, wide - 1 + deep - 1 + 6)
 
@@ -290,7 +283,7 @@
     def _():
         xraw[FX + FH:] = jnp.zeros((FH, FY, 256), BF)
 
-    build_coarse, build_fine = band_builders(bands_f, bands_c, last_band, wf, wc, t_fine, t_fwd, t_nat)
+    build_coarse, build_fine = band_builders(bands_own, bands_rim, last_rim, bands_c, wf, wc, t_fine, t_fwd, t_nat)
     loads[0].wait()
     build_coarse()
 
@@ -360,49 +353,83 @@
 
     loads[4].wait()
     wait_x()
-    packed = jnp.concatenate([xraw[0:12].reshape(768, 256), xraw[12:24].reshape(768, 256)], axis=1)
-    edges = mm(packed, perms[EDGE_F:EDGE_F + 512, :])
-    esend[0] = edges[:, :128].astype(BF).reshape(12, 64, 128)
-    esend[1] = edges[:, 128:].astype(BF).reshape(12, 64, 128)
-    for x in range(XX // 2):
-        kf[0, 4 * x:4 * x + 4, :] = edges[64 * x:64 * x + 4]
-        kf[1, 4 * x:4 * x + 4, :] = edges[64 * x + 60:64 * x + 64]
-    for y in range(2):
-        for z in range(2):
-            ksend[y, z] = kf[y, :, 128 * z:128 * z + 128].astype(BF)
     halves = mm(xraw[...].reshape(XX * FY, 256), perms[SPLIT_F:SPLIT_F + 256, :])
-    state[:, 8:72, 0:256] = halves.reshape(XX, FY, 256)
+    state[:, 8:72, :] = halves.reshape(XX, FY, 256)
     for x in range(XX):
-        yf[0, 4 * x:4 * x + 4, :] = state[x, 8:12, 0:256]
-        yf[1, 4 * x:4 * x + 4, :] = state[x, 68:72, 0:256]
+        yf[0, 4 * x:4 * x + 4, :] = state[x, 8:12, :]
+        yf[1, 4 * x:4 * x + 4, :] = state[x, 68:72, :]
     ysend[...] = yf[...].astype(BF)
-    copies = []
-    for sy in (-1, 0, 1):
-        y = (sy + 1) // 2
-        for sz in (-1, 0, 1):
-            z = (sz + 1) // 2
-            if sy == 0 and sz == 0:
-                continue
-            src, dst = ((esend.at[z], erecv.at[1 - z]) if sy == 0 else
-                        (ysend.at[y], yrecv.at[1 - y]) if sz == 0 else
-                        (ksend.at[y, z], krecv.at[1 - y, 1 - z]))
-            n = len(copies)
-            copies.append(((0, sy, sz), remote(src, dst, f_send.at[n], f_recv.at[n], beside(sy, sz))))
-    start_f, wait_f = exchange(copies)
-    start_f()
+    start_y, wait_y = exchange([
+        ((0, -1, 0), remote(ysend.at[0], yrecv.at[1], y_send.at[0], y_recv.at[0], beside(-1, 0))),
+        ((0, 1, 0), remote(ysend.at[1], yrecv.at[0], y_send.at[1], y_recv.at[1], beside(1, 0)))])
+    start_y()
     for side in range(2):
-        @pl.when(gz == side * (nz - 1))
-        def _():
-            erecv[side] = jnp.zeros((12, 64, 128), BF)
-            krecv[:, side] = jnp.zeros((2, 48, 128), BF)
-
         @pl.when(gy == side * (ny - 1))
         def _():
             yrecv[side] = jnp.zeros((96, 256), BF)
-            krecv[side] = jnp.zeros((2, 48, 128), BF)
 
     loads[5].wait()
     build_fine()
+
+    x_first = jnp.where(gx == 0, FH, 0)
+    x_end = jnp.where(gx == nx - 1, FX + FH, XX)
+    y_first = jnp.where(gy == 0, 8, 4)
+    y_end = jnp.where(gy == ny - 1, 72, 76)
+
+    def fine_input(r):
+        column = 128 * (r % 2)
+
+        def body(b, carry):
+            row = iota((YY, 128), 0)
+            group = iota((YY, 128), 1) // 16
+            packed = jnp.zeros((YY, 128), F32)
+            for j in range(8):
+                x = b * 8 + j
+                first = jnp.where((x >= x_first) & (x < x_end), y_first, YY)
+                v = jnp.where((row >= first) & (row < y_end), silu(state[x, :, column:column + 128]), 0.0)
+                u_own[x, :, 0:128] = pltpu.roll(v, 1, 0).astype(BF)
+                u_own[x, :, 128:256] = v.astype(BF)
+                u_own[x, :, 256:384] = pltpu.roll(v, YY - 1, 0).astype(BF)
+                turned = pltpu.roll(v, (16 * j + 8) % 128, 1)
+                packed = jnp.where(group == j, turned, packed)
+            even = iota((40, 128), 1) % 16 < 8
+            low, high = packed[0:40], packed[40:80]
+            rows = pl.ds(pl.multiple_of(b * 40, 8), 40)
+            zf[0, rows, :] = jnp.where(even, pltpu.roll(low, 120, 1), high)
+            zf[1, rows, :] = jnp.where(even, low, pltpu.roll(high, 8, 1))
+            return carry
+        lax.fori_loop(0, 3, body, 0)
+        zsend[r] = zf[...].astype(BF)
+        start, wait = exchange([
+            ((0, 0, -1), remote(zsend.at[r, 0], zrecv.at[r, 1], z_send.at[r, 0], z_recv.at[r, 0], beside(0, -1))),
+            ((0, 0, 1), remote(zsend.at[r, 1], zrecv.at[r, 0], z_send.at[r, 1], z_recv.at[r, 1], beside(0, 1)))])
+        start()
+        for side in range(2):
+            @pl.when(gz == side * (nz - 1))
+            def _():
+                zrecv[r, side] = jnp.zeros((128, 128), BF)
+        return wait
+
+    def fine_add(r, source, band):
+        half = (XX - 2 * r - 2) // 2
+        into = 128 - 128 * (r % 2)
+        for part_index in range(2):
+            x0 = r + part_index * half
+            out = mm(taps_x(source, x0, half), band).reshape(half, YY, 128)
+            state[x0 + 1:x0 + 1 + half, :, into:into + 128] += out
+
+    def fine_rims(r, wait):
+        wait()
+        zrf[...] = zrecv[r].astype(F32)
+        lay_rims(zrf, u_rim)
+        fine_add(r, u_rim, bands_rim[r])
+
+    wait_y()
+    for y, row in ((0, 4), (1, 72)):
+        edge = yrecv[y].astype(F32)
+        for x in range(XX):
+            state[x, row:row + 4, :] = edge[4 * x:4 * x + 4]
+    wait_z = fine_input(0)
 
     wait_c0()
     spread_rows(0)
@@ -433,6 +460,9 @@
                     if t % 4 == 3 or t in (26, 54):
                         part[t // 4 * 32:t // 4 * 32 + 32, :] = held
 
+    fine_add(0, u_own, bands_own[0])
+    fine_rims(0, wait_z)
+    wait_z = fine_input(1)
     fold(0, d2)
     wait_c1()
     spread_rows(1)
@@ -447,6 +477,10 @@
     for copy in sends1:
         copy.start()
 
+    fine_add(1, u_own, bands_own[1])
+    fine_rims(1, wait_z)
+    wait_z = fine_input(2)
+
     image_f, back_f = conv_pair(1)
     x1 = y1 - image_f
     dx2 = d2 + silu_grad(x2) * back_f
@@ -455,46 +489,7 @@
         both = jnp.concatenate([one.astype(BF), two.astype(BF)], axis=1)
         target[...] = mm(swap, mm(both, join).astype(BF)).astype(BF).reshape(16, 16, 256)
 
-    wait_f()
-    def rims(from_left, from_right, count):
-        left_lane = iota((count, 128), 1) < 64
-        return (jnp.where(left_lane, from_left, pltpu.roll(from_right, 64, 1)),
-                jnp.where(left_lane, pltpu.roll(from_left, 64, 1), from_right))
-
-    early, late = rims(erecv[0].reshape(768, 128).astype(F32), erecv[1].reshape(768, 128).astype(F32), 768)
-    state[0:12, 8:72, 256:384] = early.reshape(12, 64, 128)
-    state[12:24, 8:72, 256:384] = late.reshape(12, 64, 128)
-    for y, row in ((0, 4), (1, 72)):
-        early, late = rims(krecv[y, 0].astype(F32), krecv[y, 1].astype(F32), 48)
-        edge = yrecv[y].astype(F32)
-        for x in range(XX):
-            state[x, row:row + 4, 0:256] = edge[4 * x:4 * x + 4]
-        for x in range(XX // 2):
-            state[x, row:row + 4, 256:384] = early[4 * x:4 * x + 4]
-            state[x + 12, row:row + 4, 256:384] = late[4 * x:4 * x + 4]
-
-    limits = fine_limits(sizes)
-
-    def fine_conv(step, column, conv):
-        def spread(x, carry):
-            v = fine_input(state, x, column, limits)
-            u_fine[x, :, 0:256] = pltpu.roll(v, 1, 0).astype(BF)
-            u_fine[x, :, 256:512] = v.astype(BF)
-            u_fine[x, :, 512:768] = pltpu.roll(v, YY - 1, 0).astype(BF)
-            return carry
-        lax.fori_loop(step, XX - step, spread, 0)
-        half = (XX - 2 * step - 2) // 2
-        into = 128 - column
-        for part_index in range(2):
-            x0 = step + part_index * half
-            lhs = jnp.concatenate(
-                [u_fine[x0 + p:x0 + p + half].reshape(half * YY, 768) for p in range(3)], axis=1)
-            out = mm(lhs, bands_f[conv]).reshape(half, YY, 256)
-            state[x0 + 1:x0 + 1 + half, :, into:into + 128] += out[:, :, :128]
-            state[x0 + 1:x0 + 1 + half, :, 256:384] += out[:, :, 128:]
-
-    fine_conv(0, 0, 0)
-
+    fine_add(2, u_own, bands_own[2])
     for copy in sends1:
         copy.wait()
     total = part[mine, :]
@@ -506,7 +501,8 @@
     for copy in sends2:
         copy.start()
 
-    fine_conv(1, 128, 1)
+    fine_rims(2, wait_z)
+    wait_z = fine_input(3)
 
     for copy in sends2:
         copy.wait()
@@ -519,7 +515,9 @@
     for copy in sends3:
         copy.start()
 
-    fine_conv(2, 0, 2)
+    fine_add(3, u_own, bands_own[3])
+    wait_z()
+    last_edges[...] = zrecv[3]
 
     for copy in sends3:
         copy.wait()
@@ -532,30 +530,20 @@
                 wg_s[t - t // 28] = turned_rows[:, :32]
 
 
-def finish(sizes, state, last_band, rb_s, gi_s, wg_s, join_h,
-           fine_out, rebuilt, grads_in, wg_out, u_last, join, fo_s, sems):
-    nx, ny, nz = sizes
+def finish(state, last_rim, last_edges, rb_s, gi_s, wg_s, join_h,
+           fine_out, rebuilt, grads_in, wg_out, zrf, u_rim, join, fo_s, sems):
     copies = [pltpu.make_async_copy(s, t, sems.at[i]) for i, (s, t) in enumerate((
         (join_h, join), (rb_s, rebuilt.at[0]), (gi_s, grads_in.at[0]), (wg_s, wg_out)))]
     for copy in copies:
         copy.start()
-    limits = fine_limits(sizes)
-
-    def spread(x, carry):
-        v = fine_input(state, x, 128, limits)
-        u_last[x, :, 0:256] = pltpu.roll(v, 1, 0)[8:72].astype(BF)
-        u_last[x, :, 256:512] = v[8:72].astype(BF)
-        u_last[x, :, 512:768] = pltpu.roll(v, YY - 1, 0)[8:72].astype(BF)
-        return carry
-    lax.fori_loop(3, XX - 3, spread, 0)
+    zrf[...] = last_edges[...].astype(F32)
+    lay_rims(zrf, u_rim)
     copies[0].wait()
     for c in range(2):
         x0 = 3 + 8 * c
-        lhs = jnp.concatenate(
-            [u_last[x0 + p:x0 + p + 8].reshape(512, 768) for p in range(3)], axis=1)
-        two = mm(lhs, last_band[...]).reshape(8, FY, 128) + state[x0 + 1:x0 + 9, 8:72, 0:128]
-        one = state[x0 + 1:x0 + 9, 8:72, 128:256]
-        both = jnp.concatenate([two, one], axis=2).astype(BF).reshape(512, 256)
+        two = mm(taps_x(u_rim, x0, 8), last_rim[...]).reshape(8, YY, 128) + state[x0 + 1:x0 + 9, :, 0:128]
+        both = jnp.concatenate([two[:, 8:72], state[x0 + 1:x0 + 9, 8:72, 128:256]], axis=2)
+        both = both.astype(BF).reshape(8 * FY, 256)
         fo_s[8 * c:8 * c + 8] = mm(both, join[...]).astype(BF).reshape(8, FY, 256)
         copies.append(pltpu.make_async_copy(
             fo_s.at[pl.ds(8 * c, 8)], fine_out.at[pl.ds(8 * c, 8)], sems.at[4 + c]))
@@ -574,18 +562,17 @@
     hbm = pl.BlockSpec(memory_space=pltpu.HBM)
     scratch = [
         vm((896, 8), BF), vm((1792, 32), BF), vm((896, 128), F32), vm((1792, 128), F32), vm((1792, 128), F32),
-        vm((3, 2304, 256), BF), vm((2, 3456, 256), BF),
-        vm((XX, FY, 256), BF), vm((2, CX, CY, 256), BF), vm((2560, 256), BF),
-        vm((XX, YY, 768), BF),
-        vm((2, 12, 64, 128), BF), vm((2, 12, 64, 128), BF),
+        vm((4, 1152, 128), BF), vm((3, 384, 128), BF), vm((2, 3456, 256), BF),
+        vm((XX, FY, 256), BF), vm((2, CX, CY, 256), BF), vm((2048, 256), BF),
+        vm((XX, YY, 384), BF), vm((XX, YY, 128), BF),
         vm((2, 96, 256), F32), vm((2, 96, 256), BF), vm((2, 96, 256), BF),
-        vm((2, 48, 256), F32), vm((2, 2, 48, 128), BF), vm((2, 2, 48, 128), BF),
+        vm((2, 128, 128), F32), vm((4, 2, 128, 128), BF), vm((4, 2, 128, 128), BF), vm((2, 128, 128), F32),
         vm((2, 18, 16, 256), BF), vm((2, 2, 128, 128), BF), vm((2, 2, 128, 128), BF),
         vm((2, 2, 2, 16, 128), BF), vm((2, 288, 1152), BF),
         vm((512, 128), F32), vm((wide, ch, 128), F32), vm((deep, ch, 128), F32),
         vm((ch, 128), F32), vm((ch, 128), BF), vm((512, 128), BF),
         dma((6,)), dma((nx, 2)), dma((nx, 2)), dma((2,)), dma((2,)),
-        dma((2, 8)), dma((2, 8)), dma((8,)), dma((8,)),
+        dma((2, 8)), dma((2, 8)), dma((2,)), dma((2,)), dma((4, 2)), dma((4, 2)),
         dma((wide,)), dma((wide,)), dma((deep,)), dma((deep,)), dma((wide,)), dma((wide,)),
     ]
     inside = pl.BlockSpec(memory_space=pltpu.VMEM)
@@ -593,25 +580,25 @@
     perms = jnp.asarray(PERMS, BF)
     held = pl.pallas_call(
         functools.partial(kernel, sizes),
-        out_shape=(vm((XX, YY, 384), F32), vm((2304, 128), BF), vm((16, 16, 256), BF),
+        out_shape=(vm((XX, YY, 256), F32), vm((384, 128), BF), vm((2, 128, 128), BF), vm((16, 16, 256), BF),
                    vm((16, 16, 256), BF), vm((54, 32, 32), F32)),
         in_specs=[hbm] * 6,
-        out_specs=(inside,) * 5,
+        out_specs=(inside,) * 6,
         scratch_shapes=scratch,
         compiler_params=pltpu.CompilerParams(
             collective_id=0, has_side_effects=True, vmem_limit_bytes=40 * 1024 * 1024),
     )(*(in_hbm(v) for v in (fine_in, fine_w, coarse_out, coarse_cot, coarse_w, perms)))
     fine_out, rebuilt, grads_in, wg = pl.pallas_call(
-        functools.partial(finish, sizes),
+        finish,
         out_shape=(
             jax.ShapeDtypeStruct((FX, FY, 256), BF),
             jax.ShapeDtypeStruct((1, 16, 16, 256), BF),
             jax.ShapeDtypeStruct((1, 16, 16, 256), BF),
             jax.ShapeDtypeStruct((54, 32, 32), F32),
         ),
-        in_specs=[inside] * 5 + [hbm],
+        in_specs=[inside] * 6 + [hbm],
         out_specs=(hbm,) * 4,
-        scratch_shapes=[vm((XX, FY, 768), BF), vm((256, 256), BF), vm((FX, FY, 256), BF), dma((6,))],
+        scratch_shapes=[vm((2, 128, 128), F32), vm((XX, YY, 128), BF), vm((256, 256), BF), vm((FX, FY, 256), BF), dma((6,))],
         compiler_params=pltpu.CompilerParams(vmem_limit_bytes=24 * 1024 * 1024),
     )(*held, jnp.asarray(PERMS[JOIN_F:JOIN_F + 256], BF))
     wg = jnp.transpose(wg.reshape(2, 3, 3, 3, 32, 32), (0, 4, 5, 1, 2, 3))

time: 52 us -> 50.5 us (0.971)
  local copies, waits for them, and re-layouts: 0.9 us -> 0.01 us
  Pallas kernels: 50.3 us -> 49.7 us
    unnamed x2, local copies, waits for them, and re-layouts: 0.9 us -> 0.01 us
    pallas_call x2, Pallas kernels: 50.3 us -> 49.7 us  [the longest x1 47.2 us: on_device(): pl.pallas_call(functools.partial(kernel, sizes), out_shape=(vm((XX, YY, 2...]
where the time goes in v4:
time: 50.5 us; the launch traced here: 50.4 us
  Pallas kernels  49.7 us (98%)
  between operations  0.66 us (1%)
    pallas_call x1, Pallas kernels, on_device(): pl.pallas_call(functools.partial(kernel, sizes), out_shape=(vm((XX, YY, 2...  47.2 us
    pallas_call x1, Pallas kernels, on_device(): pl.pallas_call(finish, out_shape=(jax.ShapeDtypeStruct((FX, FY, 256), BF)...  2.55 us

profile of v4, /device:TPU:1, one launch (start us, length us, event | category | flops | bytes accessed | tf_op | source)
XLA Modules:
  0.0 50.4 jit_solution(9495852771420716998)
XLA Ops:
  0.6 0.0 copy-start
  0.6 47.2 %shard_map.102 = (f32[24,80,256]{2,1,0:T(8,128)S(1)}, bf16[384,128]{1,0:T(8,128)(2,1)S(1)}, bf16[2,128,128]{2,1,0:T(8,128)(2,1)S(1)}, bf16[16,16,256]{2,1,0:T(8,...) custom-call(bf16[16,64,256]{2,1,0:T(8,128)(2,1)} %fine_in.1, bf16[864,8]{1,0:T(8,128)(2,1)} %bitcast.10, ...), custom_call_target="tpu_custom_call" | custom-call | tf_op jit(solution)/shard_map/pallas_call | solution.py:581
  47.8 0.0 copy-done
  47.8 2.5 %shard_map.103 = (bf16[16,64,256]{2,1,0:T(8,128)(2,1)}, bf16[1,16,16,256]{3,2,1,0:T(8,128)(2,1)}, bf16[1,16,16,256]{3,2,1,0:T(8,128)(2,1)}, f32[54,32,32]{2,1,0:T(8,128)}) custom-call(f32[24,80,256]{2,1,0:T(8,128)S(1)} %get-tuple-element.14.state, bf16[384,128]{1,0:T(8,128)(2,1)S(1)} %get-tuple-element.15.last_rim, ...), custom_call_target="tpu_custom_call" | custom-call | tf_op jit(solution)/shard_map/pallas_call | solution.py:591
Async XLA Ops:
  0.6 47.2 %copy-start = (bf16[256,256]{1,0:T(8,128)(2,1)S(1)}, bf16[256,256]{1,0:T(8,128)(2,1)}, u32[]{:S(2)}) copy-start(bf16[256,256]{1,0:T(8,128)(2,1)} %constant.5.clone.join_h) | copy-start | bytes 393220

commit v5 on v3

--- a/solution.py
+++ b/solution.py
@@ -184,13 +184,14 @@
 
 
 def kernel(sizes, fine_in, fine_w, c_out, c_cot, coarse_w, perms_h,
-           state, last_band, rb_s, gi_s, wg_s,
+           fo_s, rb_s, gi_s, final,
+           state, last_band, u_last,
            wf, wc, t_fine, t_fwd, t_nat, bands_f, bands_c,
            xraw, craw, perms, u_fine, esend, erecv, yf, ysend, yrecv, kf, ksend, krecv,
            cown, cpack, crecv, ckrecv, cspread,
-           part, r1, r2, red, red_bf, final,
+           part, r1, r2, red, red_bf,
            load_sem, in_send, in_recv, x_send, x_recv, c_send, c_recv, f_send, f_recv,
-           p1_send, p1_recv, p2_send, p2_recv, p3_send, p3_recv):
+           sum_send, sum_recv):
     nx, ny, nz = sizes
     gx, gy, gz = lax.axis_index("gx"), lax.axis_index("gy"), lax.axis_index("gz")
     ky = nz // 2
@@ -293,6 +294,8 @@
     build_coarse, build_fine = band_builders(bands_f, bands_c, last_band, wf, wc, t_fine, t_fwd, t_nat)
     loads[0].wait()
     build_coarse()
+    loads[5].wait()
+    build_fine()
 
     for copy in loads[1:4]:
         copy.wait()
@@ -362,8 +365,10 @@
     wait_x()
     packed = jnp.concatenate([xraw[0:12].reshape(768, 256), xraw[12:24].reshape(768, 256)], axis=1)
     edges = mm(packed, perms[EDGE_F:EDGE_F + 512, :])
-    esend[0] = edges[:, :128].astype(BF).reshape(12, 64, 128)
-    esend[1] = edges[:, 128:].astype(BF).reshape(12, 64, 128)
+    for z in range(2):
+        both = edges[:, 128 * z:128 * z + 128].astype(BF).reshape(12, 64, 128)
+        esend[z, 0] = both[:, :32]
+        esend[z, 1] = both[:, 32:]
     for x in range(XX // 2):
         kf[0, 4 * x:4 * x + 4, :] = edges[64 * x:64 * x + 4]
         kf[1, 4 * x:4 * x + 4, :] = edges[64 * x + 60:64 * x + 64]
@@ -376,33 +381,33 @@
         yf[0, 4 * x:4 * x + 4, :] = state[x, 8:12, 0:256]
         yf[1, 4 * x:4 * x + 4, :] = state[x, 68:72, 0:256]
     ysend[...] = yf[...].astype(BF)
-    copies = []
+    copies, later = [], []
     for sy in (-1, 0, 1):
         y = (sy + 1) // 2
         for sz in (-1, 0, 1):
             z = (sz + 1) // 2
             if sy == 0 and sz == 0:
                 continue
-            src, dst = ((esend.at[z], erecv.at[1 - z]) if sy == 0 else
-                        (ysend.at[y], yrecv.at[1 - y]) if sz == 0 else
-                        (ksend.at[y, z], krecv.at[1 - y, 1 - z]))
-            n = len(copies)
-            copies.append(((0, sy, sz), remote(src, dst, f_send.at[n], f_recv.at[n], beside(sy, sz))))
+            pairs = ([(esend.at[z, part], erecv.at[1 - z, part]) for part in range(2)] if sy == 0 else
+                     [(ysend.at[y], yrecv.at[1 - y])] if sz == 0 else
+                     [(ksend.at[y, z], krecv.at[1 - y, 1 - z])])
+            for turn, (src, dst) in enumerate(pairs):
+                n = len(copies) + len(later)
+                (later if turn else copies).append(
+                    ((0, sy, sz), remote(src, dst, f_send.at[n], f_recv.at[n], beside(sy, sz))))
     start_f, wait_f = exchange(copies)
+    start_late, wait_late = exchange(later)
     start_f()
     for side in range(2):
         @pl.when(gz == side * (nz - 1))
         def _():
-            erecv[side] = jnp.zeros((12, 64, 128), BF)
+            erecv[side] = jnp.zeros((2, 12, 32, 128), BF)
             krecv[:, side] = jnp.zeros((2, 48, 128), BF)
 
         @pl.when(gy == side * (ny - 1))
         def _():
             yrecv[side] = jnp.zeros((96, 256), BF)
             krecv[side] = jnp.zeros((2, 48, 128), BF)
-
-    loads[5].wait()
-    build_fine()
 
     wait_c0()
     spread_rows(0)
@@ -410,6 +415,7 @@
     x2 = y2 - image_g
     e = d1 + silu_grad(y1) * back_g
     wait_c1 = send_rims(1, silu(x2), e)
+    start_late()
 
     place_lane = iota((32, 128), 1) // 32
 
@@ -440,30 +446,28 @@
 
     ch = 512 // wide
     mine = pl.ds(pl.multiple_of(me_wide * ch, 8), ch)
-    sends1 = []
+
+    def wait_all(buffer, send, recv):
+        for sem in (send, recv):
+            pltpu.make_async_copy(buffer, buffer, sem).wait()
+
     for d in range(1, wide):
         theirs = pl.ds(pl.multiple_of(lax.rem(me_wide + d, wide) * ch, 8), ch)
-        sends1.append(remote(part.at[theirs], r1.at[d], p1_send.at[d], p1_recv.at[d], peer_wide(d)))
-    for copy in sends1:
-        copy.start()
-
-    image_f, back_f = conv_pair(1)
-    x1 = y1 - image_f
-    dx2 = d2 + silu_grad(x2) * back_f
-    join = perms[JOIN_C:JOIN_C + 256, :]
-    for one, two, target in ((x1, x2, rb_s), (e, dx2, gi_s)):
-        both = jnp.concatenate([one.astype(BF), two.astype(BF)], axis=1)
-        target[...] = mm(swap, mm(both, join).astype(BF)).astype(BF).reshape(16, 16, 256)
+        remote(part.at[theirs], r1.at[d - 1], sum_send.at[0], sum_recv.at[0], peer_wide(d)).start()
 
     wait_f()
+    wait_late()
+
     def rims(from_left, from_right, count):
         left_lane = iota((count, 128), 1) < 64
         return (jnp.where(left_lane, from_left, pltpu.roll(from_right, 64, 1)),
                 jnp.where(left_lane, pltpu.roll(from_left, 64, 1), from_right))
 
-    early, late = rims(erecv[0].reshape(768, 128).astype(F32), erecv[1].reshape(768, 128).astype(F32), 768)
-    state[0:12, 8:72, 256:384] = early.reshape(12, 64, 128)
-    state[12:24, 8:72, 256:384] = late.reshape(12, 64, 128)
+    for half in range(2):
+        early, late = rims(*(erecv[side, half].reshape(384, 128).astype(F32) for side in range(2)), 384)
+        rows = slice(8 + 32 * half, 40 + 32 * half)
+        state[0:12, rows, 256:384] = early.reshape(12, 32, 128)
+        state[12:24, rows, 256:384] = late.reshape(12, 32, 128)
     for y, row in ((0, 4), (1, 72)):
         early, late = rims(krecv[y, 0].astype(F32), krecv[y, 1].astype(F32), 48)
         edge = yrecv[y].astype(F32)
@@ -495,34 +499,59 @@
 
     fine_conv(0, 0, 0)
 
-    for copy in sends1:
-        copy.wait()
+    image_f, back_f = conv_pair(1)
+    x1 = y1 - image_f
+    dx2 = d2 + silu_grad(x2) * back_f
+    join = perms[JOIN_C:JOIN_C + 256, :]
+    for one, two, target in ((x1, x2, rb_s), (e, dx2, gi_s)):
+        both = jnp.concatenate([one.astype(BF), two.astype(BF)], axis=1)
+        target[...] = mm(swap, mm(both, join).astype(BF)).astype(BF).reshape(16, 16, 256)
+
+    wait_all(r1, sum_send.at[0], sum_recv.at[0])
     total = part[mine, :]
-    for d in range(1, wide):
+    for d in range(wide - 1):
         total = total + r1[d]
     red[...] = total
     r2[me_deep] = total
-    sends2 = [remote(red, r2.at[me_deep], p2_send.at[d], p2_recv.at[d], peer_deep(d)) for d in range(1, deep)]
-    for copy in sends2:
-        copy.start()
+    for d in range(1, deep):
+        remote(red, r2.at[me_deep], sum_send.at[1], sum_recv.at[1], peer_deep(d)).start()
 
     fine_conv(1, 128, 1)
 
-    for copy in sends2:
-        copy.wait()
+    wait_all(r2.at[pl.ds(0, deep - 1)], sum_send.at[1], sum_recv.at[1])
     total = r2[0]
     for i in range(1, deep):
         total = total + r2[i]
     red_bf[...] = total.astype(BF)
     final[mine, :] = total.astype(BF)
-    sends3 = [remote(red_bf, final.at[mine], p3_send.at[d], p3_recv.at[d], peer_wide(d)) for d in range(1, wide)]
-    for copy in sends3:
+    for d in range(1, wide):
+        remote(red_bf, final.at[mine], sum_send.at[2], sum_recv.at[2], peer_wide(d)).start()
+
+    fine_conv(2, 0, 2)
+
+    def spread_last(x, carry):
+        v = fine_input(state, x, 128, limits)
+        u_last[x, :, 0:256] = pltpu.roll(v, 1, 0)[8:72].astype(BF)
+        u_last[x, :, 256:512] = v[8:72].astype(BF)
+        u_last[x, :, 512:768] = pltpu.roll(v, YY - 1, 0)[8:72].astype(BF)
+        return carry
+    lax.fori_loop(3, XX - 3, spread_last, 0)
+    for c in range(2):
+        x0 = 3 + 8 * c
+        lhs = jnp.concatenate(
+            [u_last[x0 + p:x0 + p + 8].reshape(512, 768) for p in range(3)], axis=1)
+        two = mm(lhs, last_band[...]).reshape(8, FY, 128) + state[x0 + 1:x0 + 9, 8:72, 0:128]
+        one = state[x0 + 1:x0 + 9, 8:72, 128:256]
+        both = jnp.concatenate([two, one], axis=2).astype(BF).reshape(512, 256)
+        fo_s[8 * c:8 * c + 8] = mm(both, perms[JOIN_F:JOIN_F + 256, :]).astype(BF).reshape(8, FY, 256)
+    wait_all(final.at[pl.ds(0, 512 - ch)], sum_send.at[2], sum_recv.at[2])
+
+
+def finish(fo_s, rb_s, gi_s, final, fine_out, rebuilt, grads_in, wg_out, wg_s, sems):
+    copies = [pltpu.make_async_copy(s, t, sems.at[i]) for i, (s, t) in enumerate((
+        (fo_s, fine_out), (rb_s, rebuilt.at[0]), (gi_s, grads_in.at[0]), (wg_s, wg_out)))]
+    for copy in copies[:3]:
         copy.start()
-
-    fine_conv(2, 0, 2)
-
-    for copy in sends3:
-        copy.wait()
     for g in range(14):
         rows = final[32 * g:32 * g + 32, :].astype(F32)
         for j in range(4):
@@ -530,37 +559,8 @@
             if t % 28 < 27:
                 turned_rows = rows if j == 0 else pltpu.roll(rows, 128 - 32 * j, 1)
                 wg_s[t - t // 28] = turned_rows[:, :32]
-
-
-def finish(sizes, state, last_band, rb_s, gi_s, wg_s, join_h,
-           fine_out, rebuilt, grads_in, wg_out, u_last, join, fo_s, sems):
-    nx, ny, nz = sizes
-    copies = [pltpu.make_async_copy(s, t, sems.at[i]) for i, (s, t) in enumerate((
-        (join_h, join), (rb_s, rebuilt.at[0]), (gi_s, grads_in.at[0]), (wg_s, wg_out)))]
+    copies[3].start()
     for copy in copies:
-        copy.start()
-    limits = fine_limits(sizes)
-
-    def spread(x, carry):
-        v = fine_input(state, x, 128, limits)
-        u_last[x, :, 0:256] = pltpu.roll(v, 1, 0)[8:72].astype(BF)
-        u_last[x, :, 256:512] = v[8:72].astype(BF)
-        u_last[x, :, 512:768] = pltpu.roll(v, YY - 1, 0)[8:72].astype(BF)
-        return carry
-    lax.fori_loop(3, XX - 3, spread, 0)
-    copies[0].wait()
-    for c in range(2):
-        x0 = 3 + 8 * c
-        lhs = jnp.concatenate(
-            [u_last[x0 + p:x0 + p + 8].reshape(512, 768) for p in range(3)], axis=1)
-        two = mm(lhs, last_band[...]).reshape(8, FY, 128) + state[x0 + 1:x0 + 9, 8:72, 0:128]
-        one = state[x0 + 1:x0 + 9, 8:72, 128:256]
-        both = jnp.concatenate([two, one], axis=2).astype(BF).reshape(512, 256)
-        fo_s[8 * c:8 * c + 8] = mm(both, join[...]).astype(BF).reshape(8, FY, 256)
-        copies.append(pltpu.make_async_copy(
-            fo_s.at[pl.ds(8 * c, 8)], fine_out.at[pl.ds(8 * c, 8)], sems.at[4 + c]))
-        copies[-1].start()
-    for copy in copies[1:]:
         copy.wait()
 
 
@@ -573,47 +573,47 @@
     vm, dma = pltpu.VMEM, pltpu.SemaphoreType.DMA
     hbm = pl.BlockSpec(memory_space=pltpu.HBM)
     scratch = [
+        vm((XX, YY, 384), F32), vm((2304, 128), BF), vm((XX, FY, 768), BF),
         vm((896, 8), BF), vm((1792, 32), BF), vm((896, 128), F32), vm((1792, 128), F32), vm((1792, 128), F32),
         vm((3, 2304, 256), BF), vm((2, 3456, 256), BF),
         vm((XX, FY, 256), BF), vm((2, CX, CY, 256), BF), vm((2560, 256), BF),
         vm((XX, YY, 768), BF),
-        vm((2, 12, 64, 128), BF), vm((2, 12, 64, 128), BF),
+        vm((2, 2, 12, 32, 128), BF), vm((2, 2, 12, 32, 128), BF),
         vm((2, 96, 256), F32), vm((2, 96, 256), BF), vm((2, 96, 256), BF),
         vm((2, 48, 256), F32), vm((2, 2, 48, 128), BF), vm((2, 2, 48, 128), BF),
         vm((2, 18, 16, 256), BF), vm((2, 2, 128, 128), BF), vm((2, 2, 128, 128), BF),
         vm((2, 2, 2, 16, 128), BF), vm((2, 288, 1152), BF),
-        vm((512, 128), F32), vm((wide, ch, 128), F32), vm((deep, ch, 128), F32),
-        vm((ch, 128), F32), vm((ch, 128), BF), vm((512, 128), BF),
+        vm((512, 128), F32), vm((wide - 1, ch, 128), F32), vm((deep, ch, 128), F32),
+        vm((ch, 128), F32), vm((ch, 128), BF),
         dma((6,)), dma((nx, 2)), dma((nx, 2)), dma((2,)), dma((2,)),
-        dma((2, 8)), dma((2, 8)), dma((8,)), dma((8,)),
-        dma((wide,)), dma((wide,)), dma((deep,)), dma((deep,)), dma((wide,)), dma((wide,)),
+        dma((2, 8)), dma((2, 8)), dma((10,)), dma((10,)),
+        dma((3,)), dma((3,)),
     ]
     inside = pl.BlockSpec(memory_space=pltpu.VMEM)
     in_hbm = functools.partial(pltpu.with_memory_space_constraint, memory_space=pltpu.HBM)
     perms = jnp.asarray(PERMS, BF)
     held = pl.pallas_call(
         functools.partial(kernel, sizes),
-        out_shape=(vm((XX, YY, 384), F32), vm((2304, 128), BF), vm((16, 16, 256), BF),
-                   vm((16, 16, 256), BF), vm((54, 32, 32), F32)),
+        out_shape=(vm((FX, FY, 256), BF), vm((16, 16, 256), BF), vm((16, 16, 256), BF), vm((512, 128), BF)),
         in_specs=[hbm] * 6,
-        out_specs=(inside,) * 5,
+        out_specs=(inside,) * 4,
         scratch_shapes=scratch,
         compiler_params=pltpu.CompilerParams(
             collective_id=0, has_side_effects=True, vmem_limit_bytes=40 * 1024 * 1024),
     )(*(in_hbm(v) for v in (fine_in, fine_w, coarse_out, coarse_cot, coarse_w, perms)))
     fine_out, rebuilt, grads_in, wg = pl.pallas_call(
-        functools.partial(finish, sizes),
+        finish,
         out_shape=(
             jax.ShapeDtypeStruct((FX, FY, 256), BF),
             jax.ShapeDtypeStruct((1, 16, 16, 256), BF),
             jax.ShapeDtypeStruct((1, 16, 16, 256), BF),
             jax.ShapeDtypeStruct((54, 32, 32), F32),
         ),
-        in_specs=[inside] * 5 + [hbm],
+        in_specs=[inside] * 4,
         out_specs=(hbm,) * 4,
-        scratch_shapes=[vm((XX, FY, 768), BF), vm((256, 256), BF), vm((FX, FY, 256), BF), dma((6,))],
+        scratch_shapes=[vm((54, 32, 32), F32), dma((4,))],
         compiler_params=pltpu.CompilerParams(vmem_limit_bytes=24 * 1024 * 1024),
-    )(*held, jnp.asarray(PERMS[JOIN_F:JOIN_F + 256], BF))
+    )(*held)
     wg = jnp.transpose(wg.reshape(2, 3, 3, 3, 32, 32), (0, 4, 5, 1, 2, 3))
     return fine_out, rebuilt, grads_in, wg
 

time: 52 us -> 47.6 us (0.915)
  Pallas kernels: 50.3 us -> 46.9 us
  local copies, waits for them, and re-layouts: 0.9 us -> 0 us
    pallas_call x2, Pallas kernels: 50.3 us -> 46.9 us  [the longest x1 45.7 us: on_device(): pl.pallas_call(functools.partial(kernel, sizes), out_shape=(vm((FX, FY, 2...]
    unnamed x2 -> x0, local copies, waits for them, and re-layouts: 0.9 us -> none
where the time goes in v5:
time: 47.6 us; the launch traced here: 47.5 us
  Pallas kernels  46.9 us (99%)
  between operations  0.64 us (1%)
    pallas_call x1, Pallas kernels, on_device(): pl.pallas_call(functools.partial(kernel, sizes), out_shape=(vm((FX, FY, 2...  45.7 us
    pallas_call x1, Pallas kernels, on_device(): pl.pallas_call(finish, out_shape=(jax.ShapeDtypeStruct((FX, FY, 256), BF)...  1.21 us

profile of v5, /device:TPU:1, one launch (start us, length us, event | category | flops | bytes accessed | tf_op | source)
XLA Modules:
  0.0 47.5 jit_solution(449003036056364268)
XLA Ops:
  0.6 45.7 %shard_map.93 = (bf16[16,64,256]{2,1,0:T(8,128)(2,1)S(1)}, bf16[16,16,256]{2,1,0:T(8,128)(2,1)S(1)}, bf16[16,16,256]{2,1,0:T(8,128)(2,1)S(1)}, bf16[512,128]{1,0:T(8,128)(2,1)S(1)}) custom-call(bf16[16,64,256]{2,1,0:T(8,128)(2,1)} %fine_in.1, bf16[864,8]{1,0:T(8,128)(2,1)} %bitcast.10, bf16[4,4,16,256]{3,2,1,0:T(8,128)(2,1)} %c_out.1, ...), custom_call_target="tpu_custom_call" | custom-call | tf_op jit(solution)/shard_map/pallas_call | solution.py:595
  46.3 1.2 %shard_map.94 = (bf16[16,64,256]{2,1,0:T(8,128)(2,1)}, bf16[1,16,16,256]{3,2,1,0:T(8,128)(2,1)}, bf16[1,16,16,256]{3,2,1,0:T(8,128)(2,1)}, f32[54,32,32]{2,1,0:T(8,128)}) custom-call(bf16[16,64,256]{2,1,0:T(8,128)(2,1)S(1)} %get-tuple-element.12.fo_s, bf16[16,16,256]{2,1,0:T(8,128)(2,1)S(1)} %get-tuple-element.13.rb_s, ...), custom_call_target="tpu_custom_call" | custom-call | tf_op jit(solution)/shard_map/pallas_call | solution.py:604

commit v6 on v5

--- a/solution.py
+++ b/solution.py
@@ -19,8 +19,7 @@
 
 Z_X2 = list(range(16)) + [-4, -3, -2, -1] + [NONE] * 4 + [16, 17, 18, 19] + [NONE] * 4
 Z_X1 = list(range(16)) + [NONE] * 4 + [-4, -3, -2, -1] + [NONE] * 4 + [16, 17, 18, 19]
-C_SLOTS = ([(0, z) for z in range(4)] + [(0, -1), (1, -1), (0, 4), (1, 4)]
-           + [(1, z) for z in range(4)])
+C_SLOTS = [(f, z) for z in range(4) for f in range(2)] + [(f, z) for z in (-1, 4) for f in range(2)]
 
 
 def constants():
@@ -41,27 +40,11 @@
     for x in range(16):
         for y in range(16):
             swap[y * 16 + x, x * 16 + y] = 1.0
-    split_coarse = np.zeros((256, 256), np.float32)
-    for z in range(4):
-        for c in range(32):
-            split_coarse[z * 64 + c, z * 32 + c] = 1.0
-            split_coarse[z * 64 + 32 + c, 128 + z * 32 + c] = 1.0
-    pack = np.zeros((512, 256), np.float32)
-    unpack = np.zeros((256, 256), np.float32)
-    lanes = np.arange(32)
-    for half in range(2):
-        for field in range(2):
-            for side in range(2):
-                pack[half * 256 + field * 128 + side * 96 + lanes,
-                     side * 128 + half * 64 + field * 32 + lanes] = 1.0
-                unpack[side * 128 + half * 64 + field * 32 + lanes,
-                       half * 128 + side * 64 + field * 32 + lanes] = 1.0
-    return np.concatenate([
-        split_fine, split_fine.T, edge_fine, swap, split_coarse, split_coarse.T, pack, unpack])
+    return np.concatenate([split_fine, split_fine.T, edge_fine, swap])
 
 
 PERMS = constants()
-SPLIT_F, JOIN_F, EDGE_F, SWAP, SPLIT_C, JOIN_C, PACK_C, UNPACK_C = 0, 256, 512, 1024, 1280, 1536, 1792, 2304
+SPLIT_F, JOIN_F, EDGE_F, SWAP = 0, 256, 512, 1024
 
 
 def silu(v):
@@ -137,13 +120,14 @@
             lane_slot = iota((32, 128), 1) // 32
             for at, (field, z) in enumerate(C_SLOTS):
                 rows = pl.ds(pl.multiple_of(i * 384 + at * 32, 32), 32)
-                piece = jnp.zeros((32, 128), F32)
+                pieces = [jnp.zeros((32, 128), F32)] * 2
                 for k in range(3):
                     if 0 <= z + 1 - k < 4:
-                        piece = jnp.where(lane_slot == z + 1 - k, tiles[field][k], piece)
-                bands_c[stage, rows, 128 * field:128 * field + 128] = piece.astype(BF)
-                other = 128 - 128 * field
-                bands_c[stage, rows, other:other + 128] = jnp.zeros((32, 128), BF)
+                        column, place = divmod((z + 1 - k) * 2 + 1 - field, 4)
+                        pieces[column] = jnp.where(
+                            lane_slot == place, tiles[(field + stage) % 2][k], pieces[column])
+                for column in range(2):
+                    bands_c[stage, rows, 128 * column:128 * column + 128] = pieces[column].astype(BF)
             return carry
         lax.fori_loop(0, 9, body, 0)
 
@@ -188,9 +172,9 @@
            state, last_band, u_last,
            wf, wc, t_fine, t_fwd, t_nat, bands_f, bands_c,
            xraw, craw, perms, u_fine, esend, erecv, yf, ysend, yrecv, kf, ksend, krecv,
-           cown, cpack, crecv, ckrecv, cspread,
+           local, plz, plyf, ply, rz, ry, rk, ystage, cown, cpack, crecv, ckrecv, cspread,
            part, r1, r2, red, red_bf,
-           load_sem, in_send, in_recv, x_send, x_recv, c_send, c_recv, f_send, f_recv,
+           load_sem, in_send, in_recv, rim_send, rim_recv, x_send, x_recv, c_send, c_recv, f_send, f_recv,
            sum_send, sum_recv):
     nx, ny, nz = sizes
     gx, gy, gz = lax.axis_index("gx"), lax.axis_index("gy"), lax.axis_index("gz")
@@ -216,11 +200,15 @@
     for d in range(1, deep):
         pl.semaphore_signal(barrier, inc=1, device_id=peer_deep(d), device_id_type=MESH)
     for sy in (-1, 0, 1):
-        for sz in (-1, 1):
-            to = {"gy": lax.rem(gy + sy + ny, ny), "gz": lax.rem(gz + sz + nz, nz)}
-            pl.semaphore_signal(barrier, inc=1, device_id=to, device_id_type=MESH)
+        for sz in (-1, 0, 1):
+            if sy or sz:
+                for g in range(nx):
+                    to = {"gx": g, "gy": lax.rem(gy + sy + ny, ny), "gz": lax.rem(gz + sz + nz, nz)}
+                    pl.semaphore_signal(barrier, inc=1, device_id=to, device_id_type=MESH)
 
     loads = [
+        (c_out, local.at[0]),
+        (c_cot, local.at[1]),
         (coarse_w, wc.at[pl.ds(0, 1728)]),
         (perms_h, perms),
         (c_out.at[gx], craw.at[0, pl.ds(gx * 4, 4)]),
@@ -234,7 +222,25 @@
     state[:, 0:8, :] = jnp.zeros((XX, 8, 384), F32)
     state[:, 72:80, :] = jnp.zeros((XX, 8, 384), F32)
     part[14 * 32:, :] = jnp.zeros((64, 128), F32)
-    pl.semaphore_wait(barrier, wide - 1 + deep - 1 + 6)
+    plyf[...] = jnp.zeros((2, 64, 256), F32)
+    loads[0].wait()
+    loads[1].wait()
+    tile_lane = iota((256, 256), 1)
+    low_half = tile_lane % 64 < 32
+    rim_left = iota((128, 128), 1) < 64
+    pair = jnp.where(low_half, silu(local[0].reshape(256, 256).astype(F32)),
+                     local[1].reshape(256, 256).astype(F32))
+    for g in range(4):
+        for x in range(4):
+            row = 64 * g + 16 * x
+            plyf[0, 16 * g + x:16 * g + x + 1, :] = pair[row:row + 1]
+            plyf[1, 16 * g + x:16 * g + x + 1, :] = pair[row + 15:row + 16]
+    ply[...] = plyf[...].astype(BF).reshape(2, 4, 16, 256)
+    by_x = pair.reshape(4, 2, 32, 256)
+    first, second = by_x[:, 0].reshape(128, 256), by_x[:, 1].reshape(128, 256)
+    plz[0] = jnp.where(rim_left, first[:, :128], pltpu.roll(second[:, :128], 64, 1)).astype(BF).reshape(4, 2, 16, 128)
+    plz[1] = jnp.where(rim_left, pltpu.roll(first[:, 128:], 64, 1), second[:, 128:]).astype(BF).reshape(4, 2, 16, 128)
+    pl.semaphore_wait(barrier, wide - 1 + deep - 1 + 8 * nx)
 
     def remote(src, dst, send, recv, to):
         return pltpu.make_async_remote_copy(
@@ -249,6 +255,33 @@
                                   in_send.at[d, i], in_recv.at[d, i], peer_x(d)))
     for copy in gathers:
         copy.start()
+
+    def when(step, sign, act):
+        at = [(g + sign * n >= 0) & (g + sign * n < size) for g, n, size in zip((gy, gz), step, (ny, nz)) if n != 0]
+
+        @pl.when(functools.reduce(jnp.logical_and, at))
+        def _():
+            act()
+
+    def beside(sy, sz):
+        return {"gy": lax.clamp(0, gy + sy, ny - 1), "gz": lax.clamp(0, gz + sz, nz - 1)}
+
+    ways = [(sy, sz) for sy in (-1, 0, 1) for sz in (-1, 0, 1) if sy or sz]
+
+    def rim_refs(sy, sz, g):
+        y, z = (sy + 1) // 2, (sz + 1) // 2
+        if sy == 0:
+            return plz.at[z, g], rz.at[1 - z]
+        if sz == 0:
+            return ply.at[y, g], ry.at[1 - y]
+        return ply.at[y, g, :, pl.ds(128 * z, 128)], rk.at[1 - y, 1 - z]
+
+    for n, (sy, sz) in enumerate(ways):
+        def send_way():
+            for g in range(nx):
+                src, dst = rim_refs(sy, sz, g)
+                remote(src, dst.at[gx], rim_send.at[n], rim_recv.at[n], {"gx": g, **beside(sy, sz)}).start()
+        when((sy, sz), 1, send_way)
     low_x = remote(fine_in.at[pl.ds(0, FH)], xraw.at[pl.ds(FX + FH, FH)],
                    x_send.at[0], x_recv.at[0], {"gx": lax.max(gx - 1, 0)})
     high_x = remote(fine_in.at[pl.ds(FX - FH, FH)], xraw.at[pl.ds(0, FH)],
@@ -277,9 +310,6 @@
                     copy.wait_recv()
         return start, wait
 
-    def beside(sy, sz):
-        return {"gy": lax.clamp(0, gy + sy, ny - 1), "gz": lax.clamp(0, gz + sz, nz - 1)}
-
     start_x, wait_x = exchange([((-1, 0, 0), low_x), ((1, 0, 0), high_x)])
     start_x()
 
@@ -292,61 +322,52 @@
         xraw[FX + FH:] = jnp.zeros((FH, FY, 256), BF)
 
     build_coarse, build_fine = band_builders(bands_f, bands_c, last_band, wf, wc, t_fine, t_fwd, t_nat)
-    loads[0].wait()
+    loads[2].wait()
     build_coarse()
-    loads[5].wait()
+    loads[7].wait()
     build_fine()
 
-    for copy in loads[1:4]:
+    def wait_all(buffer, *sems):
+        for sem in sems:
+            pltpu.make_async_copy(buffer, buffer, sem).wait()
+
+    for side in range(2):
+        @pl.when(gz == side * (nz - 1))
+        def _():
+            rz[side] = jnp.zeros((4, 2, 16, 128), BF)
+            rk[:, side] = jnp.zeros((2, 4, 16, 128), BF)
+
+        @pl.when(gy == side * (ny - 1))
+        def _():
+            ry[side] = jnp.zeros((4, 16, 256), BF)
+            rk[side] = jnp.zeros((2, 4, 16, 128), BF)
+    for copy in loads[3:6]:
         copy.wait()
     for copy in gathers:
         copy.wait()
+    for n, (sy, sz) in enumerate(ways):
+        got = rim_refs(sy, sz, 0)[1]
+        when((sy, sz), 1, functools.partial(wait_all, got, rim_send.at[n]))
+        when((sy, sz), -1, functools.partial(wait_all, got, rim_recv.at[n]))
     swap = perms[SWAP:SWAP + 256, :]
 
-    def halves_of(raw):
-        both = mm(mm(swap, raw.reshape(256, 256)).astype(BF), perms[SPLIT_C:SPLIT_C + 256, :])
-        return both[:, :128], both[:, 128:]
-
-    def send_rims(stage, a, b):
-        both = jnp.concatenate([a, b], axis=1).astype(BF)
-        cown[stage, 1:17] = both.reshape(16, 16, 256)
-        packed = mm(jnp.concatenate([both[:128], both[128:]], axis=1), perms[PACK_C:PACK_C + 512, :]).astype(BF)
-        cpack[stage, 0] = packed[:, :128]
-        cpack[stage, 1] = packed[:, 128:]
-        copies = []
-        for sy in (-1, 0, 1):
-            y = (sy + 1) // 2
-            for sz in (-1, 0, 1):
-                z = (sz + 1) // 2
-                if sy == 0 and sz == 0:
-                    continue
-                src, dst = ((cpack.at[stage, z], crecv.at[stage, 1 - z]) if sy == 0 else
-                            (cown.at[stage, 1 + 15 * y], cown.at[stage, 17 - 17 * y]) if sz == 0 else
-                            (cpack.at[stage, z, pl.ds(112 * y, 16)], ckrecv.at[stage, 1 - y, 1 - z]))
-                n = len(copies)
-                copies.append(((0, sy, sz), remote(
-                    src, dst, c_send.at[stage, n], c_recv.at[stage, n], beside(sy, sz))))
-        start, wait = exchange(copies)
-        start()
-        for side in range(2):
-            @pl.when(gz == side * (nz - 1))
-            def _():
-                crecv[stage, side] = jnp.zeros((128, 128), BF)
-                ckrecv[stage, :, side] = jnp.zeros((2, 16, 128), BF)
-
-            @pl.when(gy == side * (ny - 1))
-            def _():
-                cown[stage, 17 * side] = jnp.zeros((16, 256), BF)
-                ckrecv[stage, side] = jnp.zeros((2, 16, 128), BF)
-        return wait
-
-    def spread_rows(stage):
-        unpack = perms[UNPACK_C:UNPACK_C + 256, :]
-        inner = mm(jnp.concatenate([crecv[stage, 0], crecv[stage, 1]], axis=1), unpack)
-        ends = [mm(jnp.concatenate([ckrecv[stage, y, 0], ckrecv[stage, y, 1]], axis=1), unpack) for y in range(2)]
-        rim = jnp.concatenate([ends[0][:, 128:], inner[:, :128], inner[:, 128:], ends[1][:, :128]], axis=0)
-        both = cown[stage].reshape(288, 256).astype(F32)
-        values = jnp.concatenate([both[:, :128], rim, both[:, 128:]], axis=1)
+    def side_by_side(from_low, from_high):
+        return (jnp.where(rim_left, from_low, pltpu.roll(from_high, 64, 1)),
+                jnp.where(rim_left, pltpu.roll(from_low, 64, 1), from_high))
+
+    first, second = side_by_side(*(rz[side].reshape(128, 128).astype(F32) for side in range(2)))
+    rim = jnp.concatenate([first.reshape(4, 32, 128), second.reshape(4, 32, 128)], axis=1).reshape(256, 128)
+    turned = mm(swap, jnp.concatenate(
+        [craw[0].reshape(256, 256), craw[1].reshape(256, 256), rim.astype(BF)], axis=1))
+    outs, cots, rim = turned[:, :256], turned[:, 256:512], turned[:, 512:]
+    corner_left = iota((16, 128), 1) < 64
+    for y in range(2):
+        for g in range(4):
+            ystage[y, 4 * g:4 * g + 4, 0:256] = ry[y, g].astype(F32)[0:4]
+            corner = jnp.where(corner_left, rk[y, 1, g].astype(F32), rk[y, 0, g].astype(F32))
+            ystage[y, 4 * g:4 * g + 4, 256:384] = pltpu.roll(corner, 64, 1)[0:4]
+
+    def spread_rows(stage, values):
         row = iota((288, 384), 0) % 16
         cspread[stage, :, 0:384] = jnp.where(row == 0, 0.0, pltpu.roll(values, 1, 0)).astype(BF)
         cspread[stage, :, 384:768] = values.astype(BF)
@@ -354,14 +375,39 @@
 
     def conv_pair(stage):
         lhs = jnp.concatenate([cspread[stage, 16 * p:16 * p + 256, :] for p in range(3)], axis=1)
-        both = mm(lhs, bands_c[stage])
-        return both[:, :128], both[:, 128:]
-
-    y1, y2 = halves_of(craw[0])
-    d1, d2 = halves_of(craw[1])
-    wait_c0 = send_rims(0, silu(y1), d2)
-
-    loads[4].wait()
+        return mm(lhs, bands_c[stage])
+
+    pair = jnp.where(low_half, silu(outs), cots)
+    spread_rows(0, jnp.concatenate(
+        [ystage[0], jnp.concatenate([pair, rim], axis=1), ystage[1]], axis=0))
+    result = conv_pair(0)
+    middle = jnp.where(low_half, cots + silu_grad(outs) * result, outs - result)
+    inner = jnp.where(low_half, middle, silu(middle))
+    cown[1:17] = inner.astype(BF).reshape(16, 16, 256)
+    early, late = inner[:128], inner[128:]
+    cpack[0] = jnp.where(rim_left, early[:, :128], pltpu.roll(late[:, :128], 64, 1)).astype(BF)
+    cpack[1] = jnp.where(rim_left, pltpu.roll(early[:, 128:], 64, 1), late[:, 128:]).astype(BF)
+    copies = []
+    for n, (sy, sz) in enumerate(ways):
+        y, z = (sy + 1) // 2, (sz + 1) // 2
+        src, dst = ((cpack.at[z], crecv.at[1 - z]) if sy == 0 else
+                    (cown.at[1 + 15 * y], cown.at[17 - 17 * y]) if sz == 0 else
+                    (cown.at[1 + 15 * y, :, pl.ds(128 * z, 128)], ckrecv.at[1 - y, 1 - z]))
+        copies.append(((0, sy, sz), remote(src, dst, c_send.at[n], c_recv.at[n], beside(sy, sz))))
+    start_c, wait_c = exchange(copies)
+    start_c()
+    for side in range(2):
+        @pl.when(gz == side * (nz - 1))
+        def _():
+            crecv[side] = jnp.zeros((128, 128), BF)
+            ckrecv[:, side] = jnp.zeros((2, 16, 128), BF)
+
+        @pl.when(gy == side * (ny - 1))
+        def _():
+            cown[17 * side] = jnp.zeros((16, 256), BF)
+            ckrecv[side] = jnp.zeros((2, 16, 128), BF)
+
+    loads[6].wait()
     wait_x()
     packed = jnp.concatenate([xraw[0:12].reshape(768, 256), xraw[12:24].reshape(768, 256)], axis=1)
     edges = mm(packed, perms[EDGE_F:EDGE_F + 512, :])
@@ -398,6 +444,7 @@
     start_f, wait_f = exchange(copies)
     start_late, wait_late = exchange(later)
     start_f()
+    start_late()
     for side in range(2):
         @pl.when(gz == side * (nz - 1))
         def _():
@@ -409,25 +456,20 @@
             yrecv[side] = jnp.zeros((96, 256), BF)
             krecv[side] = jnp.zeros((2, 48, 128), BF)
 
-    wait_c0()
-    spread_rows(0)
-    image_g, back_g = conv_pair(0)
-    x2 = y2 - image_g
-    e = d1 + silu_grad(y1) * back_g
-    wait_c1 = send_rims(1, silu(x2), e)
-    start_late()
-
     place_lane = iota((32, 128), 1) // 32
 
-    def fold(stage, cot):
-        turned_cot = jnp.transpose(cot).astype(BF)
+    def fold(stage, pair):
+        columns = jnp.transpose(pair)
+        turned_cot = jnp.concatenate(
+            [columns[64 * z + 32 * (1 - stage):64 * z + 32 * (2 - stage)] for z in range(4)], axis=0).astype(BF)
+        blocks = [mm(turned_cot, cspread[stage, 16 * p:16 * p + 256, :]) for p in range(3)]
         for q in range(3):
             for p in range(3):
-                block = mm(turned_cot, cspread[stage, 16 * p:16 * p + 256, 384 * q:384 * q + 256])
+                block = blocks[p][:, 384 * q:384 * q + 384]
                 for k in range(3):
                     acc = None
                     for z in range(4):
-                        at = C_SLOTS.index((0, z + k - 1))
+                        at = C_SLOTS.index((stage, z + k - 1))
                         column = 128 * (at // 4)
                         term = jnp.where(place_lane == at % 4,
                                          block[32 * z:32 * z + 32, column:column + 128], 0.0)
@@ -439,21 +481,29 @@
                     if t % 4 == 3 or t in (26, 54):
                         part[t // 4 * 32:t // 4 * 32 + 32, :] = held
 
-    fold(0, d2)
-    wait_c1()
-    spread_rows(1)
-    fold(1, e)
+    fold(0, pair)
+    wait_c()
+    early, late = side_by_side(crecv[0].astype(F32), crecv[1].astype(F32))
+    both = cown[...].reshape(288, 256).astype(F32)
+    ends = [pltpu.roll(jnp.where(corner_left, ckrecv[y, 1].astype(F32), ckrecv[y, 0].astype(F32)), 64, 1)
+            for y in range(2)]
+    rim = jnp.concatenate([ends[0], early, late, ends[1]], axis=0)
+    spread_rows(1, jnp.concatenate([both, rim], axis=1))
+    fold(1, inner)
 
     ch = 512 // wide
     mine = pl.ds(pl.multiple_of(me_wide * ch, 8), ch)
-
-    def wait_all(buffer, send, recv):
-        for sem in (send, recv):
-            pltpu.make_async_copy(buffer, buffer, sem).wait()
 
     for d in range(1, wide):
         theirs = pl.ds(pl.multiple_of(lax.rem(me_wide + d, wide) * ch, 8), ch)
         remote(part.at[theirs], r1.at[d - 1], sum_send.at[0], sum_recv.at[0], peer_wide(d)).start()
+
+    result = conv_pair(1)
+    last = jnp.where(low_half, outs - result, cots + silu_grad(middle) * result)
+    both = mm(swap, jnp.concatenate(
+        [jnp.where(low_half, last, middle), jnp.where(low_half, middle, last)], axis=1).astype(BF)).astype(BF)
+    rb_s[...] = both[:, :256].reshape(16, 16, 256)
+    gi_s[...] = both[:, 256:].reshape(16, 16, 256)
 
     wait_f()
     wait_late()
@@ -499,14 +549,6 @@
 
     fine_conv(0, 0, 0)
 
-    image_f, back_f = conv_pair(1)
-    x1 = y1 - image_f
-    dx2 = d2 + silu_grad(x2) * back_f
-    join = perms[JOIN_C:JOIN_C + 256, :]
-    for one, two, target in ((x1, x2, rb_s), (e, dx2, gi_s)):
-        both = jnp.concatenate([one.astype(BF), two.astype(BF)], axis=1)
-        target[...] = mm(swap, mm(both, join).astype(BF)).astype(BF).reshape(16, 16, 256)
-
     wait_all(r1, sum_send.at[0], sum_recv.at[0])
     total = part[mine, :]
     for d in range(wide - 1):
@@ -576,17 +618,19 @@
         vm((XX, YY, 384), F32), vm((2304, 128), BF), vm((XX, FY, 768), BF),
         vm((896, 8), BF), vm((1792, 32), BF), vm((896, 128), F32), vm((1792, 128), F32), vm((1792, 128), F32),
         vm((3, 2304, 256), BF), vm((2, 3456, 256), BF),
-        vm((XX, FY, 256), BF), vm((2, CX, CY, 256), BF), vm((2560, 256), BF),
+        vm((XX, FY, 256), BF), vm((2, CX, CY, 256), BF), vm((1280, 256), BF),
         vm((XX, YY, 768), BF),
         vm((2, 2, 12, 32, 128), BF), vm((2, 2, 12, 32, 128), BF),
         vm((2, 96, 256), F32), vm((2, 96, 256), BF), vm((2, 96, 256), BF),
         vm((2, 48, 256), F32), vm((2, 2, 48, 128), BF), vm((2, 2, 48, 128), BF),
-        vm((2, 18, 16, 256), BF), vm((2, 2, 128, 128), BF), vm((2, 2, 128, 128), BF),
-        vm((2, 2, 2, 16, 128), BF), vm((2, 288, 1152), BF),
+        vm((2, 4, 4, 16, 256), BF), vm((2, 4, 2, 16, 128), BF), vm((2, 64, 256), F32), vm((2, 4, 16, 256), BF),
+        vm((2, 4, 2, 16, 128), BF), vm((2, 4, 16, 256), BF), vm((2, 2, 4, 16, 128), BF), vm((2, 16, 384), F32),
+        vm((18, 16, 256), BF), vm((2, 128, 128), BF), vm((2, 128, 128), BF), vm((2, 2, 16, 128), BF),
+        vm((2, 288, 1152), BF),
         vm((512, 128), F32), vm((wide - 1, ch, 128), F32), vm((deep, ch, 128), F32),
         vm((ch, 128), F32), vm((ch, 128), BF),
-        dma((6,)), dma((nx, 2)), dma((nx, 2)), dma((2,)), dma((2,)),
-        dma((2, 8)), dma((2, 8)), dma((10,)), dma((10,)),
+        dma((8,)), dma((nx, 2)), dma((nx, 2)), dma((8,)), dma((8,)), dma((2,)), dma((2,)),
+        dma((8,)), dma((8,)), dma((10,)), dma((10,)),
         dma((3,)), dma((3,)),
     ]
     inside = pl.BlockSpec(memory_space=pltpu.VMEM)

time: 47.6 us -> 46.4 us (0.975)
  Pallas kernels: 46.9 us -> 45.6 us
    pallas_call x1, Pallas kernels: 45.7 us -> 44.4 us  [on_device(): pl.pallas_call(functools.partial(kernel, sizes), out_shape=(vm((FX, FY, 2...]
where the time goes in v6:
time: 46.4 us; the launch traced here: 46.3 us
  Pallas kernels  45.6 us (98%)
  between operations  0.64 us (1%)
    pallas_call x1, Pallas kernels, on_device(): pl.pallas_call(functools.partial(kernel, sizes), out_shape=(vm((FX, FY, 2...  44.4 us
    pallas_call x1, Pallas kernels, on_device(): pl.pallas_call(finish, out_shape=(jax.ShapeDtypeStruct((FX, FY, 256), BF)...  1.21 us

profile of v6, /device:TPU:1, one launch (start us, length us, event | category | flops | bytes accessed | tf_op | source)
XLA Modules:
  0.0 46.3 jit_solution(13190511125834077946)
XLA Ops:
  0.6 44.4 %shard_map.93 = (bf16[16,64,256]{2,1,0:T(8,128)(2,1)S(1)}, bf16[16,16,256]{2,1,0:T(8,128)(2,1)S(1)}, bf16[16,16,256]{2,1,0:T(8,128)(2,1)S(1)}, bf16[512,128]{1,0:T(8,128)(2,1)S(1)}) custom-call(bf16[16,64,256]{2,1,0:T(8,128)(2,1)} %fine_in.1, bf16[864,8]{1,0:T(8,128)(2,1)} %bitcast.10, bf16[4,4,16,256]{3,2,1,0:T(8,128)(2,1)} %c_out.1, ...), custom_call_target="tpu_custom_call" | custom-call | tf_op jit(solution)/shard_map/pallas_call | solution.py:639
  45.0 1.2 %shard_map.94 = (bf16[16,64,256]{2,1,0:T(8,128)(2,1)}, bf16[1,16,16,256]{3,2,1,0:T(8,128)(2,1)}, bf16[1,16,16,256]{3,2,1,0:T(8,128)(2,1)}, f32[54,32,32]{2,1,0:T(8,128)}) custom-call(bf16[16,64,256]{2,1,0:T(8,128)(2,1)S(1)} %get-tuple-element.12.fo_s, bf16[16,16,256]{2,1,0:T(8,128)(2,1)S(1)} %get-tuple-element.13.rb_s, ...), custom_call_target="tpu_custom_call" | custom-call | tf_op jit(solution)/shard_map/pallas_call | solution.py:648

commit v7 on v6

--- a/solution.py
+++ b/solution.py
@@ -171,10 +171,10 @@
            fo_s, rb_s, gi_s, final,
            state, last_band, u_last,
            wf, wc, t_fine, t_fwd, t_nat, bands_f, bands_c,
-           xraw, craw, perms, u_fine, esend, erecv, yf, ysend, yrecv, kf, ksend, krecv,
+           xraw, craw, perms, u_fine, esend, erecv, hsend, hrecv, yf, ysend, yrecv, kf, ksend, krecv,
            local, plz, plyf, ply, rz, ry, rk, ystage, cown, cpack, crecv, ckrecv, cspread,
            part, r1, r2, red, red_bf,
-           load_sem, in_send, in_recv, rim_send, rim_recv, x_send, x_recv, c_send, c_recv, f_send, f_recv,
+           load_sem, in_send, in_recv, rim_send, rim_recv, x_send, x_recv, c_send, c_recv, f_send, f_recv, z_send, z_recv, h_send, h_recv,
            sum_send, sum_recv):
     nx, ny, nz = sizes
     gx, gy, gz = lax.axis_index("gx"), lax.axis_index("gy"), lax.axis_index("gz")
@@ -222,6 +222,53 @@
     state[:, 0:8, :] = jnp.zeros((XX, 8, 384), F32)
     state[:, 72:80, :] = jnp.zeros((XX, 8, 384), F32)
     part[14 * 32:, :] = jnp.zeros((64, 128), F32)
+    pl.semaphore_wait(barrier, wide - 1 + deep - 1 + 8 * nx)
+
+    def remote(src, dst, send, recv, to):
+        return pltpu.make_async_remote_copy(
+            src_ref=src, dst_ref=dst, send_sem=send, recv_sem=recv,
+            device_id=to, device_id_type=MESH)
+
+    gathers = []
+    for d in range(1, nx):
+        to = lax.rem(gx + d, nx)
+        for i, src in enumerate((c_out, c_cot)):
+            gathers.append(remote(src.at[to], craw.at[i, pl.ds(gx * 4, 4)],
+                                  in_send.at[d, i], in_recv.at[d, i], peer_x(d)))
+    for copy in gathers:
+        copy.start()
+
+    low_x = remote(fine_in.at[pl.ds(0, FH)], xraw.at[pl.ds(FX + FH, FH)],
+                   x_send.at[0], x_recv.at[0], {"gx": lax.max(gx - 1, 0)})
+    high_x = remote(fine_in.at[pl.ds(FX - FH, FH)], xraw.at[pl.ds(0, FH)],
+                    x_send.at[1], x_recv.at[1], {"gx": lax.min(gx + 1, nx - 1)})
+
+    def exchange(copies):
+        def inside(step, sign):
+            at = [(g + sign * s >= 0) & (g + sign * s < n)
+                  for g, s, n in zip((gx, gy, gz), step, sizes) if s != 0]
+            return functools.reduce(jnp.logical_and, at)
+
+        def start():
+            for step, copy in copies:
+                @pl.when(inside(step, 1))
+                def _():
+                    copy.start()
+
+        def wait():
+            for step, copy in copies:
+                @pl.when(inside(step, 1))
+                def _():
+                    copy.wait_send()
+
+                @pl.when(inside(step, -1))
+                def _():
+                    copy.wait_recv()
+        return start, wait
+
+    start_x, wait_x = exchange([((-1, 0, 0), low_x), ((1, 0, 0), high_x)])
+    start_x()
+
     plyf[...] = jnp.zeros((2, 64, 256), F32)
     loads[0].wait()
     loads[1].wait()
@@ -240,21 +287,6 @@
     first, second = by_x[:, 0].reshape(128, 256), by_x[:, 1].reshape(128, 256)
     plz[0] = jnp.where(rim_left, first[:, :128], pltpu.roll(second[:, :128], 64, 1)).astype(BF).reshape(4, 2, 16, 128)
     plz[1] = jnp.where(rim_left, pltpu.roll(first[:, 128:], 64, 1), second[:, 128:]).astype(BF).reshape(4, 2, 16, 128)
-    pl.semaphore_wait(barrier, wide - 1 + deep - 1 + 8 * nx)
-
-    def remote(src, dst, send, recv, to):
-        return pltpu.make_async_remote_copy(
-            src_ref=src, dst_ref=dst, send_sem=send, recv_sem=recv,
-            device_id=to, device_id_type=MESH)
-
-    gathers = []
-    for d in range(1, nx):
-        to = lax.rem(gx + d, nx)
-        for i, src in enumerate((c_out, c_cot)):
-            gathers.append(remote(src.at[to], craw.at[i, pl.ds(gx * 4, 4)],
-                                  in_send.at[d, i], in_recv.at[d, i], peer_x(d)))
-    for copy in gathers:
-        copy.start()
 
     def when(step, sign, act):
         at = [(g + sign * n >= 0) & (g + sign * n < size) for g, n, size in zip((gy, gz), step, (ny, nz)) if n != 0]
@@ -282,36 +314,21 @@
                 src, dst = rim_refs(sy, sz, g)
                 remote(src, dst.at[gx], rim_send.at[n], rim_recv.at[n], {"gx": g, **beside(sy, sz)}).start()
         when((sy, sz), 1, send_way)
-    low_x = remote(fine_in.at[pl.ds(0, FH)], xraw.at[pl.ds(FX + FH, FH)],
-                   x_send.at[0], x_recv.at[0], {"gx": lax.max(gx - 1, 0)})
-    high_x = remote(fine_in.at[pl.ds(FX - FH, FH)], xraw.at[pl.ds(0, FH)],
-                    x_send.at[1], x_recv.at[1], {"gx": lax.min(gx + 1, nx - 1)})
-
-    def exchange(copies):
-        def inside(step, sign):
-            at = [(g + sign * s >= 0) & (g + sign * s < n)
-                  for g, s, n in zip((gx, gy, gz), step, sizes) if s != 0]
-            return functools.reduce(jnp.logical_and, at)
-
-        def start():
-            for step, copy in copies:
-                @pl.when(inside(step, 1))
-                def _():
-                    copy.start()
-
-        def wait():
-            for step, copy in copies:
-                @pl.when(inside(step, 1))
-                def _():
-                    copy.wait_send()
-
-                @pl.when(inside(step, -1))
-                def _():
-                    copy.wait_recv()
-        return start, wait
-
-    start_x, wait_x = exchange([((-1, 0, 0), low_x), ((1, 0, 0), high_x)])
-    start_x()
+    loads[3].wait()
+    loads[6].wait()
+
+    def z_edges(first, second):
+        rows = first.shape[0] * FY
+        packed = jnp.concatenate([first.reshape(rows, 256), second.reshape(rows, 256)], axis=1)
+        return mm(packed, perms[EDGE_F:EDGE_F + 512, :])
+
+    edges = z_edges(xraw[4:12], xraw[12:20])
+    for z in range(2):
+        esend[z] = edges[:, 128 * z:128 * z + 128].astype(BF).reshape(8, 64, 128)
+    start_z, wait_z = exchange([
+        ((0, 0, -1), remote(esend.at[0], erecv.at[1], z_send.at[0], z_recv.at[0], beside(0, -1))),
+        ((0, 0, 1), remote(esend.at[1], erecv.at[0], z_send.at[1], z_recv.at[1], beside(0, 1)))])
+    start_z()
 
     @pl.when(gx == 0)
     def _():
@@ -341,7 +358,7 @@
         def _():
             ry[side] = jnp.zeros((4, 16, 256), BF)
             rk[side] = jnp.zeros((2, 4, 16, 128), BF)
-    for copy in loads[3:6]:
+    for copy in loads[4:6]:
         copy.wait()
     for copy in gathers:
         copy.wait()
@@ -407,14 +424,8 @@
             cown[17 * side] = jnp.zeros((16, 256), BF)
             ckrecv[side] = jnp.zeros((2, 16, 128), BF)
 
-    loads[6].wait()
     wait_x()
-    packed = jnp.concatenate([xraw[0:12].reshape(768, 256), xraw[12:24].reshape(768, 256)], axis=1)
-    edges = mm(packed, perms[EDGE_F:EDGE_F + 512, :])
-    for z in range(2):
-        both = edges[:, 128 * z:128 * z + 128].astype(BF).reshape(12, 64, 128)
-        esend[z, 0] = both[:, :32]
-        esend[z, 1] = both[:, 32:]
+    edges = z_edges(xraw[0:12], xraw[12:24])
     for x in range(XX // 2):
         kf[0, 4 * x:4 * x + 4, :] = edges[64 * x:64 * x + 4]
         kf[1, 4 * x:4 * x + 4, :] = edges[64 * x + 60:64 * x + 64]
@@ -427,34 +438,47 @@
         yf[0, 4 * x:4 * x + 4, :] = state[x, 8:12, 0:256]
         yf[1, 4 * x:4 * x + 4, :] = state[x, 68:72, 0:256]
     ysend[...] = yf[...].astype(BF)
-    copies, later = [], []
-    for sy in (-1, 0, 1):
-        y = (sy + 1) // 2
-        for sz in (-1, 0, 1):
-            z = (sz + 1) // 2
-            if sy == 0 and sz == 0:
-                continue
-            pairs = ([(esend.at[z, part], erecv.at[1 - z, part]) for part in range(2)] if sy == 0 else
-                     [(ysend.at[y], yrecv.at[1 - y])] if sz == 0 else
-                     [(ksend.at[y, z], krecv.at[1 - y, 1 - z])])
-            for turn, (src, dst) in enumerate(pairs):
-                n = len(copies) + len(later)
-                (later if turn else copies).append(
-                    ((0, sy, sz), remote(src, dst, f_send.at[n], f_recv.at[n], beside(sy, sz))))
+    copies = []
+    for sy, sz in ways:
+        if sy:
+            y, z = (sy + 1) // 2, (sz + 1) // 2
+            src, dst = ((ysend.at[y], yrecv.at[1 - y]) if sz == 0 else
+                        (ksend.at[y, z], krecv.at[1 - y, 1 - z]))
+            n = len(copies)
+            copies.append(((0, sy, sz), remote(src, dst, f_send.at[n], f_recv.at[n], beside(sy, sz))))
     start_f, wait_f = exchange(copies)
-    start_late, wait_late = exchange(later)
     start_f()
-    start_late()
     for side in range(2):
         @pl.when(gz == side * (nz - 1))
         def _():
-            erecv[side] = jnp.zeros((2, 12, 32, 128), BF)
+            erecv[side] = jnp.zeros((8, 64, 128), BF)
             krecv[:, side] = jnp.zeros((2, 48, 128), BF)
 
         @pl.when(gy == side * (ny - 1))
         def _():
             yrecv[side] = jnp.zeros((96, 256), BF)
             krecv[side] = jnp.zeros((2, 48, 128), BF)
+
+    def rims(from_left, from_right, count):
+        left_lane = iota((count, 128), 1) < 64
+        return (jnp.where(left_lane, from_left, pltpu.roll(from_right, 64, 1)),
+                jnp.where(left_lane, pltpu.roll(from_left, 64, 1), from_right))
+
+    wait_z()
+    early, late = rims(*(erecv[side].reshape(512, 128).astype(F32) for side in range(2)), 512)
+    early, late = early.reshape(8, 64, 128), late.reshape(8, 64, 128)
+    state[4:12, 8:72, 256:384] = early
+    state[12:20, 8:72, 256:384] = late
+    hsend[0] = early[:4].astype(BF)
+    hsend[1] = late[4:].astype(BF)
+    start_h, wait_h = exchange([
+        ((-1, 0, 0), remote(hsend.at[0], hrecv.at[1], h_send.at[0], h_recv.at[0], {"gx": lax.max(gx - 1, 0)})),
+        ((1, 0, 0), remote(hsend.at[1], hrecv.at[0], h_send.at[1], h_recv.at[1], {"gx": lax.min(gx + 1, nx - 1)}))])
+    start_h()
+    for side in range(2):
+        @pl.when(gx == side * (nx - 1))
+        def _():
+            hrecv[side] = jnp.zeros((4, 64, 128), BF)
 
     place_lane = iota((32, 128), 1) // 32
 
@@ -506,18 +530,10 @@
     gi_s[...] = both[:, 256:].reshape(16, 16, 256)
 
     wait_f()
-    wait_late()
-
-    def rims(from_left, from_right, count):
-        left_lane = iota((count, 128), 1) < 64
-        return (jnp.where(left_lane, from_left, pltpu.roll(from_right, 64, 1)),
-                jnp.where(left_lane, pltpu.roll(from_left, 64, 1), from_right))
-
-    for half in range(2):
-        early, late = rims(*(erecv[side, half].reshape(384, 128).astype(F32) for side in range(2)), 384)
-        rows = slice(8 + 32 * half, 40 + 32 * half)
-        state[0:12, rows, 256:384] = early.reshape(12, 32, 128)
-        state[12:24, rows, 256:384] = late.reshape(12, 32, 128)
+    wait_h()
+
+    for side, row in ((0, 0), (1, FX + FH)):
+        state[row:row + 4, 8:72, 256:384] = hrecv[side].astype(F32)
     for y, row in ((0, 4), (1, 72)):
         early, late = rims(krecv[y, 0].astype(F32), krecv[y, 1].astype(F32), 48)
         edge = yrecv[y].astype(F32)
@@ -620,7 +636,7 @@
         vm((3, 2304, 256), BF), vm((2, 3456, 256), BF),
         vm((XX, FY, 256), BF), vm((2, CX, CY, 256), BF), vm((1280, 256), BF),
         vm((XX, YY, 768), BF),
-        vm((2, 2, 12, 32, 128), BF), vm((2, 2, 12, 32, 128), BF),
+        vm((2, 8, 64, 128), BF), vm((2, 8, 64, 128), BF), vm((2, 4, 64, 128), BF), vm((2, 4, 64, 128), BF),
         vm((2, 96, 256), F32), vm((2, 96, 256), BF), vm((2, 96, 256), BF),
         vm((2, 48, 256), F32), vm((2, 2, 48, 128), BF), vm((2, 2, 48, 128), BF),
         vm((2, 4, 4, 16, 256), BF), vm((2, 4, 2, 16, 128), BF), vm((2, 64, 256), F32), vm((2, 4, 16, 256), BF),
@@ -630,7 +646,7 @@
         vm((512, 128), F32), vm((wide - 1, ch, 128), F32), vm((deep, ch, 128), F32),
         vm((ch, 128), F32), vm((ch, 128), BF),
         dma((8,)), dma((nx, 2)), dma((nx, 2)), dma((8,)), dma((8,)), dma((2,)), dma((2,)),
-        dma((8,)), dma((8,)), dma((10,)), dma((10,)),
+        dma((8,)), dma((8,)), dma((6,)), dma((6,)), dma((2,)), dma((2,)), dma((2,)), dma((2,)),
         dma((3,)), dma((3,)),
     ]
     inside = pl.BlockSpec(memory_space=pltpu.VMEM)

time: 46.4 us -> 47.4 us (1.022)
  Pallas kernels: 45.6 us -> 46.7 us
    pallas_call x1, Pallas kernels: 44.4 us -> 45.4 us  [on_device(): pl.pallas_call(functools.partial(kernel, sizes), out_shape=(vm((FX, FY, 2...]
where the time goes in v7:
time: 47.4 us; the launch traced here: 47.3 us
  Pallas kernels  46.7 us (99%)
  between operations  0.64 us (1%)
    pallas_call x1, Pallas kernels, on_device(): pl.pallas_call(functools.partial(kernel, sizes), out_shape=(vm((FX, FY, 2...  45.4 us
    pallas_call x1, Pallas kernels, on_device(): pl.pallas_call(finish, out_shape=(jax.ShapeDtypeStruct((FX, FY, 256), BF)...  1.21 us

profile of v7, /device:TPU:1, one launch (start us, length us, event | category | flops | bytes accessed | tf_op | source)
XLA Modules:
  0.0 47.3 jit_solution(17793298626074963544)
XLA Ops:
  0.6 45.4 %shard_map.93 = (bf16[16,64,256]{2,1,0:T(8,128)(2,1)S(1)}, bf16[16,16,256]{2,1,0:T(8,128)(2,1)S(1)}, bf16[16,16,256]{2,1,0:T(8,128)(2,1)S(1)}, bf16[512,128]{1,0:T(8,128)(2,1)S(1)}) custom-call(bf16[16,64,256]{2,1,0:T(8,128)(2,1)} %fine_in.1, bf16[864,8]{1,0:T(8,128)(2,1)} %bitcast.10, bf16[4,4,16,256]{3,2,1,0:T(8,128)(2,1)} %c_out.1, ...), custom_call_target="tpu_custom_call" | custom-call | tf_op jit(solution)/shard_map/pallas_call | solution.py:655
  46.1 1.2 %shard_map.94 = (bf16[16,64,256]{2,1,0:T(8,128)(2,1)}, bf16[1,16,16,256]{3,2,1,0:T(8,128)(2,1)}, bf16[1,16,16,256]{3,2,1,0:T(8,128)(2,1)}, f32[54,32,32]{2,1,0:T(8,128)}) custom-call(bf16[16,64,256]{2,1,0:T(8,128)(2,1)S(1)} %get-tuple-element.12.fo_s, bf16[16,16,256]{2,1,0:T(8,128)(2,1)S(1)} %get-tuple-element.13.rb_s, ...), custom_call_target="tpu_custom_call" | custom-call | tf_op jit(solution)/shard_map/pallas_call | solution.py:664

commit v8 on v7

--- a/solution.py
+++ b/solution.py
@@ -171,10 +171,11 @@
            fo_s, rb_s, gi_s, final,
            state, last_band, u_last,
            wf, wc, t_fine, t_fwd, t_nat, bands_f, bands_c,
-           xraw, craw, perms, u_fine, esend, erecv, hsend, hrecv, yf, ysend, yrecv, kf, ksend, krecv,
+           xraw, craw, perms, u_fine, esend, erecv, passing, hsend, hrecv, yf, ysend, yrecv, kf, ksend, krecv,
            local, plz, plyf, ply, rz, ry, rk, ystage, cown, cpack, crecv, ckrecv, cspread,
-           part, r1, r2, red, red_bf,
+           part, part_bf, r1, r2, red, red_bf,
            load_sem, in_send, in_recv, rim_send, rim_recv, x_send, x_recv, c_send, c_recv, f_send, f_recv, z_send, z_recv, h_send, h_recv,
+           pass_send, pass_recv, hand_send, hand_recv,
            sum_send, sum_recv):
     nx, ny, nz = sizes
     gx, gy, gz = lax.axis_index("gx"), lax.axis_index("gy"), lax.axis_index("gz")
@@ -193,6 +194,13 @@
 
     def peer_x(d):
         return {"gx": lax.rem(gx + d, nx)}
+
+    zc = lax.rem(gz, 2) * 2 + gx // 2
+
+    def along_z(step, dy):
+        at = lax.rem(zc + step + 4, 4)
+        row = lax.rem(gz // 2 + dy + ky, ky)
+        return {"gx": lax.rem(at, 2) * 2 + lax.rem(gx, 2), "gz": row * 2 + at // 2}
 
     barrier = pltpu.get_barrier_semaphore()
     for d in range(1, wide):
@@ -205,6 +213,10 @@
                 for g in range(nx):
                     to = {"gx": g, "gy": lax.rem(gy + sy + ny, ny), "gz": lax.rem(gz + sz + nz, nz)}
                     pl.semaphore_signal(barrier, inc=1, device_id=to, device_id_type=MESH)
+
+    for step in (-1, 1):
+        for dy in (-1, 0, 1):
+            pl.semaphore_signal(barrier, inc=1, device_id=along_z(step, dy), device_id_type=MESH)
 
     loads = [
         (c_out, local.at[0]),
@@ -222,7 +234,7 @@
     state[:, 0:8, :] = jnp.zeros((XX, 8, 384), F32)
     state[:, 72:80, :] = jnp.zeros((XX, 8, 384), F32)
     part[14 * 32:, :] = jnp.zeros((64, 128), F32)
-    pl.semaphore_wait(barrier, wide - 1 + deep - 1 + 8 * nx)
+    pl.semaphore_wait(barrier, wide - 1 + deep - 1 + 8 * nx + 6)
 
     def remote(src, dst, send, recv, to):
         return pltpu.make_async_remote_copy(
@@ -324,10 +336,42 @@
 
     edges = z_edges(xraw[4:12], xraw[12:20])
     for z in range(2):
-        esend[z] = edges[:, 128 * z:128 * z + 128].astype(BF).reshape(8, 64, 128)
+        both = edges[:, 128 * z:128 * z + 128].astype(BF).reshape(8, 64, 128)
+        esend[z, 0] = both[:, :32]
+        esend[z, 1] = both[:, 32:]
     start_z, wait_z = exchange([
-        ((0, 0, -1), remote(esend.at[0], erecv.at[1], z_send.at[0], z_recv.at[0], beside(0, -1))),
-        ((0, 0, 1), remote(esend.at[1], erecv.at[0], z_send.at[1], z_recv.at[1], beside(0, 1)))])
+        ((0, 0, -1), remote(esend.at[0, 0], erecv.at[1, 0], z_send.at[0], z_recv.at[0], beside(0, -1))),
+        ((0, 0, 1), remote(esend.at[1, 0], erecv.at[0, 0], z_send.at[1], z_recv.at[1], beside(0, 1)))])
+    above = lax.rem(zc + 1, 4)
+    gz_above = gz // 2 * 2 + above // 2
+    to_relay, handed = [], []
+    for z in range(2):
+        to_relay.append(remote(esend.at[z, 1], passing.at[z], pass_send.at[z], pass_recv.at[z], along_z(-1, 0)))
+        target = {"gx": lax.rem(above, 2) * 2 + lax.rem(gx, 2),
+                  "gz": lax.clamp(0, gz_above + 2 * z - 1, nz - 1)}
+        handed.append(remote(passing.at[z], erecv.at[1 - z, 1], hand_send.at[z], hand_recv.at[z], target))
+
+    def at_side(z, index, act):
+        @pl.when(index != (nz - 1) * z)
+        def _():
+            act()
+
+    def start_relay():
+        for z in range(2):
+            at_side(z, gz, to_relay[z].start)
+
+    def hand_on():
+        for z in range(2):
+            at_side(z, gz_above, to_relay[z].wait_recv)
+            at_side(z, gz_above, handed[z].start)
+
+    def wait_handed():
+        for z in range(2):
+            at_side(z, gz, to_relay[z].wait_send)
+            at_side(z, gz_above, handed[z].wait_send)
+            at_side(1 - z, gz, handed[z].wait_recv)
+
+    start_relay()
     start_z()
 
     @pl.when(gx == 0)
@@ -362,6 +406,7 @@
         copy.wait()
     for copy in gathers:
         copy.wait()
+    hand_on()
     for n, (sy, sz) in enumerate(ways):
         got = rim_refs(sy, sz, 0)[1]
         when((sy, sz), 1, functools.partial(wait_all, got, rim_send.at[n]))
@@ -451,7 +496,7 @@
     for side in range(2):
         @pl.when(gz == side * (nz - 1))
         def _():
-            erecv[side] = jnp.zeros((8, 64, 128), BF)
+            erecv[side] = jnp.zeros((2, 8, 32, 128), BF)
             krecv[:, side] = jnp.zeros((2, 48, 128), BF)
 
         @pl.when(gy == side * (ny - 1))
@@ -465,12 +510,14 @@
                 jnp.where(left_lane, pltpu.roll(from_left, 64, 1), from_right))
 
     wait_z()
-    early, late = rims(*(erecv[side].reshape(512, 128).astype(F32) for side in range(2)), 512)
-    early, late = early.reshape(8, 64, 128), late.reshape(8, 64, 128)
-    state[4:12, 8:72, 256:384] = early
-    state[12:20, 8:72, 256:384] = late
-    hsend[0] = early[:4].astype(BF)
-    hsend[1] = late[4:].astype(BF)
+    wait_handed()
+    for half in range(2):
+        early, late = rims(*(erecv[side, half].reshape(256, 128).astype(F32) for side in range(2)), 256)
+        early, late = early.reshape(8, 32, 128), late.reshape(8, 32, 128)
+        state[4:12, 8 + 32 * half:40 + 32 * half, 256:384] = early
+        state[12:20, 8 + 32 * half:40 + 32 * half, 256:384] = late
+        hsend[0, :, 32 * half:32 * half + 32] = early[:4].astype(BF)
+        hsend[1, :, 32 * half:32 * half + 32] = late[4:].astype(BF)
     start_h, wait_h = exchange([
         ((-1, 0, 0), remote(hsend.at[0], hrecv.at[1], h_send.at[0], h_recv.at[0], {"gx": lax.max(gx - 1, 0)})),
         ((1, 0, 0), remote(hsend.at[1], hrecv.at[0], h_send.at[1], h_recv.at[1], {"gx": lax.min(gx + 1, nx - 1)}))])
@@ -518,9 +565,10 @@
     ch = 512 // wide
     mine = pl.ds(pl.multiple_of(me_wide * ch, 8), ch)
 
+    part_bf[...] = part[...].astype(BF)
     for d in range(1, wide):
         theirs = pl.ds(pl.multiple_of(lax.rem(me_wide + d, wide) * ch, 8), ch)
-        remote(part.at[theirs], r1.at[d - 1], sum_send.at[0], sum_recv.at[0], peer_wide(d)).start()
+        remote(part_bf.at[theirs], r1.at[d - 1], sum_send.at[0], sum_recv.at[0], peer_wide(d)).start()
 
     result = conv_pair(1)
     last = jnp.where(low_half, outs - result, cots + silu_grad(middle) * result)
@@ -568,18 +616,18 @@
     wait_all(r1, sum_send.at[0], sum_recv.at[0])
     total = part[mine, :]
     for d in range(wide - 1):
-        total = total + r1[d]
-    red[...] = total
-    r2[me_deep] = total
+        total = total + r1[d].astype(F32)
+    red[...] = total.astype(BF)
+    r2[me_deep] = total.astype(BF)
     for d in range(1, deep):
         remote(red, r2.at[me_deep], sum_send.at[1], sum_recv.at[1], peer_deep(d)).start()
 
     fine_conv(1, 128, 1)
 
     wait_all(r2.at[pl.ds(0, deep - 1)], sum_send.at[1], sum_recv.at[1])
-    total = r2[0]
+    total = r2[0].astype(F32)
     for i in range(1, deep):
-        total = total + r2[i]
+        total = total + r2[i].astype(F32)
     red_bf[...] = total.astype(BF)
     final[mine, :] = total.astype(BF)
     for d in range(1, wide):
@@ -636,17 +684,18 @@
         vm((3, 2304, 256), BF), vm((2, 3456, 256), BF),
         vm((XX, FY, 256), BF), vm((2, CX, CY, 256), BF), vm((1280, 256), BF),
         vm((XX, YY, 768), BF),
-        vm((2, 8, 64, 128), BF), vm((2, 8, 64, 128), BF), vm((2, 4, 64, 128), BF), vm((2, 4, 64, 128), BF),
+        vm((2, 2, 8, 32, 128), BF), vm((2, 2, 8, 32, 128), BF), vm((2, 8, 32, 128), BF), vm((2, 4, 64, 128), BF), vm((2, 4, 64, 128), BF),
         vm((2, 96, 256), F32), vm((2, 96, 256), BF), vm((2, 96, 256), BF),
         vm((2, 48, 256), F32), vm((2, 2, 48, 128), BF), vm((2, 2, 48, 128), BF),
         vm((2, 4, 4, 16, 256), BF), vm((2, 4, 2, 16, 128), BF), vm((2, 64, 256), F32), vm((2, 4, 16, 256), BF),
         vm((2, 4, 2, 16, 128), BF), vm((2, 4, 16, 256), BF), vm((2, 2, 4, 16, 128), BF), vm((2, 16, 384), F32),
         vm((18, 16, 256), BF), vm((2, 128, 128), BF), vm((2, 128, 128), BF), vm((2, 2, 16, 128), BF),
         vm((2, 288, 1152), BF),
-        vm((512, 128), F32), vm((wide - 1, ch, 128), F32), vm((deep, ch, 128), F32),
-        vm((ch, 128), F32), vm((ch, 128), BF),
+        vm((512, 128), F32), vm((512, 128), BF), vm((wide - 1, ch, 128), BF), vm((deep, ch, 128), BF),
+        vm((ch, 128), BF), vm((ch, 128), BF),
         dma((8,)), dma((nx, 2)), dma((nx, 2)), dma((8,)), dma((8,)), dma((2,)), dma((2,)),
         dma((8,)), dma((8,)), dma((6,)), dma((6,)), dma((2,)), dma((2,)), dma((2,)), dma((2,)),
+        dma((2,)), dma((2,)), dma((2,)), dma((2,)),
         dma((3,)), dma((3,)),
     ]
     inside = pl.BlockSpec(memory_space=pltpu.VMEM)

time: 47.4 us -> 47.8 us (level)
  no operation moved by 1% of the time
where the time goes in v8:
time: 47.8 us; the launch traced here: 47.7 us
  Pallas kernels  47.1 us (99%)
  between operations  0.64 us (1%)
    pallas_call x1, Pallas kernels, on_device(): pl.pallas_call(functools.partial(kernel, sizes), out_shape=(vm((FX, FY, 2...  45.9 us
    pallas_call x1, Pallas kernels, on_device(): pl.pallas_call(finish, out_shape=(jax.ShapeDtypeStruct((FX, FY, 256), BF)...  1.21 us

profile of v8, /device:TPU:1, one launch (start us, length us, event | category | flops | bytes accessed | tf_op | source)
XLA Modules:
  0.0 47.7 jit_solution(12326127928670772120)
XLA Ops:
  0.6 45.9 %shard_map.93 = (bf16[16,64,256]{2,1,0:T(8,128)(2,1)S(1)}, bf16[16,16,256]{2,1,0:T(8,128)(2,1)S(1)}, bf16[16,16,256]{2,1,0:T(8,128)(2,1)S(1)}, bf16[512,128]{1,0:T(8,128)(2,1)S(1)}) custom-call(bf16[16,64,256]{2,1,0:T(8,128)(2,1)} %fine_in.1, bf16[864,8]{1,0:T(8,128)(2,1)} %bitcast.10, bf16[4,4,16,256]{3,2,1,0:T(8,128)(2,1)} %c_out.1, ...), custom_call_target="tpu_custom_call" | custom-call | tf_op jit(solution)/shard_map/pallas_call | solution.py:704
  46.5 1.2 %shard_map.94 = (bf16[16,64,256]{2,1,0:T(8,128)(2,1)}, bf16[1,16,16,256]{3,2,1,0:T(8,128)(2,1)}, bf16[1,16,16,256]{3,2,1,0:T(8,128)(2,1)}, f32[54,32,32]{2,1,0:T(8,128)}) custom-call(bf16[16,64,256]{2,1,0:T(8,128)(2,1)S(1)} %get-tuple-element.12.fo_s, bf16[16,16,256]{2,1,0:T(8,128)(2,1)S(1)} %get-tuple-element.13.rb_s, ...), custom_call_target="tpu_custom_call" | custom-call | tf_op jit(solution)/shard_map/pallas_call | solution.py:713

commit v9 on v6

--- a/solution.py
+++ b/solution.py
@@ -183,27 +183,23 @@
     me_wide = gy * ky + gz // 2
     me_deep = gx * 2 + lax.rem(gz, 2)
 
-    def peer_wide(d):
-        p = lax.rem(me_wide + d, wide)
-        return {"gy": p // ky, "gz": lax.rem(p, ky) * 2 + lax.rem(gz, 2)}
-
-    def peer_deep(d):
-        p = lax.rem(me_deep + d, deep)
-        return {"gx": p // 2, "gz": gz // 2 * 2 + lax.rem(p, 2)}
-
-    def peer_x(d):
-        return {"gx": lax.rem(gx + d, nx)}
-
+    gxs = [gx] + [lax.rem(gx + d, nx) for d in range(1, nx)]
+    gys = [gy] + [lax.rem(gy + d, ny) for d in range(1, ny)]
+    ks = [gz // 2] + [lax.rem(gz // 2 + d, ky) for d in range(1, ky)]
+    zs = [lax.rem(gz, 2), 1 - lax.rem(gz, 2)]
+    wide_peers = [(gys[a] * ky + ks[b], {"gy": gys[a], "gz": ks[b] * 2 + zs[0]})
+                  for a in range(ny) for b in range(ky) if a or b]
+    deep_peers = [{"gx": gxs[a], "gz": ks[0] * 2 + zs[b]} for a in range(nx) for b in range(2) if a or b]
+
+    gzs = [gz, lax.rem(gz + 1, nz), lax.rem(gz + nz - 1, nz)]
     barrier = pltpu.get_barrier_semaphore()
-    for d in range(1, wide):
-        pl.semaphore_signal(barrier, inc=1, device_id=peer_wide(d), device_id_type=MESH)
-    for d in range(1, deep):
-        pl.semaphore_signal(barrier, inc=1, device_id=peer_deep(d), device_id_type=MESH)
+    for to in [peer for _, peer in wide_peers] + deep_peers:
+        pl.semaphore_signal(barrier, inc=1, device_id=to, device_id_type=MESH)
     for sy in (-1, 0, 1):
         for sz in (-1, 0, 1):
             if sy or sz:
                 for g in range(nx):
-                    to = {"gx": g, "gy": lax.rem(gy + sy + ny, ny), "gz": lax.rem(gz + sz + nz, nz)}
+                    to = {"gx": g, "gy": gys[sy], "gz": gzs[sz]}
                     pl.semaphore_signal(barrier, inc=1, device_id=to, device_id_type=MESH)
 
     loads = [
@@ -249,10 +245,10 @@
 
     gathers = []
     for d in range(1, nx):
-        to = lax.rem(gx + d, nx)
+        to = gxs[d]
         for i, src in enumerate((c_out, c_cot)):
             gathers.append(remote(src.at[to], craw.at[i, pl.ds(gx * 4, 4)],
-                                  in_send.at[d, i], in_recv.at[d, i], peer_x(d)))
+                                  in_send.at[d, i], in_recv.at[d, i], {"gx": to}))
     for copy in gathers:
         copy.start()
 
@@ -264,7 +260,7 @@
             act()
 
     def beside(sy, sz):
-        return {"gy": lax.clamp(0, gy + sy, ny - 1), "gz": lax.clamp(0, gz + sz, nz - 1)}
+        return {"gy": gys[sy], "gz": gzs[sz]}
 
     ways = [(sy, sz) for sy in (-1, 0, 1) for sz in (-1, 0, 1) if sy or sz]
 
@@ -459,9 +455,10 @@
     place_lane = iota((32, 128), 1) // 32
 
     def fold(stage, pair):
-        columns = jnp.transpose(pair)
-        turned_cot = jnp.concatenate(
-            [columns[64 * z + 32 * (1 - stage):64 * z + 32 * (2 - stage)] for z in range(4)], axis=0).astype(BF)
+        at = iota((128, 256), 0)
+        pick = (at // 32 * 64 + at % 32 + 32 * (1 - stage) == iota((128, 256), 1)).astype(F32).astype(BF)
+        turned_cot = lax.dot_general(pick, pair.astype(BF), (((1,), (1,)), ((), ())),
+                                     preferred_element_type=F32).astype(BF)
         blocks = [mm(turned_cot, cspread[stage, 16 * p:16 * p + 256, :]) for p in range(3)]
         for q in range(3):
             for p in range(3):
@@ -494,9 +491,9 @@
     ch = 512 // wide
     mine = pl.ds(pl.multiple_of(me_wide * ch, 8), ch)
 
-    for d in range(1, wide):
-        theirs = pl.ds(pl.multiple_of(lax.rem(me_wide + d, wide) * ch, 8), ch)
-        remote(part.at[theirs], r1.at[d - 1], sum_send.at[0], sum_recv.at[0], peer_wide(d)).start()
+    for n, (index, to) in enumerate(wide_peers):
+        theirs = pl.ds(pl.multiple_of(index * ch, 8), ch)
+        remote(part.at[theirs], r1.at[n], sum_send.at[0], sum_recv.at[0], to).start()
 
     result = conv_pair(1)
     last = jnp.where(low_half, outs - result, cots + silu_grad(middle) * result)
@@ -529,14 +526,24 @@
 
     limits = fine_limits(sizes)
 
+    def over_x(step, act):
+        count = XX - 2 * step
+
+        def body(i, carry):
+            for j in range(4):
+                act(step + 4 * i + j)
+            return carry
+        lax.fori_loop(0, count // 4, body, 0)
+        for j in range(count % 4):
+            act(step + count // 4 * 4 + j)
+
     def fine_conv(step, column, conv):
-        def spread(x, carry):
+        def spread(x):
             v = fine_input(state, x, column, limits)
             u_fine[x, :, 0:256] = pltpu.roll(v, 1, 0).astype(BF)
             u_fine[x, :, 256:512] = v.astype(BF)
             u_fine[x, :, 512:768] = pltpu.roll(v, YY - 1, 0).astype(BF)
-            return carry
-        lax.fori_loop(step, XX - step, spread, 0)
+        over_x(step, spread)
         half = (XX - 2 * step - 2) // 2
         into = 128 - column
         for part_index in range(2):
@@ -555,8 +562,8 @@
         total = total + r1[d]
     red[...] = total
     r2[me_deep] = total
-    for d in range(1, deep):
-        remote(red, r2.at[me_deep], sum_send.at[1], sum_recv.at[1], peer_deep(d)).start()
+    for to in deep_peers:
+        remote(red, r2.at[me_deep], sum_send.at[1], sum_recv.at[1], to).start()
 
     fine_conv(1, 128, 1)
 
@@ -566,18 +573,17 @@
         total = total + r2[i]
     red_bf[...] = total.astype(BF)
     final[mine, :] = total.astype(BF)
-    for d in range(1, wide):
-        remote(red_bf, final.at[mine], sum_send.at[2], sum_recv.at[2], peer_wide(d)).start()
+    for _, to in wide_peers:
+        remote(red_bf, final.at[mine], sum_send.at[2], sum_recv.at[2], to).start()
 
     fine_conv(2, 0, 2)
 
-    def spread_last(x, carry):
+    def spread_last(x):
         v = fine_input(state, x, 128, limits)
         u_last[x, :, 0:256] = pltpu.roll(v, 1, 0)[8:72].astype(BF)
         u_last[x, :, 256:512] = v[8:72].astype(BF)
         u_last[x, :, 512:768] = pltpu.roll(v, YY - 1, 0)[8:72].astype(BF)
-        return carry
-    lax.fori_loop(3, XX - 3, spread_last, 0)
+    over_x(3, spread_last)
     for c in range(2):
         x0 = 3 + 8 * c
         lhs = jnp.concatenate(

time: 46.4 us -> 46.1 us (level)
  no operation moved by 1% of the time
where the time goes in v9:
time: 46.1 us; the launch traced here: 46 us
  Pallas kernels  45.4 us (98%)
  between operations  0.64 us (1%)
    pallas_call x1, Pallas kernels, on_device(): pl.pallas_call(functools.partial(kernel, sizes), out_shape=(vm((FX, FY, 2...  44.2 us
    pallas_call x1, Pallas kernels, on_device(): pl.pallas_call(finish, out_shape=(jax.ShapeDtypeStruct((FX, FY, 256), BF)...  1.21 us

profile of v9, /device:TPU:1, one launch (start us, length us, event | category | flops | bytes accessed | tf_op | source)
XLA Modules:
  0.0 46.0 jit_solution(10684717439921331201)
XLA Ops:
  0.6 44.2 %shard_map.93 = (bf16[16,64,256]{2,1,0:T(8,128)(2,1)S(1)}, bf16[16,16,256]{2,1,0:T(8,128)(2,1)S(1)}, bf16[16,16,256]{2,1,0:T(8,128)(2,1)S(1)}, bf16[512,128]{1,0:T(8,128)(2,1)S(1)}) custom-call(bf16[16,64,256]{2,1,0:T(8,128)(2,1)} %fine_in.1, bf16[864,8]{1,0:T(8,128)(2,1)} %bitcast.10, bf16[4,4,16,256]{3,2,1,0:T(8,128)(2,1)} %c_out.1, ...), custom_call_target="tpu_custom_call" | custom-call | tf_op jit(solution)/shard_map/pallas_call | solution.py:645
  44.8 1.2 %shard_map.94 = (bf16[16,64,256]{2,1,0:T(8,128)(2,1)}, bf16[1,16,16,256]{3,2,1,0:T(8,128)(2,1)}, bf16[1,16,16,256]{3,2,1,0:T(8,128)(2,1)}, f32[54,32,32]{2,1,0:T(8,128)}) custom-call(bf16[16,64,256]{2,1,0:T(8,128)(2,1)S(1)} %get-tuple-element.12.fo_s, bf16[16,16,256]{2,1,0:T(8,128)(2,1)S(1)} %get-tuple-element.13.rb_s, ...), custom_call_target="tpu_custom_call" | custom-call | tf_op jit(solution)/shard_map/pallas_call | solution.py:654

commit v10 on v7

--- a/solution.py
+++ b/solution.py
@@ -183,27 +183,23 @@
     me_wide = gy * ky + gz // 2
     me_deep = gx * 2 + lax.rem(gz, 2)
 
-    def peer_wide(d):
-        p = lax.rem(me_wide + d, wide)
-        return {"gy": p // ky, "gz": lax.rem(p, ky) * 2 + lax.rem(gz, 2)}
-
-    def peer_deep(d):
-        p = lax.rem(me_deep + d, deep)
-        return {"gx": p // 2, "gz": gz // 2 * 2 + lax.rem(p, 2)}
-
-    def peer_x(d):
-        return {"gx": lax.rem(gx + d, nx)}
-
+    gxs = [gx] + [lax.rem(gx + d, nx) for d in range(1, nx)]
+    gys = [gy] + [lax.rem(gy + d, ny) for d in range(1, ny)]
+    ks = [gz // 2] + [lax.rem(gz // 2 + d, ky) for d in range(1, ky)]
+    zs = [lax.rem(gz, 2), 1 - lax.rem(gz, 2)]
+    wide_peers = [(gys[a] * ky + ks[b], {"gy": gys[a], "gz": ks[b] * 2 + zs[0]})
+                  for a in range(ny) for b in range(ky) if a or b]
+    deep_peers = [{"gx": gxs[a], "gz": ks[0] * 2 + zs[b]} for a in range(nx) for b in range(2) if a or b]
+
+    gzs = [gz, lax.rem(gz + 1, nz), lax.rem(gz + nz - 1, nz)]
     barrier = pltpu.get_barrier_semaphore()
-    for d in range(1, wide):
-        pl.semaphore_signal(barrier, inc=1, device_id=peer_wide(d), device_id_type=MESH)
-    for d in range(1, deep):
-        pl.semaphore_signal(barrier, inc=1, device_id=peer_deep(d), device_id_type=MESH)
+    for to in [peer for _, peer in wide_peers] + deep_peers:
+        pl.semaphore_signal(barrier, inc=1, device_id=to, device_id_type=MESH)
     for sy in (-1, 0, 1):
         for sz in (-1, 0, 1):
             if sy or sz:
                 for g in range(nx):
-                    to = {"gx": g, "gy": lax.rem(gy + sy + ny, ny), "gz": lax.rem(gz + sz + nz, nz)}
+                    to = {"gx": g, "gy": gys[sy], "gz": gzs[sz]}
                     pl.semaphore_signal(barrier, inc=1, device_id=to, device_id_type=MESH)
 
     loads = [
@@ -231,10 +227,10 @@
 
     gathers = []
     for d in range(1, nx):
-        to = lax.rem(gx + d, nx)
+        to = gxs[d]
         for i, src in enumerate((c_out, c_cot)):
             gathers.append(remote(src.at[to], craw.at[i, pl.ds(gx * 4, 4)],
-                                  in_send.at[d, i], in_recv.at[d, i], peer_x(d)))
+                                  in_send.at[d, i], in_recv.at[d, i], {"gx": to}))
     for copy in gathers:
         copy.start()
 
@@ -296,7 +292,7 @@
             act()
 
     def beside(sy, sz):
-        return {"gy": lax.clamp(0, gy + sy, ny - 1), "gz": lax.clamp(0, gz + sz, nz - 1)}
+        return {"gy": gys[sy], "gz": gzs[sz]}
 
     ways = [(sy, sz) for sy in (-1, 0, 1) for sz in (-1, 0, 1) if sy or sz]
 
@@ -341,88 +337,6 @@
     build_coarse, build_fine = band_builders(bands_f, bands_c, last_band, wf, wc, t_fine, t_fwd, t_nat)
     loads[2].wait()
     build_coarse()
-    loads[7].wait()
-    build_fine()
-
-    def wait_all(buffer, *sems):
-        for sem in sems:
-            pltpu.make_async_copy(buffer, buffer, sem).wait()
-
-    for side in range(2):
-        @pl.when(gz == side * (nz - 1))
-        def _():
-            rz[side] = jnp.zeros((4, 2, 16, 128), BF)
-            rk[:, side] = jnp.zeros((2, 4, 16, 128), BF)
-
-        @pl.when(gy == side * (ny - 1))
-        def _():
-            ry[side] = jnp.zeros((4, 16, 256), BF)
-            rk[side] = jnp.zeros((2, 4, 16, 128), BF)
-    for copy in loads[4:6]:
-        copy.wait()
-    for copy in gathers:
-        copy.wait()
-    for n, (sy, sz) in enumerate(ways):
-        got = rim_refs(sy, sz, 0)[1]
-        when((sy, sz), 1, functools.partial(wait_all, got, rim_send.at[n]))
-        when((sy, sz), -1, functools.partial(wait_all, got, rim_recv.at[n]))
-    swap = perms[SWAP:SWAP + 256, :]
-
-    def side_by_side(from_low, from_high):
-        return (jnp.where(rim_left, from_low, pltpu.roll(from_high, 64, 1)),
-                jnp.where(rim_left, pltpu.roll(from_low, 64, 1), from_high))
-
-    first, second = side_by_side(*(rz[side].reshape(128, 128).astype(F32) for side in range(2)))
-    rim = jnp.concatenate([first.reshape(4, 32, 128), second.reshape(4, 32, 128)], axis=1).reshape(256, 128)
-    turned = mm(swap, jnp.concatenate(
-        [craw[0].reshape(256, 256), craw[1].reshape(256, 256), rim.astype(BF)], axis=1))
-    outs, cots, rim = turned[:, :256], turned[:, 256:512], turned[:, 512:]
-    corner_left = iota((16, 128), 1) < 64
-    for y in range(2):
-        for g in range(4):
-            ystage[y, 4 * g:4 * g + 4, 0:256] = ry[y, g].astype(F32)[0:4]
-            corner = jnp.where(corner_left, rk[y, 1, g].astype(F32), rk[y, 0, g].astype(F32))
-            ystage[y, 4 * g:4 * g + 4, 256:384] = pltpu.roll(corner, 64, 1)[0:4]
-
-    def spread_rows(stage, values):
-        row = iota((288, 384), 0) % 16
-        cspread[stage, :, 0:384] = jnp.where(row == 0, 0.0, pltpu.roll(values, 1, 0)).astype(BF)
-        cspread[stage, :, 384:768] = values.astype(BF)
-        cspread[stage, :, 768:1152] = jnp.where(row == 15, 0.0, pltpu.roll(values, 287, 0)).astype(BF)
-
-    def conv_pair(stage):
-        lhs = jnp.concatenate([cspread[stage, 16 * p:16 * p + 256, :] for p in range(3)], axis=1)
-        return mm(lhs, bands_c[stage])
-
-    pair = jnp.where(low_half, silu(outs), cots)
-    spread_rows(0, jnp.concatenate(
-        [ystage[0], jnp.concatenate([pair, rim], axis=1), ystage[1]], axis=0))
-    result = conv_pair(0)
-    middle = jnp.where(low_half, cots + silu_grad(outs) * result, outs - result)
-    inner = jnp.where(low_half, middle, silu(middle))
-    cown[1:17] = inner.astype(BF).reshape(16, 16, 256)
-    early, late = inner[:128], inner[128:]
-    cpack[0] = jnp.where(rim_left, early[:, :128], pltpu.roll(late[:, :128], 64, 1)).astype(BF)
-    cpack[1] = jnp.where(rim_left, pltpu.roll(early[:, 128:], 64, 1), late[:, 128:]).astype(BF)
-    copies = []
-    for n, (sy, sz) in enumerate(ways):
-        y, z = (sy + 1) // 2, (sz + 1) // 2
-        src, dst = ((cpack.at[z], crecv.at[1 - z]) if sy == 0 else
-                    (cown.at[1 + 15 * y], cown.at[17 - 17 * y]) if sz == 0 else
-                    (cown.at[1 + 15 * y, :, pl.ds(128 * z, 128)], ckrecv.at[1 - y, 1 - z]))
-        copies.append(((0, sy, sz), remote(src, dst, c_send.at[n], c_recv.at[n], beside(sy, sz))))
-    start_c, wait_c = exchange(copies)
-    start_c()
-    for side in range(2):
-        @pl.when(gz == side * (nz - 1))
-        def _():
-            crecv[side] = jnp.zeros((128, 128), BF)
-            ckrecv[:, side] = jnp.zeros((2, 16, 128), BF)
-
-        @pl.when(gy == side * (ny - 1))
-        def _():
-            cown[17 * side] = jnp.zeros((16, 256), BF)
-            ckrecv[side] = jnp.zeros((2, 16, 128), BF)
 
     wait_x()
     edges = z_edges(xraw[0:12], xraw[12:24])
@@ -459,6 +373,89 @@
             yrecv[side] = jnp.zeros((96, 256), BF)
             krecv[side] = jnp.zeros((2, 48, 128), BF)
 
+    def wait_all(buffer, *sems):
+        for sem in sems:
+            pltpu.make_async_copy(buffer, buffer, sem).wait()
+
+    for side in range(2):
+        @pl.when(gz == side * (nz - 1))
+        def _():
+            rz[side] = jnp.zeros((4, 2, 16, 128), BF)
+            rk[:, side] = jnp.zeros((2, 4, 16, 128), BF)
+
+        @pl.when(gy == side * (ny - 1))
+        def _():
+            ry[side] = jnp.zeros((4, 16, 256), BF)
+            rk[side] = jnp.zeros((2, 4, 16, 128), BF)
+    for copy in loads[4:6]:
+        copy.wait()
+    for copy in gathers:
+        copy.wait()
+    for n, (sy, sz) in enumerate(ways):
+        got = rim_refs(sy, sz, 0)[1]
+        when((sy, sz), 1, functools.partial(wait_all, got, rim_send.at[n]))
+        when((sy, sz), -1, functools.partial(wait_all, got, rim_recv.at[n]))
+    swap = perms[SWAP:SWAP + 256, :]
+
+    def side_by_side(from_low, from_high):
+        return (jnp.where(rim_left, from_low, pltpu.roll(from_high, 64, 1)),
+                jnp.where(rim_left, pltpu.roll(from_low, 64, 1), from_high))
+
+    first, second = side_by_side(*(rz[side].reshape(128, 128).astype(F32) for side in range(2)))
+    rim = jnp.concatenate([first.reshape(4, 32, 128), second.reshape(4, 32, 128)], axis=1).reshape(256, 128)
+    turned = mm(swap, jnp.concatenate(
+        [craw[0].reshape(256, 256), craw[1].reshape(256, 256), rim.astype(BF)], axis=1))
+    outs, cots, rim = turned[:, :256], turned[:, 256:512], turned[:, 512:]
+    corner_left = iota((16, 128), 1) < 64
+    for y in range(2):
+        for g in range(4):
+            ystage[y, 4 * g:4 * g + 4, 0:256] = ry[y, g].astype(F32)[0:4]
+            corner = jnp.where(corner_left, rk[y, 1, g].astype(F32), rk[y, 0, g].astype(F32))
+            ystage[y, 4 * g:4 * g + 4, 256:384] = pltpu.roll(corner, 64, 1)[0:4]
+
+    def spread_rows(stage, values):
+        row = iota((288, 384), 0) % 16
+        cspread[stage, :, 0:384] = jnp.where(row == 0, 0.0, pltpu.roll(values, 1, 0)).astype(BF)
+        cspread[stage, :, 384:768] = values.astype(BF)
+        cspread[stage, :, 768:1152] = jnp.where(row == 15, 0.0, pltpu.roll(values, 287, 0)).astype(BF)
+
+    def conv_pair(stage):
+        lhs = jnp.concatenate([cspread[stage, 16 * p:16 * p + 256, :] for p in range(3)], axis=1)
+        return mm(lhs, bands_c[stage])
+
+    pair = jnp.where(low_half, silu(outs), cots)
+    spread_rows(0, jnp.concatenate(
+        [ystage[0], jnp.concatenate([pair, rim], axis=1), ystage[1]], axis=0))
+    result = conv_pair(0)
+    middle = jnp.where(low_half, cots + silu_grad(outs) * result, outs - result)
+    inner = jnp.where(low_half, middle, silu(middle))
+    cown[1:17] = inner.astype(BF).reshape(16, 16, 256)
+    early, late = inner[:128], inner[128:]
+    cpack[0] = jnp.where(rim_left, early[:, :128], pltpu.roll(late[:, :128], 64, 1)).astype(BF)
+    cpack[1] = jnp.where(rim_left, pltpu.roll(early[:, 128:], 64, 1), late[:, 128:]).astype(BF)
+    copies = []
+    for n, (sy, sz) in enumerate(ways):
+        y, z = (sy + 1) // 2, (sz + 1) // 2
+        src, dst = ((cpack.at[z], crecv.at[1 - z]) if sy == 0 else
+                    (cown.at[1 + 15 * y], cown.at[17 - 17 * y]) if sz == 0 else
+                    (cown.at[1 + 15 * y, :, pl.ds(128 * z, 128)], ckrecv.at[1 - y, 1 - z]))
+        copies.append(((0, sy, sz), remote(src, dst, c_send.at[n], c_recv.at[n], beside(sy, sz))))
+    start_c, wait_c = exchange(copies)
+    start_c()
+    for side in range(2):
+        @pl.when(gz == side * (nz - 1))
+        def _():
+            crecv[side] = jnp.zeros((128, 128), BF)
+            ckrecv[:, side] = jnp.zeros((2, 16, 128), BF)
+
+        @pl.when(gy == side * (ny - 1))
+        def _():
+            cown[17 * side] = jnp.zeros((16, 256), BF)
+            ckrecv[side] = jnp.zeros((2, 16, 128), BF)
+
+    loads[7].wait()
+    build_fine()
+
     def rims(from_left, from_right, count):
         left_lane = iota((count, 128), 1) < 64
         return (jnp.where(left_lane, from_left, pltpu.roll(from_right, 64, 1)),
@@ -483,9 +480,10 @@
     place_lane = iota((32, 128), 1) // 32
 
     def fold(stage, pair):
-        columns = jnp.transpose(pair)
-        turned_cot = jnp.concatenate(
-            [columns[64 * z + 32 * (1 - stage):64 * z + 32 * (2 - stage)] for z in range(4)], axis=0).astype(BF)
+        at = iota((128, 256), 0)
+        pick = (at // 32 * 64 + at % 32 + 32 * (1 - stage) == iota((128, 256), 1)).astype(F32).astype(BF)
+        turned_cot = lax.dot_general(pick, pair.astype(BF), (((1,), (1,)), ((), ())),
+                                     preferred_element_type=F32).astype(BF)
         blocks = [mm(turned_cot, cspread[stage, 16 * p:16 * p + 256, :]) for p in range(3)]
         for q in range(3):
             for p in range(3):
@@ -518,9 +516,9 @@
     ch = 512 // wide
     mine = pl.ds(pl.multiple_of(me_wide * ch, 8), ch)
 
-    for d in range(1, wide):
-        theirs = pl.ds(pl.multiple_of(lax.rem(me_wide + d, wide) * ch, 8), ch)
-        remote(part.at[theirs], r1.at[d - 1], sum_send.at[0], sum_recv.at[0], peer_wide(d)).start()
+    for n, (index, to) in enumerate(wide_peers):
+        theirs = pl.ds(pl.multiple_of(index * ch, 8), ch)
+        remote(part.at[theirs], r1.at[n], sum_send.at[0], sum_recv.at[0], to).start()
 
     result = conv_pair(1)
     last = jnp.where(low_half, outs - result, cots + silu_grad(middle) * result)
@@ -545,14 +543,24 @@
 
     limits = fine_limits(sizes)
 
+    def over_x(step, act):
+        count = XX - 2 * step
+
+        def body(i, carry):
+            for j in range(4):
+                act(step + 4 * i + j)
+            return carry
+        lax.fori_loop(0, count // 4, body, 0)
+        for j in range(count % 4):
+            act(step + count // 4 * 4 + j)
+
     def fine_conv(step, column, conv):
-        def spread(x, carry):
+        def spread(x):
             v = fine_input(state, x, column, limits)
             u_fine[x, :, 0:256] = pltpu.roll(v, 1, 0).astype(BF)
             u_fine[x, :, 256:512] = v.astype(BF)
             u_fine[x, :, 512:768] = pltpu.roll(v, YY - 1, 0).astype(BF)
-            return carry
-        lax.fori_loop(step, XX - step, spread, 0)
+        over_x(step, spread)
         half = (XX - 2 * step - 2) // 2
         into = 128 - column
         for part_index in range(2):
@@ -571,8 +579,8 @@
         total = total + r1[d]
     red[...] = total
     r2[me_deep] = total
-    for d in range(1, deep):
-        remote(red, r2.at[me_deep], sum_send.at[1], sum_recv.at[1], peer_deep(d)).start()
+    for to in deep_peers:
+        remote(red, r2.at[me_deep], sum_send.at[1], sum_recv.at[1], to).start()
 
     fine_conv(1, 128, 1)
 
@@ -582,18 +590,17 @@
         total = total + r2[i]
     red_bf[...] = total.astype(BF)
     final[mine, :] = total.astype(BF)
-    for d in range(1, wide):
-        remote(red_bf, final.at[mine], sum_send.at[2], sum_recv.at[2], peer_wide(d)).start()
+    for _, to in wide_peers:
+        remote(red_bf, final.at[mine], sum_send.at[2], sum_recv.at[2], to).start()
 
     fine_conv(2, 0, 2)
 
-    def spread_last(x, carry):
+    def spread_last(x):
         v = fine_input(state, x, 128, limits)
         u_last[x, :, 0:256] = pltpu.roll(v, 1, 0)[8:72].astype(BF)
         u_last[x, :, 256:512] = v[8:72].astype(BF)
         u_last[x, :, 512:768] = pltpu.roll(v, YY - 1, 0)[8:72].astype(BF)
-        return carry
-    lax.fori_loop(3, XX - 3, spread_last, 0)
+    over_x(3, spread_last)
     for c in range(2):
         x0 = 3 + 8 * c
         lhs = jnp.concatenate(

time: 47.4 us -> 47.2 us (level)
  no operation moved by 1% of the time
where the time goes in v10:
time: 47.2 us; the launch traced here: 47.1 us
  Pallas kernels  46.5 us (99%)
  between operations  0.64 us (1%)
    pallas_call x1, Pallas kernels, on_device(): pl.pallas_call(functools.partial(kernel, sizes), out_shape=(vm((FX, FY, 2...  45.3 us
    pallas_call x1, Pallas kernels, on_device(): pl.pallas_call(finish, out_shape=(jax.ShapeDtypeStruct((FX, FY, 256), BF)...  1.21 us

profile of v10, /device:TPU:1, one launch (start us, length us, event | category | flops | bytes accessed | tf_op | source)
XLA Modules:
  0.0 47.1 jit_solution(8073999278714105986)
XLA Ops:
  0.6 45.3 %shard_map.93 = (bf16[16,64,256]{2,1,0:T(8,128)(2,1)S(1)}, bf16[16,16,256]{2,1,0:T(8,128)(2,1)S(1)}, bf16[16,16,256]{2,1,0:T(8,128)(2,1)S(1)}, bf16[512,128]{1,0:T(8,128)(2,1)S(1)}) custom-call(bf16[16,64,256]{2,1,0:T(8,128)(2,1)} %fine_in.1, bf16[864,8]{1,0:T(8,128)(2,1)} %bitcast.10, bf16[4,4,16,256]{3,2,1,0:T(8,128)(2,1)} %c_out.1, ...), custom_call_target="tpu_custom_call" | custom-call | tf_op jit(solution)/shard_map/pallas_call | solution.py:662
  45.9 1.2 %shard_map.94 = (bf16[16,64,256]{2,1,0:T(8,128)(2,1)}, bf16[1,16,16,256]{3,2,1,0:T(8,128)(2,1)}, bf16[1,16,16,256]{3,2,1,0:T(8,128)(2,1)}, f32[54,32,32]{2,1,0:T(8,128)}) custom-call(bf16[16,64,256]{2,1,0:T(8,128)(2,1)S(1)} %get-tuple-element.12.fo_s, bf16[16,16,256]{2,1,0:T(8,128)(2,1)S(1)} %get-tuple-element.13.rb_s, ...), custom_call_target="tpu_custom_call" | custom-call | tf_op jit(solution)/shard_map/pallas_call | solution.py:671

commit v11 on v10

--- a/solution.py
+++ b/solution.py
@@ -324,7 +324,6 @@
     start_z, wait_z = exchange([
         ((0, 0, -1), remote(esend.at[0], erecv.at[1], z_send.at[0], z_recv.at[0], beside(0, -1))),
         ((0, 0, 1), remote(esend.at[1], erecv.at[0], z_send.at[1], z_recv.at[1], beside(0, 1)))])
-    start_z()
 
     @pl.when(gx == 0)
     def _():
@@ -361,6 +360,7 @@
             n = len(copies)
             copies.append(((0, sy, sz), remote(src, dst, f_send.at[n], f_recv.at[n], beside(sy, sz))))
     start_f, wait_f = exchange(copies)
+    start_z()
     start_f()
     for side in range(2):
         @pl.when(gz == side * (nz - 1))

time: 47.2 us -> 46.5 us (0.985)
  Pallas kernels: 46.5 us -> 45.7 us
    pallas_call x1, Pallas kernels: 45.3 us -> 44.5 us  [on_device(): pl.pallas_call(functools.partial(kernel, sizes), out_shape=(vm((FX, FY, 2...]
where the time goes in v11:
time: 46.5 us; the launch traced here: 46.4 us
  Pallas kernels  45.7 us (98%)
  between operations  0.64 us (1%)
    pallas_call x1, Pallas kernels, on_device(): pl.pallas_call(functools.partial(kernel, sizes), out_shape=(vm((FX, FY, 2...  44.5 us
    pallas_call x1, Pallas kernels, on_device(): pl.pallas_call(finish, out_shape=(jax.ShapeDtypeStruct((FX, FY, 256), BF)...  1.21 us

profile of v11, /device:TPU:1, one launch (start us, length us, event | category | flops | bytes accessed | tf_op | source)
XLA Modules:
  0.0 46.4 jit_solution(7101392079698021565)
XLA Ops:
  0.6 44.5 %shard_map.93 = (bf16[16,64,256]{2,1,0:T(8,128)(2,1)S(1)}, bf16[16,16,256]{2,1,0:T(8,128)(2,1)S(1)}, bf16[16,16,256]{2,1,0:T(8,128)(2,1)S(1)}, bf16[512,128]{1,0:T(8,128)(2,1)S(1)}) custom-call(bf16[16,64,256]{2,1,0:T(8,128)(2,1)} %fine_in.1, bf16[864,8]{1,0:T(8,128)(2,1)} %bitcast.10, bf16[4,4,16,256]{3,2,1,0:T(8,128)(2,1)} %c_out.1, ...), custom_call_target="tpu_custom_call" | custom-call | tf_op jit(solution)/shard_map/pallas_call | solution.py:662
  45.2 1.2 %shard_map.94 = (bf16[16,64,256]{2,1,0:T(8,128)(2,1)}, bf16[1,16,16,256]{3,2,1,0:T(8,128)(2,1)}, bf16[1,16,16,256]{3,2,1,0:T(8,128)(2,1)}, f32[54,32,32]{2,1,0:T(8,128)}) custom-call(bf16[16,64,256]{2,1,0:T(8,128)(2,1)S(1)} %get-tuple-element.12.fo_s, bf16[16,16,256]{2,1,0:T(8,128)(2,1)S(1)} %get-tuple-element.13.rb_s, ...), custom_call_target="tpu_custom_call" | custom-call | tf_op jit(solution)/shard_map/pallas_call | solution.py:671

commit v12 on v9

--- a/solution.py
+++ b/solution.py
@@ -13,7 +13,7 @@
 F32 = jnp.float32
 
 FX, FY, FZ, FH = 16, 64, 16, 4
-XX, YY = FX + 2 * FH, 80
+XX, YY = FX + 2 * FH, 72
 CX, CY, CZ = 16, 16, 4
 NONE = 99
 
@@ -151,7 +151,7 @@
     nx, ny, nz = sizes
     gx, gy, gz = lax.axis_index("gx"), lax.axis_index("gy"), lax.axis_index("gz")
     return (jnp.where(gx == 0, FH, 0), jnp.where(gx == nx - 1, FX + FH, XX),
-            jnp.where(gy == 0, 8, 4), jnp.where(gy == ny - 1, 72, 76),
+            jnp.where(gy == 0, 4, 0), jnp.where(gy == ny - 1, 68, 72),
             jnp.where(gz == 0, 64, 0), jnp.where(gz == nz - 1, 64, 128))
 
 
@@ -215,8 +215,6 @@
     loads = [pltpu.make_async_copy(s, t, load_sem.at[i]) for i, (s, t) in enumerate(loads)]
     for copy in loads:
         copy.start()
-    state[:, 0:8, :] = jnp.zeros((XX, 8, 384), F32)
-    state[:, 72:80, :] = jnp.zeros((XX, 8, 384), F32)
     part[14 * 32:, :] = jnp.zeros((64, 128), F32)
     plyf[...] = jnp.zeros((2, 64, 256), F32)
     loads[0].wait()
@@ -418,10 +416,10 @@
         for z in range(2):
             ksend[y, z] = kf[y, :, 128 * z:128 * z + 128].astype(BF)
     halves = mm(xraw[...].reshape(XX * FY, 256), perms[SPLIT_F:SPLIT_F + 256, :])
-    state[:, 8:72, 0:256] = halves.reshape(XX, FY, 256)
+    state[:, 4:68, 0:256] = halves.reshape(XX, FY, 256)
     for x in range(XX):
-        yf[0, 4 * x:4 * x + 4, :] = state[x, 8:12, 0:256]
-        yf[1, 4 * x:4 * x + 4, :] = state[x, 68:72, 0:256]
+        yf[0, 4 * x:4 * x + 4, :] = state[x, 4:8, 0:256]
+        yf[1, 4 * x:4 * x + 4, :] = state[x, 64:68, 0:256]
     ysend[...] = yf[...].astype(BF)
     copies, later = [], []
     for sy in (-1, 0, 1):
@@ -512,10 +510,10 @@
 
     for half in range(2):
         early, late = rims(*(erecv[side, half].reshape(384, 128).astype(F32) for side in range(2)), 384)
-        rows = slice(8 + 32 * half, 40 + 32 * half)
+        rows = slice(4 + 32 * half, 36 + 32 * half)
         state[0:12, rows, 256:384] = early.reshape(12, 32, 128)
         state[12:24, rows, 256:384] = late.reshape(12, 32, 128)
-    for y, row in ((0, 4), (1, 72)):
+    for y, row in ((0, 0), (1, 68)):
         early, late = rims(krecv[y, 0].astype(F32), krecv[y, 1].astype(F32), 48)
         edge = yrecv[y].astype(F32)
         for x in range(XX):
@@ -580,16 +578,15 @@
 
     def spread_last(x):
         v = fine_input(state, x, 128, limits)
-        u_last[x, :, 0:256] = pltpu.roll(v, 1, 0)[8:72].astype(BF)
-        u_last[x, :, 256:512] = v[8:72].astype(BF)
-        u_last[x, :, 512:768] = pltpu.roll(v, YY - 1, 0)[8:72].astype(BF)
+        for q in range(3):
+            u_last[x, :, 256 * q:256 * q + 256] = pltpu.roll(v, YY - 3 - q, 0)[0:64].astype(BF)
     over_x(3, spread_last)
     for c in range(2):
         x0 = 3 + 8 * c
         lhs = jnp.concatenate(
             [u_last[x0 + p:x0 + p + 8].reshape(512, 768) for p in range(3)], axis=1)
-        two = mm(lhs, last_band[...]).reshape(8, FY, 128) + state[x0 + 1:x0 + 9, 8:72, 0:128]
-        one = state[x0 + 1:x0 + 9, 8:72, 128:256]
+        two = mm(lhs, last_band[...]).reshape(8, FY, 128) + state[x0 + 1:x0 + 9, 4:68, 0:128]
+        one = state[x0 + 1:x0 + 9, 4:68, 128:256]
         both = jnp.concatenate([two, one], axis=2).astype(BF).reshape(512, 256)
         fo_s[8 * c:8 * c + 8] = mm(both, perms[JOIN_F:JOIN_F + 256, :]).astype(BF).reshape(8, FY, 256)
     wait_all(final.at[pl.ds(0, 512 - ch)], sum_send.at[2], sum_recv.at[2])

time: 46.1 us -> 45.9 us (level)
  no operation moved by 1% of the time
where the time goes in v12:
time: 45.9 us; the launch traced here: 45.8 us
  Pallas kernels  45.1 us (98%)
  between operations  0.64 us (1%)
    pallas_call x1, Pallas kernels, on_device(): pl.pallas_call(functools.partial(kernel, sizes), out_shape=(vm((FX, FY, 2...  43.9 us
    pallas_call x1, Pallas kernels, on_device(): pl.pallas_call(finish, out_shape=(jax.ShapeDtypeStruct((FX, FY, 256), BF)...  1.21 us

profile of v12, /device:TPU:1, one launch (start us, length us, event | category | flops | bytes accessed | tf_op | source)
XLA Modules:
  0.0 45.8 jit_solution(8295300937108926361)
XLA Ops:
  0.6 43.9 %shard_map.93 = (bf16[16,64,256]{2,1,0:T(8,128)(2,1)S(1)}, bf16[16,16,256]{2,1,0:T(8,128)(2,1)S(1)}, bf16[16,16,256]{2,1,0:T(8,128)(2,1)S(1)}, bf16[512,128]{1,0:T(8,128)(2,1)S(1)}) custom-call(bf16[16,64,256]{2,1,0:T(8,128)(2,1)} %fine_in.1, bf16[864,8]{1,0:T(8,128)(2,1)} %bitcast.10, bf16[4,4,16,256]{3,2,1,0:T(8,128)(2,1)} %c_out.1, ...), custom_call_target="tpu_custom_call" | custom-call | tf_op jit(solution)/shard_map/pallas_call | solution.py:642
  44.6 1.2 %shard_map.94 = (bf16[16,64,256]{2,1,0:T(8,128)(2,1)}, bf16[1,16,16,256]{3,2,1,0:T(8,128)(2,1)}, bf16[1,16,16,256]{3,2,1,0:T(8,128)(2,1)}, f32[54,32,32]{2,1,0:T(8,128)}) custom-call(bf16[16,64,256]{2,1,0:T(8,128)(2,1)S(1)} %get-tuple-element.12.fo_s, bf16[16,16,256]{2,1,0:T(8,128)(2,1)S(1)} %get-tuple-element.13.rb_s, ...), custom_call_target="tpu_custom_call" | custom-call | tf_op jit(solution)/shard_map/pallas_call | solution.py:651

commit v13 on v12

--- a/solution.py
+++ b/solution.py
@@ -173,7 +173,7 @@
            wf, wc, t_fine, t_fwd, t_nat, bands_f, bands_c,
            xraw, craw, perms, u_fine, esend, erecv, yf, ysend, yrecv, kf, ksend, krecv,
            local, plz, plyf, ply, rz, ry, rk, ystage, cown, cpack, crecv, ckrecv, cspread,
-           part, r1, r2, red, red_bf,
+           part, part_bf, r1, r2, red, red_bf,
            load_sem, in_send, in_recv, rim_send, rim_recv, x_send, x_recv, c_send, c_recv, f_send, f_recv,
            sum_send, sum_recv):
     nx, ny, nz = sizes
@@ -489,9 +489,10 @@
     ch = 512 // wide
     mine = pl.ds(pl.multiple_of(me_wide * ch, 8), ch)
 
+    part_bf[...] = part[...].astype(BF)
     for n, (index, to) in enumerate(wide_peers):
         theirs = pl.ds(pl.multiple_of(index * ch, 8), ch)
-        remote(part.at[theirs], r1.at[n], sum_send.at[0], sum_recv.at[0], to).start()
+        remote(part_bf.at[theirs], r1.at[n], sum_send.at[0], sum_recv.at[0], to).start()
 
     result = conv_pair(1)
     last = jnp.where(low_half, outs - result, cots + silu_grad(middle) * result)
@@ -557,18 +558,18 @@
     wait_all(r1, sum_send.at[0], sum_recv.at[0])
     total = part[mine, :]
     for d in range(wide - 1):
-        total = total + r1[d]
-    red[...] = total
-    r2[me_deep] = total
+        total = total + r1[d].astype(F32)
+    red[...] = total.astype(BF)
+    r2[me_deep] = total.astype(BF)
     for to in deep_peers:
         remote(red, r2.at[me_deep], sum_send.at[1], sum_recv.at[1], to).start()
 
     fine_conv(1, 128, 1)
 
     wait_all(r2.at[pl.ds(0, deep - 1)], sum_send.at[1], sum_recv.at[1])
-    total = r2[0]
+    total = r2[0].astype(F32)
     for i in range(1, deep):
-        total = total + r2[i]
+        total = total + r2[i].astype(F32)
     red_bf[...] = total.astype(BF)
     final[mine, :] = total.astype(BF)
     for _, to in wide_peers:
@@ -630,8 +631,8 @@
         vm((2, 4, 2, 16, 128), BF), vm((2, 4, 16, 256), BF), vm((2, 2, 4, 16, 128), BF), vm((2, 16, 384), F32),
         vm((18, 16, 256), BF), vm((2, 128, 128), BF), vm((2, 128, 128), BF), vm((2, 2, 16, 128), BF),
         vm((2, 288, 1152), BF),
-        vm((512, 128), F32), vm((wide - 1, ch, 128), F32), vm((deep, ch, 128), F32),
-        vm((ch, 128), F32), vm((ch, 128), BF),
+        vm((512, 128), F32), vm((512, 128), BF), vm((wide - 1, ch, 128), BF), vm((deep, ch, 128), BF),
+        vm((ch, 128), BF), vm((ch, 128), BF),
         dma((8,)), dma((nx, 2)), dma((nx, 2)), dma((8,)), dma((8,)), dma((2,)), dma((2,)),
         dma((8,)), dma((8,)), dma((10,)), dma((10,)),
         dma((3,)), dma((3,)),

time: 45.9 us -> 45.7 us (level)
  no operation moved by 1% of the time
where the time goes in v13:
time: 45.7 us; the launch traced here: 45.6 us
  Pallas kernels  44.9 us (98%)
  between operations  0.64 us (1%)
    pallas_call x1, Pallas kernels, on_device(): pl.pallas_call(functools.partial(kernel, sizes), out_shape=(vm((FX, FY, 2...  43.7 us
    pallas_call x1, Pallas kernels, on_device(): pl.pallas_call(finish, out_shape=(jax.ShapeDtypeStruct((FX, FY, 256), BF)...  1.21 us

profile of v13, /device:TPU:1, one launch (start us, length us, event | category | flops | bytes accessed | tf_op | source)
XLA Modules:
  0.0 45.6 jit_solution(2857061945123609332)
XLA Ops:
  0.6 43.7 %shard_map.93 = (bf16[16,64,256]{2,1,0:T(8,128)(2,1)S(1)}, bf16[16,16,256]{2,1,0:T(8,128)(2,1)S(1)}, bf16[16,16,256]{2,1,0:T(8,128)(2,1)S(1)}, bf16[512,128]{1,0:T(8,128)(2,1)S(1)}) custom-call(bf16[16,64,256]{2,1,0:T(8,128)(2,1)} %fine_in.1, bf16[864,8]{1,0:T(8,128)(2,1)} %bitcast.10, bf16[4,4,16,256]{3,2,1,0:T(8,128)(2,1)} %c_out.1, ...), custom_call_target="tpu_custom_call" | custom-call | tf_op jit(solution)/shard_map/pallas_call | solution.py:643
  44.4 1.2 %shard_map.94 = (bf16[16,64,256]{2,1,0:T(8,128)(2,1)}, bf16[1,16,16,256]{3,2,1,0:T(8,128)(2,1)}, bf16[1,16,16,256]{3,2,1,0:T(8,128)(2,1)}, f32[54,32,32]{2,1,0:T(8,128)}) custom-call(bf16[16,64,256]{2,1,0:T(8,128)(2,1)S(1)} %get-tuple-element.12.fo_s, bf16[16,16,256]{2,1,0:T(8,128)(2,1)S(1)} %get-tuple-element.13.rb_s, ...), custom_call_target="tpu_custom_call" | custom-call | tf_op jit(solution)/shard_map/pallas_call | solution.py:652
